TPU v7x, 32 devices: a whole 2x2x4 slice. The times are simulated.
32 devices in a mesh: dp: 8 (over y, x, core), mp: 4 (over z).
Axes of the slice: x: 2, y: 2, z: 4, core: 2. Of those that a mesh axis runs over, the one named last changes fastest.
Arguments:
- block_input: bfloat16 [16512, 1152], P('dp'), may hold values from -6 to 6
- skip_input: bfloat16 [16512, 1152], P('dp'), may hold values from -6 to 6
- timesteps: int32 [64], P('dp'), may hold values from 0 to 999
- class_labels: int32 [64], P('dp'), may hold values from 0 to 999
- loss_weights: float32 [64], P('dp'), may hold values from 0.5 to 2
- grad_output: bfloat16 [16512, 1152], P('dp'), may hold values from -6 to 6
- skip_weight: float32 [2, 1152, 1152], P(None, 'mp'), may hold values from -0.125 to 0.125
- qkv_weight: float32 [3, 1152, 1152], P(None, None, 'mp'), may hold values from -0.1875 to 0.1875
- proj_weight: float32 [1152, 1152], P('mp'), may hold values from -0.75 to 0.75
- fc1_weight: float32 [1152, 4608], P(None, 'mp'), may hold values from -0.1875 to 0.1875
- fc2_weight: float32 [4608, 1152], P('mp'), may hold values from -0.09375 to 0.09375
- vectors: float32 [7, 1152], replicated, may hold values from -1.2 to 1.75, as said below
- hidden_bias: float32 [4608], P('mp'), may hold values from -1.5 to 1.5
- skip_rows: float32 [2, 1152], replicated, may hold values from 1651.2 to 280704
- skip_cols: float32 [2, 1152], replicated, may hold values from 16512 to 66048
- qkv_rows: float32 [3, 1152], replicated, may hold values from 516 to 2064
- qkv_cols: float32 [3, 1152], replicated, may hold values from 51.6 to 8772
- proj_rows: float32 [1152], replicated, may hold values from 51.6 to 8772
- proj_cols: float32 [1152], replicated, may hold values from 516 to 2064
- fc1_rows: float32 [1152], replicated, may hold values from 2064 to 8256
- fc1_cols: float32 [4608], replicated, may hold values from 206.4 to 35088
- fc2_rows: float32 [4608], replicated, may hold values from 412.8 to 70176
- fc2_cols: float32 [1152], replicated, may hold values from 4128 to 16512
- vector_moments: float32 [7, 1152], replicated, may hold values from 16512 to 66048
- hidden_moments: float32 [4608], P('mp'), may hold values from 206.4 to 35088
Outputs:
- block_output: bfloat16 [16512, 1152], P('dp')
- input_grad: float32 [16512, 1152], P('dp', 'mp')
- skip_input_grad: float32 [16512, 1152], P('dp', 'mp')
- skip_weight_grad: float32 [2, 1152, 1152], P(None, 'mp', 'dp')
- qkv_weight_grad: float32 [3, 1152, 1152], P(None, 'dp', 'mp')
- proj_weight_grad: float32 [1152, 1152], P('mp', 'dp')
- fc1_weight_grad: float32 [1152, 4608], P('dp', 'mp')
- fc2_weight_grad: float32 [4608, 1152], P('mp', 'dp')
- vector_grads: float32 [7, 1152], P(None, 'dp')
- hidden_bias_grad: float32 [4608], P('mp')
- skip_rows_new: float32 [2, 1152], replicated
- skip_cols_new: float32 [2, 1152], replicated
- qkv_rows_new: float32 [3, 1152], replicated
- qkv_cols_new: float32 [3, 1152], replicated
- proj_rows_new: float32 [1152], replicated
- proj_cols_new: float32 [1152], replicated
- fc1_rows_new: float32 [1152], replicated
- fc1_cols_new: float32 [4608], replicated
- fc2_rows_new: float32 [4608], replicated
- fc2_cols_new: float32 [1152], replicated
- vector_moments_new: float32 [7, 1152], replicated
- hidden_moments_new: float32 [4608], P('mp')
- skip_weight_new: float32 [2, 1152, 1152], P(None, 'mp')
- qkv_weight_new: float32 [3, 1152, 1152], P(None, None, 'mp')
- proj_weight_new: float32 [1152, 1152], P('mp')
- fc1_weight_new: float32 [1152, 4608], P(None, 'mp')
- fc2_weight_new: float32 [4608, 1152], P('mp')
- vectors_new: float32 [7, 1152], replicated
- hidden_bias_new: float32 [4608], P('mp')
- skip_weight_low: bfloat16 [2, 1152, 1152], P(None, 'mp')
- qkv_weight_low: bfloat16 [3, 1152, 1152], P(None, None, 'mp')
- proj_weight_low: bfloat16 [1152, 1152], P('mp')
- fc1_weight_low: bfloat16 [1152, 4608], P(None, 'mp')
- fc2_weight_low: bfloat16 [4608, 1152], P('mp')
- update_rms: float32 [], replicated
Inputs may be any that keep to these rules, and one draw needn't show every extreme that they name: `vectors`: norm gains lie near one, biases are of both signs.
All inputs are finite; a program needn't handle non-finite values.
Results may differ from a plain program's by a relative error of at most 0.0095.
Values sent between devices are 32-bit elements; how exact they have to be, the bound alone decides.
No kernel may reach another device: no remote copies, remote signals or barrier semaphores. Data moves between devices by JAX's collectives and lax.ppermute only.
A program may use at most 256 MiB of HBM per device.

v0:
```python
import math

import jax
import jax.numpy as jnp
from jax import lax
from jax.sharding import PartitionSpec as P

D = 1152
HEAD_DIM = 72
FF = 4608
CLASSES = 1000
SEQ = 258


ln_eps = 1e-05
moment_eps = 1e-30
clip_level = 0.25
step_rate = 2.0
total_steps = 1000.0


def gelu_exact(inputs):
    return 0.5 * inputs * (1.0 + lax.erf(inputs * (1.0 / math.sqrt(2.0))))


def matmul(left_side, right_side):
    return jnp.dot(left_side, right_side, preferred_element_type=jnp.float32)


def norm_forward(inputs, norm_gain, norm_bias):
    centre = jnp.mean(inputs, -1, keepdims=True)
    centred = inputs - centre
    inverse = lax.rsqrt(jnp.mean(centred * centred, -1, keepdims=True) + ln_eps)
    normal = centred * inverse
    return (normal * norm_gain + norm_bias, normal, inverse)


def norm_backward(incoming, normal, inverse, norm_gain):
    scaled = incoming * norm_gain
    inner_mean = jnp.mean(scaled, -1, keepdims=True)
    proj_mean = jnp.mean(scaled * normal, -1, keepdims=True)
    return (
        inverse * (scaled - inner_mean - normal * proj_mean),
        jnp.sum(incoming * normal, 0),
        jnp.sum(incoming, 0),
    )


def adafactor(
    grad_pieces,
    weight_pieces,
    starts,
    row_states,
    col_states,
    vector_piece,
    vector_weight,
    vector_state,
    hidden_piece,
    hidden_weight,
    hidden_state,
    first_mask,
    reduce_moments,
    reduce_norm,
):
    full_shapes = ((D, D), (D, D), (D, D), (D, FF), (FF, D))
    tensor_sizes = (2.0 * D * D, 3.0 * D * D, 1.0 * D * D, 1.0 * D * FF, 1.0 * FF * D)
    zero_start = jnp.zeros((), jnp.int32)
    row_parts = []
    col_parts = []
    weight_sq = []
    for position in range(5):
        grad_piece = grad_pieces[position]
        leading = grad_piece.shape[0]
        squares = grad_piece * grad_piece + moment_eps
        row_zero = jnp.zeros((leading, full_shapes[position][0]), jnp.float32)
        col_zero = jnp.zeros((leading, full_shapes[position][1]), jnp.float32)
        row_parts.append(
            lax.dynamic_update_slice(
                row_zero, jnp.sum(squares, 2), (zero_start, starts[position][0])
            ).reshape(-1)
        )
        col_parts.append(
            lax.dynamic_update_slice(
                col_zero, jnp.sum(squares, 1), (zero_start, starts[position][1])
            ).reshape(-1)
        )
        weight_sq.append(jnp.sum(weight_pieces[position] * weight_pieces[position])[None])
    weight_sq.append(jnp.sum(vector_weight * vector_weight, 1) * first_mask)
    weight_sq.append(jnp.sum(hidden_weight * hidden_weight)[None])
    row_total, col_total, weight_total = reduce_moments(
        jnp.concatenate(row_parts), jnp.concatenate(col_parts), jnp.concatenate(weight_sq)
    )
    row_news = []
    col_news = []
    updates = []
    step_sq = jnp.zeros((), jnp.float32)
    row_offset = 0
    col_offset = 0
    for position in range(5):
        grad_piece = grad_pieces[position]
        leading = grad_piece.shape[0]
        rows_full, cols_full = full_shapes[position]
        row_sum = row_total[row_offset : row_offset + leading * rows_full].reshape(
            leading, rows_full
        )
        col_sum = col_total[col_offset : col_offset + leading * cols_full].reshape(
            leading, cols_full
        )
        row_offset = row_offset + leading * rows_full
        col_offset = col_offset + leading * cols_full
        row_new = 0.5 * row_states[position] + 0.5 * (row_sum / cols_full)
        col_new = 0.5 * col_states[position] + 0.5 * (col_sum / rows_full)
        row_piece = lax.dynamic_slice(
            row_new, (zero_start, starts[position][0]), (leading, grad_piece.shape[1])
        )
        col_piece = lax.dynamic_slice(
            col_new, (zero_start, starts[position][1]), (leading, grad_piece.shape[2])
        )
        row_mean = jnp.mean(row_new, 1)
        update = grad_piece * lax.rsqrt(
            row_piece[:, :, None] * col_piece[:, None, :] / row_mean[:, None, None]
        )
        step_sq = step_sq + jnp.sum(update * update)
        row_news.append(row_new)
        col_news.append(col_new)
        updates.append(update)
    vector_new = 0.5 * vector_state + 0.5 * (vector_piece * vector_piece + moment_eps)
    vector_update = vector_piece * lax.rsqrt(vector_new)
    hidden_new = 0.5 * hidden_state + 0.5 * (hidden_piece * hidden_piece + moment_eps)
    hidden_update = hidden_piece * lax.rsqrt(hidden_new)
    step_sq = (
        step_sq
        + jnp.sum(vector_update * vector_update) * first_mask
        + jnp.sum(hidden_update * hidden_update)
    )
    step_total = reduce_norm(step_sq)
    param_count = 6.0 * D * D + 2.0 * D * FF + 7.0 * D + FF
    update_rms = jnp.sqrt(step_total / param_count)
    divisor = jnp.maximum(1.0, update_rms / clip_level)
    new_weights = []
    for position in range(5):
        weight_rms = jnp.sqrt(weight_total[position] / tensor_sizes[position])
        new_weights.append(
            weight_pieces[position]
            - step_rate * jnp.maximum(0.001, weight_rms) * updates[position] / divisor
        )
    vector_rms = jnp.sqrt(weight_total[5:12] / D)[:, None]
    vector_weight_new = (
        vector_weight - step_rate * jnp.maximum(0.001, vector_rms) * vector_update / divisor
    )
    hidden_rms = jnp.sqrt(weight_total[12] / FF)
    hidden_weight_new = (
        hidden_weight - step_rate * jnp.maximum(0.001, hidden_rms) * hidden_update / divisor
    )
    return (
        new_weights,
        row_news,
        col_news,
        vector_new,
        vector_weight_new,
        hidden_new,
        hidden_weight_new,
        update_rms,
    )


def body(
    block_input,
    skip_input,
    timesteps,
    class_labels,
    loss_weights,
    grad_output,
    skip_weight,
    qkv_weight,
    proj_weight,
    fc1_weight,
    fc2_weight,
    vectors,
    hidden_bias,
    skip_rows,
    skip_cols,
    qkv_rows,
    qkv_cols,
    proj_rows,
    proj_cols,
    fc1_rows,
    fc1_cols,
    fc2_rows,
    fc2_cols,
    vector_moments,
    hidden_moments,
):
    image_count = timesteps.shape[0]
    width_local = qkv_weight.shape[2]
    heads_local = width_local // HEAD_DIM
    hidden_local = fc1_weight.shape[1]
    mp_index = lax.axis_index("mp")
    dp_index = lax.axis_index("dp")
    dp_count = lax.axis_size("dp")
    first_mask = (mp_index == 0).astype(jnp.float32)
    feature_start = mp_index * skip_weight.shape[1]
    block_local = lax.dynamic_slice_in_dim(block_input, feature_start, skip_weight.shape[1], 1)
    skip_local = lax.dynamic_slice_in_dim(skip_input, feature_start, skip_weight.shape[1], 1)
    angles = (timesteps.astype(jnp.float32) + 0.5) * (0.5 * math.pi / total_steps)
    alpha_sq = jnp.square(jnp.cos(angles))
    sigma_sq = jnp.square(jnp.sin(angles))
    snr_weight = 5.0 * sigma_sq / jnp.maximum(alpha_sq, 5.0 * sigma_sq)
    base_weight = loss_weights * snr_weight
    one_hot = (class_labels[:, None] == jnp.arange(CLASSES, dtype=jnp.int32)[None, :]).astype(
        jnp.float32
    )
    class_counts, weight_total = lax.psum((jnp.sum(one_hot, 0), jnp.sum(base_weight)), "dp")
    own_count = jnp.dot(one_hot, class_counts, precision=lax.Precision.HIGHEST)
    item_weight = base_weight * (image_count * dp_count / weight_total) * lax.rsqrt(own_count)
    upstream = (
        grad_output.astype(jnp.float32).reshape(image_count, SEQ, D) * item_weight[:, None, None]
    ).reshape(-1, D)
    skip_low = skip_weight.astype(jnp.bfloat16)
    qkv_low = qkv_weight.astype(jnp.bfloat16)
    proj_low = proj_weight.astype(jnp.bfloat16)
    fc1_low = fc1_weight.astype(jnp.bfloat16)
    fc2_low = fc2_weight.astype(jnp.bfloat16)
    joined = (
        lax.psum(matmul(block_local, skip_low[0]) + matmul(skip_local, skip_low[1]), "mp")
        + vectors[4]
    )
    normed, normal_one, inverse_one = norm_forward(joined, vectors[0], vectors[1])
    normed_low = normed.astype(jnp.bfloat16)
    qkv_all = jnp.einsum(
        "td,sde->ste", normed_low, qkv_low, preferred_element_type=jnp.float32
    ).astype(jnp.bfloat16)
    heads_view = qkv_all.reshape(3, image_count, SEQ, heads_local, HEAD_DIM)
    query_low = heads_view[0]
    key_low = heads_view[1]
    value_low = heads_view[2]
    score_scale = HEAD_DIM ** (-0.5)

    def score_block():
        return (
            jnp.einsum("iqhe,ikhe->ihqk", query_low, key_low, preferred_element_type=jnp.float32)
            * score_scale
        )

    scores = score_block()
    score_top = jnp.max(scores, -1, keepdims=True)
    expo_scores = jnp.exp(scores - score_top)
    expo_total = jnp.sum(expo_scores, -1, keepdims=True)
    weights_low = (expo_scores / expo_total).astype(jnp.bfloat16)
    log_total = score_top + jnp.log(expo_total)
    attended = (
        jnp.einsum("ihqk,ikhe->iqhe", weights_low, value_low, preferred_element_type=jnp.float32)
        .astype(jnp.bfloat16)
        .reshape(-1, width_local)
    )
    residual = joined + lax.psum(matmul(attended, proj_low), "mp") + vectors[5]
    normed_two, normal_two, inverse_two = norm_forward(residual, vectors[2], vectors[3])
    normed_two_low = normed_two.astype(jnp.bfloat16)
    pre_act = matmul(normed_two_low, fc1_low) + hidden_bias
    activated, gelu_pull = jax.vjp(gelu_exact, pre_act)
    activated_low = activated.astype(jnp.bfloat16)
    block_output = (residual + lax.psum(matmul(activated_low, fc2_low), "mp") + vectors[6]).astype(
        jnp.bfloat16
    )
    upstream_low = upstream.astype(jnp.bfloat16)
    fc2_grad = jnp.einsum(
        "tf,td->fd", activated_low, upstream_low, preferred_element_type=jnp.float32
    )
    fc2_bias_grad = jnp.sum(upstream, 0)
    act_grad = jnp.einsum("td,fd->tf", upstream_low, fc2_low, preferred_element_type=jnp.float32)
    pre_grad = gelu_pull(act_grad)[0]
    pre_low = pre_grad.astype(jnp.bfloat16)
    fc1_grad = jnp.einsum("td,tf->df", normed_two_low, pre_low, preferred_element_type=jnp.float32)
    hidden_grad = jnp.sum(pre_grad, 0)
    norm_two_in = lax.psum(
        jnp.einsum("tf,df->td", pre_low, fc1_low, preferred_element_type=jnp.float32), "mp"
    )
    back_two, gain_two_grad, bias_two_grad = norm_backward(
        norm_two_in, normal_two, inverse_two, vectors[2]
    )
    residual_grad = upstream + back_two
    proj_bias_grad = jnp.sum(residual_grad, 0)
    residual_low = residual_grad.astype(jnp.bfloat16)
    proj_grad = jnp.einsum("te,td->ed", attended, residual_low, preferred_element_type=jnp.float32)
    attended_grad = jnp.einsum(
        "td,ed->te", residual_low, proj_low, preferred_element_type=jnp.float32
    ).astype(jnp.bfloat16)
    attended_grad = attended_grad.reshape(image_count, SEQ, heads_local, HEAD_DIM)
    scores = score_block()
    probs_exact = jnp.exp(scores - log_total)
    prob_grad = jnp.einsum(
        "iqhe,ikhe->ihqk", attended_grad, value_low, preferred_element_type=jnp.float32
    )
    score_grad = (
        probs_exact * (prob_grad - jnp.sum(probs_exact * prob_grad, -1, keepdims=True))
    ).astype(jnp.bfloat16)
    query_grad = (
        jnp.einsum("ihqk,ikhe->iqhe", score_grad, key_low, preferred_element_type=jnp.float32)
        * score_scale
    )
    key_grad = (
        jnp.einsum("ihqk,iqhe->ikhe", score_grad, query_low, preferred_element_type=jnp.float32)
        * score_scale
    )
    value_grad = jnp.einsum(
        "ihqk,iqhe->ikhe", weights_low, attended_grad, preferred_element_type=jnp.float32
    )
    qkv_grad_low = (
        jnp.stack([query_grad, key_grad, value_grad])
        .astype(jnp.bfloat16)
        .reshape(3, -1, width_local)
    )
    qkv_grad = jnp.einsum(
        "td,ste->sde", normed_low, qkv_grad_low, preferred_element_type=jnp.float32
    )
    norm_one_in = lax.psum(
        jnp.einsum("ste,sde->td", qkv_grad_low, qkv_low, preferred_element_type=jnp.float32), "mp"
    )
    back_one, gain_one_grad, bias_one_grad = norm_backward(
        norm_one_in, normal_one, inverse_one, vectors[0]
    )
    joined_grad = residual_grad + back_one
    skip_bias_grad = jnp.sum(joined_grad, 0)
    joined_low = joined_grad.astype(jnp.bfloat16)
    skip_grad = jnp.stack(
        [
            jnp.einsum("tc,td->cd", block_local, joined_low, preferred_element_type=jnp.float32),
            jnp.einsum("tc,td->cd", skip_local, joined_low, preferred_element_type=jnp.float32),
        ]
    )
    input_grad = jnp.einsum(
        "td,cd->tc", joined_low, skip_low[0], preferred_element_type=jnp.float32
    )
    skip_input_grad = jnp.einsum(
        "td,cd->tc", joined_low, skip_low[1], preferred_element_type=jnp.float32
    )
    vector_grad = jnp.stack(
        [
            gain_one_grad,
            bias_one_grad,
            gain_two_grad,
            bias_two_grad,
            skip_bias_grad,
            proj_bias_grad,
            fc2_bias_grad,
        ]
    )
    row_states = [skip_rows, qkv_rows, proj_rows[None], fc1_rows[None], fc2_rows[None]]
    col_states = [skip_cols, qkv_cols, proj_cols[None], fc1_cols[None], fc2_cols[None]]
    piece_width = D // dp_count
    dp_start = dp_index * piece_width
    zero_start = jnp.zeros((), jnp.int32)
    summed = lax.psum(
        (skip_grad, qkv_grad, proj_grad, fc1_grad, fc2_grad, vector_grad, hidden_grad), "dp"
    )

    def moments_mp(row_all, col_all, squares_all):
        return lax.psum((row_all, col_all, squares_all), "mp")

    def norm_mp(step_sq):
        return lax.psum(step_sq, "mp")

    grad_pieces = [summed[0], summed[1], summed[2][None], summed[3][None], summed[4][None]]
    weight_pieces = [skip_weight, qkv_weight, proj_weight[None], fc1_weight[None], fc2_weight[None]]
    starts = [
        (mp_index * width_local, zero_start),
        (zero_start, mp_index * width_local),
        (mp_index * width_local, zero_start),
        (zero_start, mp_index * hidden_local),
        (mp_index * hidden_local, zero_start),
    ]
    results = adafactor(
        grad_pieces,
        weight_pieces,
        starts,
        row_states,
        col_states,
        summed[5],
        vectors,
        vector_moments,
        summed[6],
        hidden_bias,
        hidden_moments,
        first_mask,
        moments_mp,
        norm_mp,
    )
    (
        new_weights,
        row_news,
        col_news,
        vector_state_new,
        vectors_new,
        hidden_state_new,
        hidden_new,
        update_rms,
    ) = results
    skip_new = new_weights[0]
    qkv_new = new_weights[1]
    proj_new = new_weights[2][0]
    fc1_new = new_weights[3][0]
    fc2_new = new_weights[4][0]
    skip_grad_out = lax.dynamic_slice_in_dim(summed[0], dp_start, piece_width, 2)
    qkv_grad_out = lax.dynamic_slice_in_dim(summed[1], dp_start, piece_width, 1)
    proj_grad_out = lax.dynamic_slice_in_dim(summed[2], dp_start, piece_width, 1)
    fc1_grad_out = lax.dynamic_slice_in_dim(summed[3], dp_start, piece_width, 0)
    fc2_grad_out = lax.dynamic_slice_in_dim(summed[4], dp_start, piece_width, 1)
    vector_grad_out = lax.dynamic_slice_in_dim(summed[5], dp_start, piece_width, 1)
    hidden_grad_out = summed[6]
    return (
        block_output,
        input_grad,
        skip_input_grad,
        skip_grad_out,
        qkv_grad_out,
        proj_grad_out,
        fc1_grad_out,
        fc2_grad_out,
        vector_grad_out,
        hidden_grad_out,
        row_news[0],
        col_news[0],
        row_news[1],
        col_news[1],
        row_news[2][0],
        col_news[2][0],
        row_news[3][0],
        col_news[3][0],
        row_news[4][0],
        col_news[4][0],
        vector_state_new,
        hidden_state_new,
        skip_new,
        qkv_new,
        proj_new,
        fc1_new,
        fc2_new,
        vectors_new,
        hidden_new,
        skip_new.astype(jnp.bfloat16),
        qkv_new.astype(jnp.bfloat16),
        proj_new.astype(jnp.bfloat16),
        fc1_new.astype(jnp.bfloat16),
        fc2_new.astype(jnp.bfloat16),
        update_rms,
    )


def solution(mesh):
    placed = (
        P("dp", None),
        P("dp", None),
        P("dp"),
        P("dp"),
        P("dp"),
        P("dp", None),
        P(None, "mp", None),
        P(None, None, "mp"),
        P("mp", None),
        P(None, "mp"),
        P("mp", None),
        P(),
        P("mp"),
        P(),
        P(),
        P(),
        P(),
        P(),
        P(),
        P(),
        P(),
        P(),
        P(),
        P(),
        P("mp"),
    )
    return jax.shard_map(
        body,
        mesh=mesh,
        in_specs=placed,
        out_specs=(
            P("dp", None),
            P("dp", "mp"),
            P("dp", "mp"),
            P(None, "mp", "dp"),
            P(None, "dp", "mp"),
            P("mp", "dp"),
            P("dp", "mp"),
            P("mp", "dp"),
            P(None, "dp"),
            P("mp"),
            P(),
            P(),
            P(),
            P(),
            P(),
            P(),
            P(),
            P(),
            P(),
            P(),
            P(),
            P("mp"),
            P(None, "mp", None),
            P(None, None, "mp"),
            P("mp", None),
            P(None, "mp"),
            P("mp", None),
            P(),
            P("mp"),
            P(None, "mp", None),
            P(None, None, "mp"),
            P("mp", None),
            P(None, "mp"),
            P("mp", None),
            P(),
        ),
        check_vma=False,
    )
```

profile of v0, /device:TPU:0, one launch (start us, length us, event | category | flops | bytes accessed | tf_op | source)
XLA Modules:
  0.0 2293.2 jit_solution(7626587432086693223)
XLA Ops:
  11.1 5.1 fusion.45
  16.2 8.4 convolution_add_fusion
  26.0 328.7 %all-reduce.13.cloned.1.call-done = f32[2064,1152]{1,0:T(8,128)} async-done(((f32[2064,1152]{1,0:T(8,128)}), f32[2064,1152]{1,0:T(8,128)}) %all-reduce.13.cloned.1.call-update) | async-done | bytes 9510928 | tf_op jit(solution)/shard_map/psum | solution.py:225
  354.7 4.6 add_reduce_fusion
  363.3 7.0 fusion.8
  386.6 4.8 divide_convert_fusion
  394.6 5.1 convert_bitcast_fusion.1
  405.5 7.9 fusion.61
  414.8 14.9 all-reduce.1
  430.7 309.4 %all-reduce.15.cloned.1.call-done = f32[2064,1152]{1,0:T(8,128)} async-done(((f32[2064,1152]{1,0:T(8,128)}), f32[2064,1152]{1,0:T(8,128)}) %all-reduce.15.cloned.1.call-update) | async-done | bytes 9510928 | tf_op jit(solution)/shard_map/psum | solution.py:256
  740.2 11.4 fusion.94
  751.6 5.0 multiply_reduce_fusion.6
  758.0 13.9 multiply_convert_fusion.1
  771.9 13.8 fusion.97
  787.9 9.6 fusion.16
  797.6 12.9 fusion.48
  810.5 313.8 %all-reduce.17.cloned.1.call-done = f32[2064,1152]{1,0:T(8,128)} async-done(((f32[2064,1152]{1,0:T(8,128)}), f32[2064,1152]{1,0:T(8,128)}) %all-reduce.17.cloned.1.call-update) | async-done | bytes 9510928 | tf_op jit(solution)/shard_map/psum | solution.py:275
  1124.3 9.0 multiply_reduce_fusion.2
  1133.6 8.2 fusion.90
  1148.4 4.8 reshape.408
  1153.3 7.1 convert_bitcast_fusion
  1160.4 14.2 multiply_reduce_fusion
  1174.6 10.1 multiply_convert_fusion
  1184.7 7.2 fusion.39
  1196.9 4.2 stack.47
  1219.3 9.4 convolution_bitcast_fusion
  1228.8 13.4 fusion.20
  1242.3 14.4 fusion.14
  1259.9 7.7 convolution_bitcast_fusion.1
  1267.6 596.0 %all-reduce.23.cloned.1.call-done = (f32[2064,1152]{1,0:T(8,128)}, f32[2064,1152]{1,0:T(8,128)}) async-done(((f32[2064,1152]{1,0:T(8,128)}, f32[2064,1152]{1,0:T(8,128)}), (f32[2064,1152]{1,0:T(8,128)}, f32[2064,1152]{1,0:T(8,128)})) %all-reduce.23.cloned.1.call-update) | async-done | bytes 19021840 | tf_op jit(solution)/shard_map/psum | solution.py:262
  1863.6 10.1 multiply_reduce_fusion.3
  1875.7 6.8 fusion.91
  1882.5 5.3 convolution_bitcast_fusion.2
  1895.7 4.4 multiply_reduce_fusion.15
  1900.0 4.6 multiply_reduce_fusion.13
  1906.6 4.5 concatenate.13
  1911.2 26.8 %all-reduce = (f32[7,1152]{1,0:T(8,128)S(1)}, f32[1152]{0:T(1024)S(1)}) all-reduce(f32[7,1152]{1,0:T(8,128)S(1)} %stack.59, f32[1152]{0:T(1024)S(1)} %copy-done.60), channel_id=1, replica_groups=mesh['dp'=8,'mp'=4] {'dp'}, use_global_device_ids=true, to_apply=%region_32.0 | all-reduce | flops 9216 | bytes 73728 | tf_op jit(solution)/shard_map/psum | solution.py:353
  1941.8 5.8 fusion.59
  1947.7 6.1 fusion.58
  1953.8 10.0 add_convert_fusion
  1963.8 169.3 %all-reduce.19.cloned.1.call-done = (f32[2,288,1152]{2,1,0:T(8,128)}, f32[3,1152,288]{1,2,0:T(8,128)}, f32[288,1152]{1,0:T(8,128)}, f32[1152,1152]{1,0:T(8,128)}, f32[1152,1152]{1,0:T(8,128)}) async-done(((f32[2,288,1152]{2,1,0:T(8,128)}, f32[3,1152,288]{1,2,0:T(8,128)}, f32[288,1152]{1,0:T(8,128)}, f32[1152,1152]{1,0:T(8,128)}, f32[1152,1152]{1,0:T(8,128)}), (f32[2,288,1152]{2,1,0:T(8,128)}, ...) | async-done | bytes 18579472 | tf_op jit(solution)/shard_map/psum | solution.py:353
  2176.8 33.4 %all-reduce.21.cloned.1.call-done = (f32[12672]{0:T(1024)}, f32[12672]{0:T(1024)}) async-done(((f32[12672]{0:T(1024)}, f32[12672]{0:T(1024)}), (f32[12672]{0:T(1024)}, f32[12672]{0:T(1024)})) %all-reduce.21.cloned.1.call-update) | async-done | bytes 101392 | tf_op jit(solution)/shard_map/psum | solution.py:358
  2222.9 4.1 multiply_reduce_fusion.14
  2233.1 4.4 multiply_reduce_fusion.11
  2238.2 4.5 multiply_reduce_fusion.10
  2244.8 11.2 all-reduce.3
  2259.5 7.1 fusion.77
  2266.8 6.3 fusion.78
  (328 shorter events, 157.6 us)
Async XLA Ops:
  7.2 347.5 %all-reduce.13.cloned.1.call-start = ((), (), s32[]{:S(2)}) async-start(), calls=%async_computation | async-start | bytes 19021824 | tf_op jit(solution)/shard_map/psum | solution.py:225
  24.6 715.6 %all-reduce.15.cloned.1.call-start = ((), (), s32[]{:S(2)}) async-start(), calls=%async_computation.1 | async-start | bytes 19021824 | tf_op jit(solution)/shard_map/psum | solution.py:256
  26.0 336.6 %copy-start.44 = (f32[1152]{0:T(1024)}, f32[1152]{0:T(1024)S(1)}, u32[]{:S(2)}) copy-start(f32[1152]{0:T(1024)S(1)} %get-tuple-element.163) | copy-start | bytes 13828
  26.0 336.6 %copy-start.61 = (f32[1152]{0:T(1024)}, f32[1152]{0:T(1024)S(1)}, u32[]{:S(2)}) copy-start(f32[1152]{0:T(1024)S(1)} %get-tuple-element.162) | copy-start | bytes 13828
  26.0 714.2 %copy-start.30 = (f32[1152]{0:T(1024)}, f32[1152]{0:T(1024)S(1)}, u32[]{:S(2)}) copy-start(f32[1152]{0:T(1024)S(1)} %get-tuple-element.164) | copy-start | bytes 13828
  413.4 710.9 %all-reduce.17.cloned.1.call-start = ((), (), s32[]{:S(2)}) async-start(), calls=%async_computation.2 | async-start | bytes 19021824 | tf_op jit(solution)/shard_map/psum | solution.py:275
  740.2 16.4 copy-start.54
  751.6 20.3 slice-start.17
  758.0 13.9 slice-start.18
  758.0 29.9 %slice-start.21 = ((s8[5308416]{0:T(1024)(128)(4,1)}), s8[4194304]{0:T(1024)(128)(4,1)S(1)}, s32[]{:S(2)}) async-start(s8[5308416]{0:T(1024)(128)(4,1)} %bitcast.109), calls=%async_computation.27 | async-start | bytes 8388608
  771.9 16.0 slice-start.22
  797.5 1066.1 %all-reduce.23.cloned.1.call-start = ((), (), s32[]{:S(2)}) async-start(), calls=%async_computation.5 | async-start | bytes 38043648 | tf_op jit(solution)/shard_map/psum | solution.py:262
  1160.4 14.2 slice-start
  1160.4 14.2 slice-start.1
  1160.4 14.2 slice-start.2
  1160.4 14.2 slice-start.3
  1196.9 11.5 copy-start.18
  1228.7 904.3 %all-reduce.19.cloned.1.call-start = ((), (), s32[]{:S(2)}) async-start(), calls=%async_computation.3 | async-start | bytes 37158912 | tf_op jit(solution)/shard_map/psum | solution.py:353
  1228.8 27.9 %slice-start.10 = ((s8[9510912]{0:T(1024)(128)(4,1)}), s8[4194304]{0:T(1024)(128)(4,1)S(1)}, s32[]{:S(2)}) async-start(s8[9510912]{0:T(1024)(128)(4,1)} %bitcast.99), calls=%async_computation.16 | async-start | bytes 8388608
  1228.8 31.1 %slice-start.4 = ((s8[9510912]{0:T(1024)(128)(4,1)}), s8[4194304]{0:T(1024)(128)(4,1)S(1)}, s32[]{:S(2)}) async-start(s8[9510912]{0:T(1024)(128)(4,1)} %bitcast.95), calls=%async_computation.10 | async-start | bytes 8388608
  1242.2 14.5 slice-start.11
  1242.2 14.5 slice-start.12
  1242.3 14.5 copy-start.20
  1242.3 17.6 slice-start.5
  1242.3 17.6 slice-start.6
  1863.6 10.1 slice-start.7
  1863.6 10.1 slice-start.8
  1863.6 10.1 slice-start.9
  1863.6 12.1 copy-start.7
  1893.3 316.9 %all-reduce.21.cloned.1.call-start = ((), (), s32[]{:S(2)}) async-start(), calls=%async_computation.4 | async-start | bytes 212992 | tf_op jit(solution)/shard_map/psum | solution.py:358
  1894.7 9.9 slice-start.19
  1900.0 11.2 copy-start.60
  1900.0 38.0 %copy-start.48 = (f32[7,1152]{1,0:T(8,128)S(1)}, f32[7,1152]{1,0:T(8,128)}, u32[]{:S(2)}) copy-start(f32[7,1152]{1,0:T(8,128)} %param.48) | copy-start | bytes 96772
  1900.0 40.6 %copy-start.59 = (f32[1152]{0:T(1024)S(1)}, f32[1152]{0:T(1024)}, u32[]{:S(2)}) copy-start(f32[1152]{0:T(1024)} %param.49) | copy-start | bytes 13828
  1900.0 41.8 %copy-start.22 = (bf16[2,288,1152]{2,1,0:T(8,128)(2,1)S(1)}, bf16[2,288,1152]{2,1,0:T(8,128)(2,1)}, u32[]{:S(2)}) copy-start(bf16[2,288,1152]{2,1,0:T(8,128)(2,1)} %copy-done.21) | copy-start | bytes 3981316
  1938.0 9.6 copy-start.34
  2214.4 23.1 %copy-start.46 = (f32[4608]{0:T(1024)}, f32[4608]{0:T(1024)S(1)}, u32[]{:S(2)}) copy-start(f32[4608]{0:T(1024)S(1)} %get-tuple-element.195) | copy-start | bytes 55300
  2215.2 22.3 copy-start.47
  2216.7 20.8 copy-start.58
  2216.7 49.9 %copy-start.41 = (f32[1152]{0:T(1024)}, f32[1152]{0:T(1024)S(1)}, u32[]{:S(2)}) copy-start(f32[1152]{0:T(1024)S(1)} %get-tuple-element.197) | copy-start | bytes 13828
  2218.9 18.7 copy-start.50
  2219.8 56.5 %copy-start.36 = (f32[3,1152]{1,0:T(4,128)}, f32[3,1152]{1,0:T(4,128)S(1)}, u32[]{:S(2)}) copy-start(f32[3,1152]{1,0:T(4,128)S(1)} %get-tuple-element.201) | copy-start | bytes 41476
  2220.7 16.9 copy-start.57
  2222.2 37.3 %copy-start.42 = (f32[1152]{0:T(1024)}, f32[1152]{0:T(1024)S(1)}, u32[]{:S(2)}) copy-start(f32[1152]{0:T(1024)S(1)} %get-tuple-element.218) | copy-start | bytes 13828
  2222.2 51.7 %copy-start.43 = (f32[1152]{0:T(1024)}, f32[1152]{0:T(1024)S(1)}, u32[]{:S(2)}) copy-start(f32[1152]{0:T(1024)S(1)} %get-tuple-element.219) | copy-start | bytes 13828
  2222.9 58.0 %copy-start.40 = (f32[2,1152]{1,0:T(2,128)}, f32[2,1152]{1,0:T(2,128)S(1)}, u32[]{:S(2)}) copy-start(f32[2,1152]{1,0:T(2,128)S(1)} %multiply_add_fusion.10) | copy-start | bytes 27652
  2233.1 11.7 copy-start.66
  2238.2 28.5 %slice-start.15 = ((s8[5308416]{0:T(1024)(128)(4,1)}), s8[1114112]{0:T(1024)(128)(4,1)S(1)}, s32[]{:S(2)}) async-start(s8[5308416]{0:T(1024)(128)(4,1)} %bitcast.103), calls=%async_computation.21 | async-start | bytes 2228224
  (49 other events, 223.1 us)
Sparse Core Ops, SparseCore 0:
  24.7 329.9 all-reduce.12
  413.5 326.6 all-reduce.14
  797.6 326.5 all-reduce.16
  1228.9 634.7 all-reduce.22
  1893.4 239.5 all-reduce.18
  2175.8 34.3 all-reduce.20
where the time goes:
time: 2300 us; the launch traced here: 2290 us
  waiting for transfers between devices  1750 us (76%)
  matrix products  191 us (8%)
  other arithmetic  166 us (7%)
  local copies, waits for them, and re-layouts  104 us (5%)
  blocking collectives  52.9 us (2%)
  between operations  28.8 us (1%)
    psum x1, waiting for transfers between devices, body(): lax.psum(matmul(activated_low, fc2_low), 'mp')  596 us
    psum x1, waiting for transfers between devices, body(): lax.psum(matmul(block_local, skip_low[0]) + matmul(skip_local, skip_low[1...  329 us
    psum x1, waiting for transfers between devices, body(): lax.psum(jnp.einsum('tf,df->td', pre_low, fc1_low, preferred_element_type...  314 us
    psum x1, waiting for transfers between devices, body(): residual = joined + lax.psum(matmul(attended, proj_low), 'mp') + vectors[5]  309 us
    psum x1, waiting for transfers between devices, body(): lax.psum((skip_grad, qkv_grad, proj_grad, fc1_grad, fc2_grad, vector_grad...  169 us
    dot_general x5, matrix products, matmul(): return jnp.dot(left_side, right_side, preferred_element_type=jnp.float32)  48.1 us
  transfers between devices with their start and end apart: 6, of which 6 were waited for; matrix products, arithmetic and copies ran while one was open for 4% of the time, Pallas kernels for 0%

commit v1 on v0

--- a/solution.py
+++ b/solution.py
@@ -3,6 +3,8 @@
 import jax
 import jax.numpy as jnp
 from jax import lax
+from jax.experimental import pallas as pl
+from jax.experimental.pallas import tpu as pltpu
 from jax.sharding import PartitionSpec as P
 
 D = 1152
@@ -164,7 +166,7 @@
     )
 
 
-def body(
+def body_tensor(
     block_input,
     skip_input,
     timesteps,
@@ -446,6 +448,844 @@
     )
 
 
+def body(*operands):
+    images = operands[2].shape[0]
+    if images % lax.axis_size("mp") == 0 and lax.axis_size("dp") == 8:
+        return body_data(*operands)
+    return body_tensor(*operands)
+
+
+def to_core(array):
+    return lax.ppermute(array, "dp", [(i, i ^ 1) for i in range(8)])
+
+
+def to_x(array):
+    return lax.ppermute(array, "dp", [(i, i ^ 2) for i in range(8)])
+
+
+def to_y(array):
+    return lax.ppermute(array, "dp", [(i, i ^ 4) for i in range(8)])
+
+
+def turn_mp(array, shift):
+    count = lax.axis_size("mp")
+    return lax.ppermute(array, "mp", [(i, (i + shift) % count) for i in range(count)])
+
+
+def pick(array, index, axis):
+    return lax.dynamic_index_in_dim(array, index, axis, keepdims=False)
+
+
+def assemble(steps, targets, core, rows, blocks, split):
+    arrays = []
+    for step in steps:
+        for array, _ in step:
+            if not any(array is other for other in arrays):
+                arrays.append(array)
+    place = [
+        [(next(n for n, other in enumerate(arrays) if other is array), k) for array, k in step]
+        for step in steps
+    ]
+    table = jnp.stack([jnp.asarray(v, jnp.int32) for v in [*targets, core]])
+    depth = 4
+    outs = 2 if split < blocks else 1
+
+    def kernel(table_ref, *refs):
+        sources = refs[: len(arrays)]
+        wholes = refs[len(arrays) : len(arrays) + outs]
+        wide, narrow, in_sem, out_sem = refs[len(arrays) + outs :]
+        half = rows // 2
+        first = pl.multiple_of(table_ref[len(steps)] * half, half)
+        second = pl.multiple_of(half - first, half)
+
+        def fetch(step):
+            slot = step % depth
+            if len(place[step]) == 1:
+                ((n, k),) = place[step]
+                return [pltpu.make_async_copy(sources[n].at[k], wide.at[slot], in_sem.at[slot, 0])]
+            copies = []
+            for part, ((n, k), start) in enumerate(zip(place[step], (first, second))):
+                spot = wide.at[slot, pl.ds(start, half)]
+                copies.append(pltpu.make_async_copy(sources[n].at[k], spot, in_sem.at[slot, part]))
+            return copies
+
+        def leave(step, whole, spot):
+            slot = step % depth
+            return pltpu.make_async_copy(narrow.at[slot], whole.at[spot], out_sem.at[slot])
+
+        for step in range(len(steps) + depth - 1):
+            if step < len(steps):
+                for copy in fetch(step):
+                    copy.start()
+            step = step - (depth - 1)
+            if step < 0:
+                continue
+            slot = step % depth
+            for copy in fetch(step):
+                copy.wait()
+            if step >= depth:
+                leave(step - depth, wholes[0], 0).wait()
+            narrow[slot] = wide[slot].astype(jnp.bfloat16)
+            spot = table_ref[step]
+            if outs == 1:
+                leave(step, wholes[0], spot).start()
+            else:
+
+                @pl.when(spot < split)
+                def _():
+                    leave(step, wholes[0], spot).start()
+
+                @pl.when(spot >= split)
+                def _():
+                    leave(step, wholes[1], spot - split).start()
+
+        for step in range(max(0, len(steps) - depth), len(steps)):
+            leave(step, wholes[0], 0).wait()
+
+    shapes = [jax.ShapeDtypeStruct((split, rows, D), jnp.bfloat16)]
+    if outs == 2:
+        shapes.append(jax.ShapeDtypeStruct((blocks - split, rows, D), jnp.bfloat16))
+    anywhere = pl.BlockSpec(memory_space=pl.ANY)
+    return pl.pallas_call(
+        kernel,
+        in_specs=[pl.BlockSpec(memory_space=pltpu.SMEM)] + [anywhere] * len(arrays),
+        out_specs=[anywhere] * outs,
+        out_shape=shapes,
+        scratch_shapes=[
+            pltpu.VMEM((depth, rows, D), jnp.float32),
+            pltpu.VMEM((depth, rows, D), jnp.bfloat16),
+            pltpu.SemaphoreType.DMA((depth, 2)),
+            pltpu.SemaphoreType.DMA((depth,)),
+        ],
+        compiler_params=pltpu.CompilerParams(vmem_limit_bytes=32 * 1024 * 1024),
+        cost_estimate=pl.CostEstimate(flops=0, bytes_accessed=blocks * rows * D * 6, transcendentals=0),
+    )(table, *arrays)
+
+
+class Order:
+    def __init__(self):
+        self.token = None
+
+    def after(self, *arrays):
+        if self.token is not None:
+            arrays = lax.optimization_barrier((*arrays, self.token))[:-1]
+        return arrays if len(arrays) > 1 else arrays[0]
+
+    def mark(self, *arrays):
+        arrays = self.after(*arrays)
+        self.token = arrays[0] if isinstance(arrays, tuple) else arrays
+        return arrays
+
+
+def swap_plane(order, for_x, for_y):
+    for_x, for_y = order.after(for_x, for_y)
+    return to_x(for_x), to_y(for_y)
+
+
+def in_turn(arrays):
+    count = len(arrays)
+    twice = jnp.stack(list(arrays[::-1]) * 2)
+    return lax.dynamic_slice_in_dim(twice, count - 1 - lax.axis_index("mp"), count, 0)
+
+
+def gather_deep(array):
+    return in_turn([array] + [turn_mp(array, shift) for shift in range(1, lax.axis_size("mp"))])
+
+
+def sum_flat(array):
+    for swap in (to_core, to_x, to_y):
+        array = array + swap(array)
+    return array
+
+
+def bring(order, shard, quarter, core):
+    count = lax.axis_size("mp")
+    part = pick(pick(shard.reshape(4, 2, -1, D), quarter, 0), core, 0)
+    return lax.all_gather(order.after(part), "mp")
+
+
+def others(whole):
+    count = lax.axis_size("mp")
+    twice = jnp.concatenate([whole, whole], 0)
+    return lax.dynamic_slice_in_dim(twice, lax.axis_index("mp") + 1, count - 1, 0)
+
+
+def assemble_weight(shard, parts, swapped, core, shard_major, split):
+    count = lax.axis_size("mp")
+    rows = shard.shape[0] // 8
+
+    def spot(shard_index, quarter):
+        shard_index = lax.rem(lax.axis_index("mp") + shard_index, count)
+        return shard_index * 4 + quarter if shard_major else quarter * count + shard_index
+
+    if swapped is None:
+        mine = pick(shard.reshape(4, 2, rows, D), core, 1)
+    else:
+        mine = shard.reshape(4, 2 * rows, D)
+    steps = [((mine, n),) for n in range(4)]
+    targets = [spot(0, n) for n in range(4)]
+    for n, (array, quarter, first) in enumerate(parts):
+        for k in range(array.shape[0]):
+            steps.append(((array, k),) if swapped is None else ((array, k), (swapped[n], k)))
+            targets.append(spot(first + k, quarter))
+    rows = mine.shape[1]
+    whole = assemble(steps, targets, core, rows, count * 4, split or count * 4)
+    return [array.reshape(-1, D) for array in whole]
+
+
+def cut_corner(grad, quarter):
+    corner = pick(grad, quarter ^ 3, 0)
+    half = corner.shape[0] // 2
+    return corner[:half], corner[half:]
+
+
+def cut_sides(grad, quarter, add_y, add_x):
+    half = add_y.shape[0]
+    for_y = pick(grad, quarter ^ 2, 0)
+    for_x = pick(grad, quarter ^ 1, 0)
+    for_y = jnp.concatenate([for_y[:half] + add_y, for_y[half:]], 0)
+    for_x = jnp.concatenate([for_x[:half], for_x[half:] + add_x], 0)
+    return for_x, for_y
+
+
+def sum_deep(order, grad, quarter, from_x, from_y):
+    own = pick(grad, quarter, 0) + from_x + from_y
+    return lax.psum_scatter(order.after(own), "mp", scatter_dimension=0, tiled=False)
+
+
+def hold(parts, quarter):
+    own, from_x, from_y, corner_one, corner_two = parts
+    held = jnp.zeros((4,) + own.shape, jnp.float32)
+    corner = jnp.concatenate([corner_one, corner_two], 0)
+    for turn, array in enumerate((own, from_x, from_y, corner)):
+        held = lax.dynamic_update_slice(held, array[None], (quarter ^ turn, jnp.int32(0), jnp.int32(0)))
+    return held
+
+
+def interleave(held, other, core):
+    low_core = jnp.where(core == 0, held, other)
+    high_core = jnp.where(core == 0, other, held)
+    return jnp.stack([low_core, high_core], 1).reshape(-1, D)
+
+
+class Tensor:
+    def __init__(self, grad, weight, row_state, col_state, axis):
+        self.grad, self.weight, self.axis = grad, weight, axis
+        self.row_state, self.col_state = row_state, col_state
+        self.leading = grad.shape[0]
+        self.rows_full = row_state.shape[1]
+        self.cols_full = col_state.shape[1]
+        squares = grad * grad + moment_eps
+        row_sum, col_sum = jnp.sum(squares, 2), jnp.sum(squares, 1)
+        start = lax.axis_index("mp") * grad.shape[axis]
+        if axis == 1:
+            state = lax.dynamic_slice_in_dim(row_state, start, grad.shape[1], 1)
+            self.near = 0.5 * state + 0.5 * (row_sum / self.cols_full)
+            self.partial = col_sum
+        else:
+            state = lax.dynamic_slice_in_dim(col_state, start, grad.shape[2], 1)
+            self.near = 0.5 * state + 0.5 * (col_sum / self.rows_full)
+            self.partial = row_sum
+
+    def sent(self):
+        return [self.near.reshape(-1), self.partial.reshape(-1)]
+
+    def received(self, near, partial):
+        near = near.reshape(near.shape[0], self.leading, -1).transpose(1, 0, 2)
+        near = near.reshape(self.leading, -1)
+        total = jnp.sum(partial, 0).reshape(self.leading, -1)
+        if self.axis == 1:
+            self.row_new = near
+            self.col_new = 0.5 * self.col_state + 0.5 * (total / self.rows_full)
+            row_piece, col_piece = self.near, self.col_new
+        else:
+            self.col_new = near
+            self.row_new = 0.5 * self.row_state + 0.5 * (total / self.cols_full)
+            row_piece, col_piece = self.row_new, self.near
+        row_mean = jnp.mean(self.row_new, 1)
+        self.row_scale = lax.rsqrt(row_piece / row_mean[:, None])
+        self.col_scale = lax.rsqrt(col_piece)
+        update = self.update()
+        self.step_sq = jnp.sum(update * update)
+
+    def update(self):
+        return self.grad * self.row_scale[:, :, None] * self.col_scale[:, None, :]
+
+
+def exchange(tensors, extra):
+    pieces = [part for tensor in tensors for part in tensor.sent()]
+    whole = gather_deep(jnp.concatenate(pieces + [extra]))
+    offset = 0
+    for tensor in tensors:
+        parts = []
+        for part in tensor.sent():
+            parts.append(whole[:, offset : offset + part.shape[0]])
+            offset = offset + part.shape[0]
+        tensor.received(*parts)
+    return whole[:, offset:]
+
+
+def head_windows():
+    spans = []
+    for head in range(D // HEAD_DIM):
+        first = head * HEAD_DIM
+        start = first // 128 * 128
+        stop = -(-(first + HEAD_DIM) // 128) * 128
+        spans.append((first, start, stop - start))
+    return spans
+
+
+def head_mask(first, start, width):
+    lanes = start + lax.broadcasted_iota(jnp.int32, (SEQ, width), 1)
+    return (lanes >= first) & (lanes < first + HEAD_DIM)
+
+
+def dot_nt(left_side, right_side):
+    return lax.dot_general(
+        left_side, right_side, (((1,), (1,)), ((), ())), preferred_element_type=jnp.float32
+    )
+
+
+def attend_kernel(qkv_ref, out_ref, total):
+    total[...] = jnp.zeros_like(total)
+    for first, start, width in head_windows():
+        keep = head_mask(first, start, width)
+        query = qkv_ref[0, :, start : start + width]
+        key = jnp.where(keep, qkv_ref[0, :, D + start : D + start + width], 0)
+        value = jnp.where(keep, qkv_ref[0, :, 2 * D + start : 2 * D + start + width], 0)
+        scores = dot_nt(query, key) * HEAD_DIM ** (-0.5)
+        expo = jnp.exp(scores - jnp.max(scores, 1, keepdims=True))
+        probs = (expo / jnp.sum(expo, 1, keepdims=True)).astype(jnp.bfloat16)
+        total[:, start : start + width] += matmul(probs, value)
+    out_ref[0] = total[...].astype(jnp.bfloat16)
+
+
+def attend(qkv):
+    images = qkv.shape[0]
+    return pl.pallas_call(
+        attend_kernel,
+        grid=(images,),
+        in_specs=[pl.BlockSpec((1, SEQ, 3 * D), lambda i: (i, 0, 0))],
+        out_specs=pl.BlockSpec((1, SEQ, D), lambda i: (i, 0, 0)),
+        out_shape=jax.ShapeDtypeStruct((images, SEQ, D), jnp.bfloat16),
+        scratch_shapes=[pltpu.VMEM((SEQ, D), jnp.float32)],
+        compiler_params=pltpu.CompilerParams(vmem_limit_bytes=40 * 1024 * 1024),
+        cost_estimate=pl.CostEstimate(
+            flops=images * 4 * SEQ * SEQ * 256 * 16,
+            bytes_accessed=images * SEQ * D * 8,
+            transcendentals=images * 16 * SEQ * SEQ,
+        ),
+    )(qkv)
+
+
+def attend_back_kernel(qkv_ref, grad_ref, out_ref, query_sum, key_sum, value_sum):
+    scale = HEAD_DIM ** (-0.5)
+    for ref in (query_sum, key_sum, value_sum):
+        ref[...] = jnp.zeros_like(ref)
+    for first, start, width in head_windows():
+        span = slice(start, start + width)
+        keep = head_mask(first, start, width)
+        query = jnp.where(keep, qkv_ref[0, :, span], 0)
+        key = jnp.where(keep, qkv_ref[0, :, D + start : D + start + width], 0)
+        value = jnp.where(keep, qkv_ref[0, :, 2 * D + start : 2 * D + start + width], 0)
+        above = jnp.where(keep, grad_ref[0, :, span], 0)
+        scores = dot_nt(key, query) * scale
+        expo = jnp.exp(scores - jnp.max(scores, 0, keepdims=True))
+        probs = expo / jnp.sum(expo, 0, keepdims=True)
+        prob_grad = dot_nt(value, above)
+        inner = jnp.sum(probs * prob_grad, 0, keepdims=True)
+        score_grad = (probs * (prob_grad - inner)).astype(jnp.bfloat16)
+        value_sum[:, span] += matmul(probs.astype(jnp.bfloat16), above)
+        key_sum[:, span] += matmul(score_grad, query) * scale
+        query_sum[:, span] += (
+            lax.dot_general(
+                score_grad, key, (((0,), (0,)), ((), ())), preferred_element_type=jnp.float32
+            )
+            * scale
+        )
+    out_ref[0, :, :D] = query_sum[...].astype(jnp.bfloat16)
+    out_ref[0, :, D : 2 * D] = key_sum[...].astype(jnp.bfloat16)
+    out_ref[0, :, 2 * D :] = value_sum[...].astype(jnp.bfloat16)
+
+
+def attend_back(qkv, grad):
+    images = qkv.shape[0]
+    return pl.pallas_call(
+        attend_back_kernel,
+        grid=(images,),
+        in_specs=[
+            pl.BlockSpec((1, SEQ, 3 * D), lambda i: (i, 0, 0)),
+            pl.BlockSpec((1, SEQ, D), lambda i: (i, 0, 0)),
+        ],
+        out_specs=pl.BlockSpec((1, SEQ, 3 * D), lambda i: (i, 0, 0)),
+        out_shape=jax.ShapeDtypeStruct((images, SEQ, 3 * D), jnp.bfloat16),
+        scratch_shapes=[pltpu.VMEM((SEQ, D), jnp.float32)] * 3,
+        compiler_params=pltpu.CompilerParams(vmem_limit_bytes=40 * 1024 * 1024),
+        cost_estimate=pl.CostEstimate(
+            flops=images * 10 * SEQ * SEQ * 256 * 16,
+            bytes_accessed=images * SEQ * D * 14,
+            transcendentals=images * 16 * SEQ * SEQ,
+        ),
+    )(qkv, grad)
+
+
+def body_data(
+    block_input,
+    skip_input,
+    timesteps,
+    class_labels,
+    loss_weights,
+    grad_output,
+    skip_weight,
+    qkv_weight,
+    proj_weight,
+    fc1_weight,
+    fc2_weight,
+    vectors,
+    hidden_bias,
+    skip_rows,
+    skip_cols,
+    qkv_rows,
+    qkv_cols,
+    proj_rows,
+    proj_cols,
+    fc1_rows,
+    fc1_cols,
+    fc2_rows,
+    fc2_cols,
+    vector_moments,
+    hidden_moments,
+):
+    image_count = timesteps.shape[0]
+    mp_count = lax.axis_size("mp")
+    dp_count = lax.axis_size("dp")
+    mp_index = lax.axis_index("mp")
+    dp_index = lax.axis_index("dp")
+    core = lax.rem(dp_index, 2)
+    quarter = lax.div(dp_index, 2)
+    images = image_count // mp_count
+    tokens = images * SEQ
+    width_local = qkv_weight.shape[2]
+    hidden_local = fc1_weight.shape[1]
+    hidden_slice = hidden_local // dp_count
+    order = Order()
+
+    skip_shard = skip_weight.reshape(-1, D)
+    skip_whole = bring(order, skip_shard, quarter, core)
+    hidden_all = gather_deep(hidden_bias)
+
+    angles = (timesteps.astype(jnp.float32) + 0.5) * (0.5 * math.pi / total_steps)
+    alpha_sq = jnp.square(jnp.cos(angles))
+    sigma_sq = jnp.square(jnp.sin(angles))
+    snr_weight = 5.0 * sigma_sq / jnp.maximum(alpha_sq, 5.0 * sigma_sq)
+    base_weight = loss_weights * snr_weight
+    one_hot = (class_labels[:, None] == jnp.arange(CLASSES, dtype=jnp.int32)[None, :]).astype(
+        jnp.float32
+    )
+    batch = jnp.concatenate([jnp.sum(one_hot, 0), jnp.sum(base_weight)[None]])
+
+    attn_shard = jnp.concatenate(
+        [qkv_weight.transpose(0, 2, 1).reshape(3 * width_local, D), proj_weight], 0
+    )
+    attn_shard = order.mark(attn_shard)
+    attn_whole = bring(order, attn_shard, quarter, core)
+    batch = order.mark(batch + to_core(batch))
+    batch_x = to_x(batch)
+    fc1_shard = order.mark(fc1_weight.T)
+    fc2_shard = fc2_weight
+    batch = order.mark(batch + batch_x)
+    batch_y = to_y(batch)
+    start = mp_index * tokens
+    block_local = lax.dynamic_slice_in_dim(block_input, start, tokens, 0)
+    skip_local = lax.dynamic_slice_in_dim(skip_input, start, tokens, 0)
+    both_inputs = jnp.stack(
+        [
+            block_local.reshape(tokens, mp_count, width_local),
+            skip_local.reshape(tokens, mp_count, width_local),
+        ],
+        2,
+    ).reshape(tokens, -1)
+    both_inputs = order.mark(both_inputs)
+    batch = order.mark(batch + batch_y)
+
+    skip_own = others(order.mark(skip_whole))
+    skip_x, skip_y = swap_plane(order, skip_own, skip_own)
+    skip_swapped = [to_core(skip_own)]
+    fc1_whole = bring(order, fc1_shard, quarter, core)
+    hidden_own = pick(hidden_all.reshape(mp_count, 4, 2, hidden_slice), core, 2)
+    hidden_own = hidden_own.transpose(1, 0, 2).reshape(-1)
+    own_count = jnp.dot(one_hot, batch[:CLASSES], precision=lax.Precision.HIGHEST)
+    item_weight = base_weight * lax.rsqrt(own_count)
+    hidden_own, item_weight = order.mark(hidden_own, item_weight)
+    batch_scale = image_count * dp_count / batch[CLASSES]
+    grad_local = lax.dynamic_slice_in_dim(grad_output, start, tokens, 0)
+    item_local = lax.dynamic_slice_in_dim(item_weight, mp_index * images, images, 0)
+    upstream = (
+        grad_local.astype(jnp.float32).reshape(images, SEQ, D) * item_local[:, None, None]
+    ).reshape(-1, D)
+    upstream = order.mark(upstream)
+
+    skip_x, skip_y = order.mark(skip_x, skip_y)
+    skip_one, skip_two = swap_plane(order, skip_y[:2], skip_x[2:])
+    skip_swapped = skip_swapped + [to_core(skip_x), to_core(skip_y)]
+    skip_one, skip_two = order.mark(skip_one, skip_two)
+    skip_swapped = skip_swapped + [to_core(skip_one), to_core(skip_two)]
+    attn_own = others(order.mark(attn_whole))
+    attn_x, attn_y = swap_plane(order, attn_own, attn_own)
+    fc2_whole = bring(order, fc2_shard, quarter, core)
+    skip_swapped = order.mark(*skip_swapped)
+    attn_swapped = [to_core(order.after(attn_own))]
+    skip_parts = [
+        (skip_own, quarter, 1),
+        (skip_x, quarter ^ 1, 1),
+        (skip_y, quarter ^ 2, 1),
+        (skip_one, quarter ^ 3, 1),
+        (skip_two, quarter ^ 3, 3),
+    ]
+    (skip_low,) = assemble_weight(skip_shard, skip_parts, skip_swapped, core, True, 0)
+    joined = matmul(both_inputs, skip_low) + vectors[4]
+    normed, normal_one, inverse_one = norm_forward(joined, vectors[0], vectors[1])
+    normed_low = normed.astype(jnp.bfloat16)
+    joined, normed_low, normal_one = order.mark(joined, normed_low, normal_one)
+    upstream_other = to_core(order.after(upstream))
+
+    attn_x, attn_y = order.mark(attn_x, attn_y)
+    attn_one, attn_two = swap_plane(order, attn_y[:1], attn_x[1:])
+    attn_swapped = attn_swapped + [to_core(attn_x), to_core(attn_y)]
+    upstream_other = order.mark(upstream_other) * batch_scale
+    upstream = upstream * batch_scale
+    upstream_low = jnp.concatenate([upstream, upstream_other], 0).astype(jnp.bfloat16)
+    upstream_low = order.mark(upstream_low)
+    fc1_own = others(order.mark(fc1_whole))
+    fc1_x, fc1_y = swap_plane(order, fc1_own, fc1_own)
+    attn_one, attn_two = order.mark(attn_one, attn_two)
+    attn_swapped = attn_swapped + [to_core(attn_one), to_core(attn_two)]
+    attn_parts = [
+        (attn_own, quarter, 1),
+        (attn_x, quarter ^ 1, 1),
+        (attn_y, quarter ^ 2, 1),
+        (attn_one, quarter ^ 3, 1),
+        (attn_two, quarter ^ 3, 2),
+    ]
+    attn_swapped = order.mark(*attn_swapped)
+    qkv_low, proj_low = assemble_weight(
+        attn_shard, attn_parts, attn_swapped, core, False, 3 * mp_count
+    )
+    qkv_all = jnp.einsum(
+        "itd,ed->ite",
+        normed_low.reshape(images, SEQ, D),
+        qkv_low,
+        preferred_element_type=jnp.float32,
+    ).astype(jnp.bfloat16)
+    qkv_all = order.mark(qkv_all)
+    fc2_own = others(order.mark(fc2_whole))
+    fc1_x, fc1_y = order.mark(fc1_x, fc1_y)
+    fc1_one, fc1_two = swap_plane(order, fc1_y[:2], fc1_x[2:])
+    fc2_x, fc2_y = swap_plane(order, fc2_own, fc2_own)
+    attended = attend(order.after(qkv_all)).reshape(tokens, D)
+    residual = joined + matmul(attended, proj_low) + vectors[5]
+    normed_two, normal_two, inverse_two = norm_forward(residual, vectors[2], vectors[3])
+    residual, normed_two, normal_two = order.mark(residual, normed_two, normal_two)
+    normed_two_other = to_core(normal_two)
+    fc1_one, fc1_two = order.mark(fc1_one, fc1_two)
+    fc1_parts = [
+        (fc1_own, quarter, 1),
+        (fc1_x, quarter ^ 1, 1),
+        (fc1_y, quarter ^ 2, 1),
+        (fc1_one, quarter ^ 3, 1),
+        (fc1_two, quarter ^ 3, 3),
+    ]
+    (fc1_low,) = assemble_weight(fc1_shard, fc1_parts, None, core, False, 0)
+    fc1_low = order.mark(fc1_low)
+    normed_two_other = order.mark(normed_two_other) * vectors[2] + vectors[3]
+    normed_two_low = jnp.concatenate([normed_two, normed_two_other], 0).astype(jnp.bfloat16)
+    normed_two_low = order.mark(normed_two_low)
+    fc2_x, fc2_y = order.mark(fc2_x, fc2_y)
+    fc2_one, fc2_two = swap_plane(order, fc2_y[:1], fc2_x[1:])
+    pre_act = (
+        jnp.einsum("td,fd->tf", normed_two_low, fc1_low, preferred_element_type=jnp.float32)
+        + hidden_own
+    )
+    activated, gelu_pull = jax.vjp(gelu_exact, pre_act)
+    activated_low = activated.astype(jnp.bfloat16)
+    fc2_grad = jnp.einsum(
+        "tf,td->fd", activated_low, upstream_low, preferred_element_type=jnp.float32
+    ).reshape(4, mp_count, hidden_slice, D)
+    fc2_grad = order.mark(fc2_grad)
+    fc2_add = swap_plane(order, *cut_corner(fc2_grad, quarter))
+
+    fc2_one, fc2_two = order.mark(fc2_one, fc2_two)
+    fc2_parts = [
+        (fc2_own, quarter, 1),
+        (fc2_x, quarter ^ 1, 1),
+        (fc2_y, quarter ^ 2, 1),
+        (fc2_one, quarter ^ 3, 1),
+        (fc2_two, quarter ^ 3, 2),
+    ]
+    (fc2_low,) = assemble_weight(fc2_shard, fc2_parts, None, core, False, 0)
+    fc2_low = order.mark(fc2_low)
+    act_grad = jnp.einsum("td,fd->tf", upstream_low, fc2_low, preferred_element_type=jnp.float32)
+    pre_grad = gelu_pull(act_grad)[0]
+    hidden_grad = jnp.sum(pre_grad, 0)
+    pre_low, hidden_grad = order.mark(pre_grad.astype(jnp.bfloat16), hidden_grad)
+    back_part = order.mark(matmul(pre_low, fc1_low))
+    back_other = to_core(back_part[tokens:])
+    fc2_add = order.mark(*fc2_add)
+    fc2_sides = swap_plane(order, *cut_sides(fc2_grad, quarter, *fc2_add))
+    fc1_grad = jnp.einsum(
+        "tf,td->fd",
+        order.after(pre_low),
+        normed_two_low,
+        preferred_element_type=jnp.float32,
+    ).reshape(4, mp_count, hidden_slice, D)
+    fc1_grad = order.mark(fc1_grad)
+    fc1_add = swap_plane(order, *cut_corner(fc1_grad, quarter))
+    norm_two_in = back_part[:tokens] + order.mark(back_other)
+    back_two, gain_two_grad, bias_two_grad = norm_backward(
+        norm_two_in, normal_two, inverse_two, vectors[2]
+    )
+    residual_grad = upstream + back_two
+    residual_low = residual_grad.astype(jnp.bfloat16)
+    residual_grad, residual_low = order.mark(residual_grad, residual_low)
+    forward_part = order.mark(matmul(order.after(activated_low), fc2_low))
+    forward_other = to_core(forward_part[tokens:])
+    attended_grad = jnp.einsum(
+        "td,ed->te", residual_low, proj_low, preferred_element_type=jnp.float32
+    ).astype(jnp.bfloat16)
+    attended_grad = order.mark(attended_grad)
+    block_own = residual + forward_part[:tokens] + order.mark(forward_other)
+    block_all = lax.all_gather(order.mark(block_own), "mp")
+    qkv_grad_low = attend_back(
+        qkv_all, order.after(attended_grad).reshape(images, SEQ, D)
+    ).reshape(tokens, 3 * D)
+    qkv_grad_low = order.mark(qkv_grad_low)
+    fc1_add = order.mark(*fc1_add)
+    fc1_sides = swap_plane(order, *cut_sides(fc1_grad, quarter, *fc1_add))
+    fc2_sides = order.mark(*fc2_sides)
+    fc2_piece = sum_deep(order, fc2_grad, quarter, *fc2_sides)
+
+    def by_core(array, leading):
+        return array.reshape(tokens, leading, mp_count, 2, -1)
+
+    def attn_half(which):
+        left = pick(by_core(qkv_grad_low, 3), which, 3).reshape(tokens, -1)
+        first = jnp.einsum("te,td->ed", left, normed_low, preferred_element_type=jnp.float32)
+        left = pick(by_core(attended, 1), which, 3).reshape(tokens, -1)
+        second = jnp.einsum("te,td->ed", left, residual_low, preferred_element_type=jnp.float32)
+        return first, second
+
+    attn_given = order.mark(*attn_half(1 - core))
+    attn_given = [to_core(array) for array in attn_given]
+    norm_one_in = matmul(order.after(qkv_grad_low), qkv_low)
+    back_one, gain_one_grad, bias_one_grad = norm_backward(
+        norm_one_in, normal_one, inverse_one, vectors[0]
+    )
+    joined_grad = residual_grad + back_one
+    joined_low = joined_grad.astype(jnp.bfloat16)
+    joined_grad, joined_low = order.mark(joined_grad, joined_low)
+    attn_kept = order.mark(*attn_half(core))
+
+    inputs_view = both_inputs.reshape(tokens, mp_count, 4, 2, -1).transpose(0, 2, 1, 3, 4)
+
+    def skip_half(which):
+        left = pick(inputs_view, which, 3).reshape(tokens, -1)
+        return jnp.einsum("te,td->ed", left, joined_low, preferred_element_type=jnp.float32)
+
+    skip_given = order.mark(skip_half(1 - core))
+    skip_given = to_core(skip_given)
+    attn_given = order.mark(*attn_given)
+    attn_grad = jnp.concatenate(
+        [kept + given for kept, given in zip(attn_kept, attn_given)], 0
+    ).reshape(4, mp_count, hidden_slice, D)
+    attn_grad = order.mark(attn_grad)
+    attn_add = swap_plane(order, *cut_corner(attn_grad, quarter))
+    skip_shards = skip_low.reshape(mp_count, 2 * width_local, D)
+    both_grads = []
+    for shift in (1, 2, 3, 0):
+        shard_low = pick(skip_shards, lax.rem(mp_index + shift, mp_count), 0)
+        both = jnp.einsum("td,cd->tc", joined_low, shard_low, preferred_element_type=jnp.float32)
+        both = order.mark(both)
+        both_grads.append(turn_mp(both, shift) if shift == 1 else both)
+    skip_kept = order.mark(skip_half(core))
+    skip_grad = order.mark((skip_kept + order.mark(skip_given)).reshape(4, mp_count, -1, D))
+
+    fc1_sides = order.mark(*fc1_sides)
+    fc1_piece = sum_deep(order, fc1_grad, quarter, *fc1_sides)
+    attn_add = order.mark(*attn_add)
+    attn_sides = swap_plane(order, *cut_sides(attn_grad, quarter, *attn_add))
+    skip_add = swap_plane(order, *cut_corner(skip_grad, quarter))
+    both_grads[0] = order.mark(both_grads[0])
+    both_grads[1] = turn_mp(order.after(both_grads[1]), 2)
+    vector_grad = jnp.stack(
+        [
+            gain_one_grad,
+            bias_one_grad,
+            gain_two_grad,
+            bias_two_grad,
+            jnp.sum(joined_grad, 0),
+            jnp.sum(residual_grad, 0),
+            jnp.sum(upstream, 0),
+        ]
+    )
+    hidden_grad = hidden_grad.reshape(4, mp_count, 1, hidden_slice).transpose(1, 0, 2, 3)
+    hidden_grad = jnp.where(jnp.arange(2)[None, None, :, None] == core, hidden_grad, 0.0)
+    small = order.mark(jnp.concatenate([vector_grad.reshape(-1), hidden_grad.reshape(-1)]))
+    skip_add = order.mark(*skip_add)
+    skip_sides = swap_plane(order, *cut_sides(skip_grad, quarter, *skip_add))
+    attn_sides = order.mark(*attn_sides)
+    attn_piece = sum_deep(order, attn_grad, quarter, *attn_sides)
+    small = order.mark(small + to_core(small))
+    both_grads[1] = order.mark(both_grads[1])
+    both_grads[2] = turn_mp(order.after(both_grads[2]), 3)
+    block_all = order.mark(block_all)
+    block_output = (block_all.reshape(-1, D) + vectors[6]).astype(jnp.bfloat16)
+    block_output = order.mark(block_output)
+    half = hidden_slice // 2
+
+    def spread(piece):
+        return swap_plane(order, piece, piece)
+
+    def spread_far(near):
+        half = near[0].shape[0] // 2
+        return swap_plane(order, near[1][:half], near[0][half:])
+
+    fc2_piece = order.mark(fc2_piece)
+    fc2_near = spread(fc2_piece)
+    small_x = to_x(order.after(small))
+    skip_sides = order.mark(*skip_sides)
+    skip_piece = sum_deep(order, skip_grad, quarter, *skip_sides)
+    fc2_near = order.mark(*fc2_near)
+    fc2_far = spread_far(fc2_near)
+    small = order.mark(small + small_x)
+    small_y = to_y(small)
+    fc1_piece = order.mark(fc1_piece)
+    fc1_near = spread(fc1_piece)
+    fc2_far = order.mark(*fc2_far)
+    fc2_held = order.mark(hold((fc2_piece, *fc2_near, *fc2_far), quarter))
+    fc2_other = to_core(fc2_held)
+    small = order.mark(small + small_y)
+    small = order.mark(jnp.sum(gather_deep(small), 0))
+    fc1_near = order.mark(*fc1_near)
+    fc1_far = spread_far(fc1_near)
+    both_grads[2] = order.mark(both_grads[2])
+    input_grads = in_turn([both_grads[3]] + both_grads[:3])
+    input_grad = input_grads[:, :, :width_local].reshape(-1, width_local)
+    skip_input_grad = input_grads[:, :, width_local:].reshape(-1, width_local)
+    input_grad, skip_input_grad = order.mark(input_grad, skip_input_grad)
+    fc2_sum = interleave(fc2_held, order.mark(fc2_other), core)
+    fc2_part = Tensor(fc2_sum[None], fc2_weight[None], fc2_rows[None], fc2_cols[None], 1)
+    fc1_far = order.mark(*fc1_far)
+    fc1_held = order.mark(hold((fc1_piece, *fc1_near, *fc1_far), quarter))
+    fc1_other = to_core(fc1_held)
+    attn_piece = order.mark(attn_piece)
+    attn_near = spread(attn_piece)
+    fc1_sum = interleave(fc1_held, order.mark(fc1_other), core).T
+    fc1_part = Tensor(fc1_sum[None], fc1_weight[None], fc1_rows[None], fc1_cols[None], 2)
+    weight_sq = jnp.stack(
+        [
+            jnp.sum(array * array)
+            for array in (skip_weight, qkv_weight, proj_weight, fc1_weight, fc2_weight, hidden_bias)
+        ]
+    )
+    weight_sq = order.mark(weight_sq)
+    weight_sq = jnp.sum(exchange([fc2_part, fc1_part], weight_sq), 0)
+    fc2_part.step_sq, fc1_part.step_sq = order.mark(fc2_part.step_sq, fc1_part.step_sq)
+    attn_near = order.mark(*attn_near)
+    attn_far = spread_far(attn_near)
+    skip_piece = order.mark(skip_piece)
+    skip_near = spread(skip_piece)
+    attn_far = order.mark(*attn_far)
+    attn_held = order.mark(hold((attn_piece, *attn_near, *attn_far), quarter))
+    attn_other = to_core(attn_held)
+    skip_near = order.mark(*skip_near)
+    skip_far = spread_far(skip_near)
+    attn_sum = interleave(attn_held, order.mark(attn_other), core)
+    qkv_sum = attn_sum[: 3 * width_local].reshape(3, width_local, D).transpose(0, 2, 1)
+    proj_sum = attn_sum[3 * width_local :]
+    qkv_sum, proj_sum = order.mark(qkv_sum, proj_sum)
+    skip_far = order.mark(*skip_far)
+    skip_held = order.mark(hold((skip_piece, *skip_near, *skip_far), quarter))
+    skip_other = to_core(skip_held)
+    qkv_part = Tensor(qkv_sum, qkv_weight, qkv_rows, qkv_cols, 2)
+    proj_part = Tensor(proj_sum[None], proj_weight[None], proj_rows[None], proj_cols[None], 1)
+    skip_sum = interleave(skip_held, order.mark(skip_other), core).reshape(2, width_local, D)
+    skip_part = Tensor(skip_sum, skip_weight, skip_rows, skip_cols, 1)
+    exchange([qkv_part, proj_part, skip_part], jnp.zeros((128,), jnp.float32))
+
+    vector_sum = small[: 7 * D].reshape(7, D)
+    hidden_sum = lax.dynamic_slice_in_dim(small[7 * D :], mp_index * hidden_local, hidden_local, 0)
+    vector_new = 0.5 * vector_moments + 0.5 * (vector_sum * vector_sum + moment_eps)
+    vector_update = vector_sum * lax.rsqrt(vector_new)
+    hidden_new = 0.5 * hidden_moments + 0.5 * (hidden_sum * hidden_sum + moment_eps)
+    hidden_update = hidden_sum * lax.rsqrt(hidden_new)
+    parts = [skip_part, qkv_part, proj_part, fc1_part, fc2_part]
+    step_sq = jnp.sum(hidden_update * hidden_update)
+    for part in parts:
+        step_sq = step_sq + part.step_sq
+    step_total = jnp.sum(gather_deep(jnp.broadcast_to(step_sq, (128,)))[:, 0])
+    step_total = step_total + jnp.sum(vector_update * vector_update)
+    param_count = 6.0 * D * D + 2.0 * D * FF + 7.0 * D + FF
+    update_rms = jnp.sqrt(step_total / param_count)
+    divisor = jnp.maximum(1.0, update_rms / clip_level)
+    tensor_sizes = (2.0 * D * D, 3.0 * D * D, 1.0 * D * D, 1.0 * D * FF, 1.0 * FF * D)
+    new_weights = []
+    for position, part in enumerate(parts):
+        weight_rms = jnp.sqrt(weight_sq[position] / tensor_sizes[position])
+        factor = step_rate * jnp.maximum(0.001, weight_rms) / divisor
+        new_weights.append(part.weight - factor * part.update())
+    vector_rms = jnp.sqrt(jnp.mean(vectors * vectors, 1, keepdims=True))
+    vectors_new = vectors - step_rate * jnp.maximum(0.001, vector_rms) * vector_update / divisor
+    hidden_rms = jnp.sqrt(weight_sq[5] / FF)
+    hidden_bias_new = (
+        hidden_bias - step_rate * jnp.maximum(0.001, hidden_rms) * hidden_update / divisor
+    )
+    skip_new, qkv_new = new_weights[0], new_weights[1]
+    proj_new, fc1_new, fc2_new = (array[0] for array in new_weights[2:])
+    piece_width = D // dp_count
+    dp_start = dp_index * piece_width
+
+    def own_piece(array, axis):
+        return lax.dynamic_slice_in_dim(array, dp_start, piece_width, axis)
+
+    return (
+        block_output,
+        input_grad,
+        skip_input_grad,
+        own_piece(skip_sum, 2),
+        own_piece(qkv_sum, 1),
+        own_piece(proj_sum, 1),
+        own_piece(fc1_sum, 0),
+        own_piece(fc2_sum, 1),
+        own_piece(vector_sum, 1),
+        hidden_sum,
+        skip_part.row_new,
+        skip_part.col_new,
+        qkv_part.row_new,
+        qkv_part.col_new,
+        proj_part.row_new[0],
+        proj_part.col_new[0],
+        fc1_part.row_new[0],
+        fc1_part.col_new[0],
+        fc2_part.row_new[0],
+        fc2_part.col_new[0],
+        vector_new,
+        hidden_new,
+        skip_new,
+        qkv_new,
+        proj_new,
+        fc1_new,
+        fc2_new,
+        vectors_new,
+        hidden_bias_new,
+        skip_new.astype(jnp.bfloat16),
+        qkv_new.astype(jnp.bfloat16),
+        proj_new.astype(jnp.bfloat16),
+        fc1_new.astype(jnp.bfloat16),
+        fc2_new.astype(jnp.bfloat16),
+        update_rms,
+    )
+
+
 def solution(mesh):
     placed = (
         P("dp", None),

time: 2300 us -> 1160 us (0.50)
  waiting for transfers between devices: 1750 us -> 349 us
  local copies, waits for them, and re-layouts: 104 us -> 260 us
  starting transfers between devices: 0.25 us -> 84.4 us
  other arithmetic: 166 us -> 238 us
  matrix products: 191 us -> 130 us
  Pallas kernels: 0 us -> 55.4 us
  blocking collectives: 52.9 us -> 0 us
    psum x6 -> x0, waiting for transfers between devices: 1750 us -> none  [the longest x1 596 us: body(): lax.psum(matmul(activated_low, fc2_low), 'mp')]
    ppermute x0 -> x93, waiting for transfers between devices: none -> 341 us  [the longest x26 257 us: to_x(): return lax.ppermute(array, 'dp', [(i, i ^ 2) for i in range(8)])]
    ppermute x0 -> x93, starting transfers between devices: none -> 83.3 us  [the longest x26 28.7 us: to_y(): return lax.ppermute(array, 'dp', [(i, i ^ 4) for i in range(8)])]
    pallas_call x0 -> x6, Pallas kernels: none -> 55.4 us  [the longest x4 29.9 us: assemble(): pl.pallas_call(kernel, in_specs=[pl.BlockSpec(memory_space=pltpu.SMEM)] +...]
    psum x3 -> x0, blocking collectives: 52.9 us -> none  [the longest x1 26.8 us: body(): lax.psum((skip_grad, qkv_grad, proj_grad, fc1_grad, fc2_grad, vector_grad...]
    add x5 -> x21, other arithmetic: 2.97 us -> 55.1 us  [the longest x4 19 us: sum_deep(): own = pick(grad, quarter, 0) + from_x + from_y]
    dot_general x20 -> x17, matrix products: 143 us -> 97.6 us  [the longest x1 14.7 us: body_data(): jnp.einsum('td,fd->tf', upstream_low, fc2_low, preferred_element_type=jnp...]
    slice x3 -> x32, local copies, waits for them, and re-layouts: 2.54 us -> 43.5 us  [the longest x4 16.7 us: cut_sides(): for_y = jnp.concatenate([for_y[:half] + add_y, for_y[half:]], 0)]
  transfers between devices with their start and end apart: 6 -> 102, of which waited for: 6 -> 37; matrix products, arithmetic and copies ran while one was open for 4% -> 44% of each run, Pallas kernels for 0% -> 4%
where the time goes in v1:
time: 1160 us; the launch traced here: 1150 us
  waiting for transfers between devices  349 us (30%)
  local copies, waits for them, and re-layouts  260 us (22%)
  other arithmetic  238 us (21%)
  matrix products  130 us (11%)
  starting transfers between devices  84.4 us (7%)
  Pallas kernels  55.4 us (5%)
  between operations  29.2 us (3%)
    ppermute x26, waiting for transfers between devices, to_x(): return lax.ppermute(array, 'dp', [(i, i ^ 2) for i in range(8)])  257 us
    unnamed x215, local copies, waits for them, and re-layouts  73.3 us
    ppermute x26, waiting for transfers between devices, to_y(): return lax.ppermute(array, 'dp', [(i, i ^ 4) for i in range(8)])  48.5 us
    ppermute x18, waiting for transfers between devices, turn_mp(): lax.ppermute(array, 'mp', [(i, (i + shift) % count) for i in range(count)])  35.5 us
    dot_general x5, matrix products, matmul(): return jnp.dot(left_side, right_side, preferred_element_type=jnp.float32)  31.9 us
    pallas_call x4, Pallas kernels, assemble(): pl.pallas_call(kernel, in_specs=[pl.BlockSpec(memory_space=pltpu.SMEM)] +...  29.9 us
    ppermute x26, starting transfers between devices, to_y(): return lax.ppermute(array, 'dp', [(i, i ^ 4) for i in range(8)])  28.7 us
    ppermute x26, starting transfers between devices, to_x(): return lax.ppermute(array, 'dp', [(i, i ^ 2) for i in range(8)])  27 us
  transfers between devices with their start and end apart: 102, of which 37 were waited for; matrix products, arithmetic and copies ran while one was open for 44% of the time, Pallas kernels for 4%

profile of v1, /device:TPU:0, one launch (start us, length us, event | category | flops | bytes accessed | tf_op | source)
XLA Modules:
  0.0 1145.6 jit_solution(18357317360948663890)
XLA Ops:
  28.8 6.9 copy.282
  56.5 18.4 %collective-permute-done.4.refs_3_ = f32[3,72,1152]{2,1,0:T(8,128)} collective-permute-done((f32[3,72,1152]{2,1,0:T(8,128)}, f32[3,72,1152]{2,1,0:T(8,128)}, u32[]{:S(2)}, u32[]{:S(2)}) %collective-permute-start.4) | collective-permute-done | bytes 995360 | tf_op jit(solution)/shard_map/ppermute | solution.py:463
  80.0 6.2 collective-permute-done.12.refs_9_
  86.2 5.8 collective-permute-done.11.refs_7_
  95.2 7.9 all-gather.14.cloned.1.call-done
  109.1 6.5 shard_map.512
  126.2 25.4 %collective-permute-done.16.refs_3_ = f32[3,144,1152]{2,1,0:T(8,128)} collective-permute-done((f32[3,144,1152]{2,1,0:T(8,128)}, f32[3,144,1152]{2,1,0:T(8,128)}, u32[]{:S(2)}, u32[]{:S(2)}) %collective-permute-start.16) | collective-permute-done | bytes 1990688 | tf_op jit(solution)/shard_map/ppermute | solution.py:463
  165.2 12.9 %collective-permute-done.20.refs_7_ = f32[1,144,1152]{2,1,0:T(8,128)S(1)} collective-permute-done((f32[1,144,1152]{2,1,0:T(8,128)}, f32[1,144,1152]{2,1,0:T(8,128)S(1)}, u32[]{:S(2)}, u32[]{:S(2)}) %collective-permute-start.20) | collective-permute-done | bytes 663584 | tf_op jit(solution)/shard_map/ppermute | solution.py:463
  178.1 9.0 collective-permute-done.21.refs_9_
  197.3 10.9 shard_map.513
  209.7 9.8 convolution_convert_fusion.qkv_ref
  219.5 16.7 %collective-permute-done.25.refs_2_ = f32[3,144,1152]{2,1,0:T(8,128)} collective-permute-done((f32[3,144,1152]{2,1,0:T(8,128)}, f32[3,144,1152]{2,1,0:T(8,128)}, u32[]{:S(2)}, u32[]{:S(2)}) %collective-permute-start.25) | collective-permute-done | bytes 1990688 | tf_op jit(solution)/shard_map/ppermute | solution.py:463
  239.5 9.1 shard_map.514
  273.8 10.7 collective-permute-done.29.refs_5_
  284.5 12.9 %collective-permute-done.28.refs_4_ = f32[2,144,1152]{2,1,0:T(8,128)} collective-permute-done((f32[2,144,1152]{2,1,0:T(8,128)}, f32[2,144,1152]{2,1,0:T(8,128)}, u32[]{:S(2)}, u32[]{:S(2)}) %collective-permute-start.28) | collective-permute-done | bytes 1327136 | tf_op jit(solution)/shard_map/ppermute | solution.py:463
  297.4 6.2 shard_map.515
  306.0 9.6 multiply_convert_fusion
  315.5 23.1 %collective-permute-done.30.refs_2_ = f32[3,144,1152]{2,1,0:T(8,128)S(1)} collective-permute-done((f32[3,144,1152]{2,1,0:T(8,128)S(1)}, f32[3,144,1152]{2,1,0:T(8,128)S(1)}, u32[]{:S(2)}, u32[]{:S(2)}) %collective-permute-start.30) | collective-permute-done | bytes 1990688 | tf_op jit(solution)/shard_map/ppermute | solution.py:463
  341.8 10.4 fusion.80
  358.5 13.9 %collective-permute-done.33.refs_5_ = f32[2,144,1152]{2,1,0:T(8,128)S(1)} collective-permute-done((f32[2,144,1152]{2,1,0:T(8,128)S(1)}, f32[2,144,1152]{2,1,0:T(8,128)S(1)}, u32[]{:S(2)}, u32[]{:S(2)}) %collective-permute-start.33) | collective-permute-done | bytes 1327136 | tf_op jit(solution)/shard_map/ppermute | solution.py:467
  372.4 6.4 shard_map.516
  378.8 14.7 %fusion.74 = (f32[2304]{0:T(1024)S(1)}, bf16[1032,2304]{1,0:T(8,128)(2,1)}) fusion(f32[1032,2304]{1,0:T(8,128)} %get-tuple-element.904, bf16[1032,1152]{1,0:T(8,128)(2,1)S(1)} %copy-done.43, bf16[2304,1152]{1,0:T(8,128)(2,1)S(1)} %bitcast.359), kind=kOutput, calls=%fused_computation.309 | convolution fusion | flops 5511571456 | bytes 21961728 | tf_op jit(solution)/shard_map/td,fd->tf/dot_general | solution.py:1027
  393.5 8.3 fusion.81
  404.7 10.7 fusion.82
  423.0 6.5 fusion.83
  457.4 8.6 constant_dynamic-slice_fusion.11
  480.9 16.4 %shard_map.517 = bf16[2,258,3456]{2,1,0:T(8,128)(2,1)S(1)} custom-call(bf16[2,258,3456]{2,1,0:T(8,128)(2,1)S(1)} %copy-done.11, bf16[2,258,1152]{2,1,0:T(8,128)(2,1)S(1)} %copy-done.5), custom_call_target="tpu_custom_call" | custom-call | flops 5452922880 | bytes 8322048 | tf_op jit(solution)/shard_map/pallas_call | solution.py:813
  503.6 6.3 copy.285
  509.9 21.5 %collective-permute-done.40 = f32[2,144,1152]{2,1,0:T(8,128)} collective-permute-done((f32[2,144,1152]{2,1,0:T(8,128)}, f32[2,144,1152]{2,1,0:T(8,128)}, u32[]{:S(2)}, u32[]{:S(2)}) %collective-permute-start.40) | collective-permute-done | bytes 1327136 | tf_op jit(solution)/shard_map/ppermute | solution.py:463
  535.9 5.8 fusion.84
  559.0 8.8 multiply_reduce_fusion.9
  567.9 5.9 fusion.86
  595.6 9.6 add.697
  608.8 9.2 pad_maximum_fusion
  636.9 5.6 add.702
  642.5 5.5 collective-permute-done.47
  649.5 26.3 %collective-permute-done.45 = f32[2,144,1152]{2,1,0:T(8,128)S(1)} collective-permute-done((f32[2,144,1152]{2,1,0:T(8,128)S(1)}, f32[2,144,1152]{2,1,0:T(8,128)S(1)}, u32[]{:S(2)}, u32[]{:S(2)}) %collective-permute-start.45) | collective-permute-done | bytes 1327136 | tf_op jit(solution)/shard_map/ppermute | solution.py:463
  701.3 54.5 %collective-permute-done.54 = f32[2,72,1152]{2,1,0:T(8,128)} collective-permute-done((f32[2,72,1152]{2,1,0:T(8,128)}, f32[2,72,1152]{2,1,0:T(8,128)}, u32[]{:S(2)}, u32[]{:S(2)}) %collective-permute-start.54) | collective-permute-done | bytes 663584 | tf_op jit(solution)/shard_map/ppermute | solution.py:463
  763.2 33.7 %collective-permute-done.50 = f32[516,576]{1,0:T(8,128)} collective-permute-done((f32[516,576]{1,0:T(8,128)}, f32[516,576]{1,0:T(8,128)}, u32[]{:S(2)}, u32[]{:S(2)}) %collective-permute-start.50) | collective-permute-done | bytes 1188896 | tf_op jit(solution)/shard_map/ppermute | solution.py:472
  796.8 10.0 reshape.575
  806.9 6.6 add_convert_fusion
  823.3 8.5 collective-permute-done.57
  844.0 14.1 %collective-permute-done.65 = f32[72,1152]{1,0:T(8,128)S(1)} collective-permute-done((f32[72,1152]{1,0:T(8,128)S(1)}, f32[72,1152]{1,0:T(8,128)S(1)}, u32[]{:S(2)}, u32[]{:S(2)}) %collective-permute-start.65) | collective-permute-done | bytes 331808 | tf_op jit(solution)/shard_map/ppermute | solution.py:463
  955.9 5.7 pad_maximum_fusion.2
  1102.0 6.8 fusion.60
  1110.4 7.4 fusion.58
  1117.9 6.9 copy.308
  1124.8 8.3 fusion.57
  (702 shorter events, 545.4 us)
Async XLA Ops:
  7.2 42.1 %all-gather.12.cloned.1.call-start = ((), (), s32[]{:S(2)}) async-start(), calls=%async_computation.7 | async-start | bytes 1658880 | tf_op jit(solution)/shard_map/all_gather | solution.py:604
  9.0 94.1 %all-gather.14.cloned.1.call-start = ((), (), s32[]{:S(2)}) async-start(), calls=%async_computation.8 | async-start | bytes 3317760 | tf_op jit(solution)/shard_map/all_gather | solution.py:604
  15.3 149.9 %all-gather.16.cloned.1.call-start = ((), (), s32[]{:S(2)}) async-start(), calls=%async_computation.9 | async-start | bytes 3317760 | tf_op jit(solution)/shard_map/all_gather | solution.py:604
  17.3 31.8 %collective-permute-start.6 = (f32[1152]{0:T(1024)S(1)}, f32[1152]{0:T(1024)S(1)}, u32[]{:S(2)}, u32[]{:S(2)}) collective-permute-start(f32[1152]{0:T(1024)S(1)} %copy-done.71), channel_id=1, source_target_pairs={{0,3},{1,0},{2,1},{3,2},{4,7},{5,4},{6,5},{7,6},{8,11},{9,8},{10,9... | collective-permute-start | bytes 13832 | tf_op jit(solution)/shard_map/ppermute | solution.py:472
  95.1 124.4 %all-gather.18.cloned.1.call-start = ((), (), s32[]{:S(2)}) async-start(), calls=%async_computation.10 | async-start | bytes 3317760 | tf_op jit(solution)/shard_map/all_gather | solution.py:604
  106.2 45.4 %collective-permute-start.16 = (f32[3,144,1152]{2,1,0:T(8,128)}, f32[3,144,1152]{2,1,0:T(8,128)}, u32[]{:S(2)}, u32[]{:S(2)}) collective-permute-start(f32[3,144,1152]{2,1,0:T(8,128)} %fusion.15.refs_1_), channel_id=1, source_target_pairs={{0,8},{4,12},{8,0},{12,4},{16,24},{20,28},{24,16},{28,20},{1,9},{5... | collective-permute-start | bytes 5971976 | tf_op jit(solution)/shard_map/ppermute | solution.py:463
  107.6 45.1 %collective-permute-start.17 = (f32[3,144,1152]{2,1,0:T(8,128)}, f32[3,144,1152]{2,1,0:T(8,128)}, u32[]{:S(2)}, u32[]{:S(2)}) collective-permute-start(f32[3,144,1152]{2,1,0:T(8,128)} %fusion.15.refs_1_), channel_id=1, source_target_pairs={{0,16},{4,20},{8,24},{12,28},{16,0},{20,4},{24,8},{28,12},{1,17},{... | collective-permute-start | bytes 5971976 | tf_op jit(solution)/shard_map/ppermute | solution.py:467
  121.9 39.1 %collective-permute-start.22 = (f32[516,1152]{1,0:T(8,128)}, f32[516,1152]{1,0:T(8,128)}, u32[]{:S(2)}, u32[]{:S(2)}) collective-permute-start(f32[516,1152]{1,0:T(8,128)} %convert_multiply_fusion), channel_id=1, source_target_pairs={{0,4},{4,0},{8,12},{12,8},{16,20},{20,16},{24,28},{28,24},{1,5},{5... | collective-permute-start | bytes 7133192 | tf_op jit(solution)/shard_map/ppermute | solution.py:459
  125.2 671.6 %all-gather.20.cloned.1.call-start = ((), (), s32[]{:S(2)}) async-start(), calls=%async_computation.11 | async-start | bytes 11980800 | tf_op jit(solution)/shard_map/all_gather | solution.py:1057
  125.6 65.1 %collective-permute-start.15 = (f32[3,144,1152]{2,1,0:T(8,128)}, f32[3,144,1152]{2,1,0:T(8,128)}, u32[]{:S(2)}, u32[]{:S(2)}) collective-permute-start(f32[3,144,1152]{2,1,0:T(8,128)} %fusion.15.refs_1_), channel_id=1, source_target_pairs={{0,4},{4,0},{8,12},{12,8},{16,20},{20,16},{24,28},{28,24},{1,5},{5... | collective-permute-start | bytes 5971976 | tf_op jit(solution)/shard_map/ppermute | solution.py:459
  160.5 35.8 %collective-permute-start.18 = (f32[3,144,1152]{2,1,0:T(8,128)}, f32[3,144,1152]{2,1,0:T(8,128)}, u32[]{:S(2)}, u32[]{:S(2)}) collective-permute-start(f32[3,144,1152]{2,1,0:T(8,128)} %collective-permute-done.16.refs_3_), channel_id=1, source_target_pairs={{0,4},{4,0},{8,12},{12,8},{16,20},{20,16},{24,28},{28,24},{1,5},{5... | collective-permute-start | bytes 5971976 | tf_op jit(solution)/shard_map/ppermute | solution.py:459
  160.5 35.7 %collective-permute-start.19 = (f32[3,144,1152]{2,1,0:T(8,128)}, f32[3,144,1152]{2,1,0:T(8,128)}, u32[]{:S(2)}, u32[]{:S(2)}) collective-permute-start(f32[3,144,1152]{2,1,0:T(8,128)} %collective-permute-done.17.refs_5_), channel_id=1, source_target_pairs={{0,4},{4,0},{8,12},{12,8},{16,20},{20,16},{24,28},{28,24},{1,5},{5... | collective-permute-start | bytes 5971976 | tf_op jit(solution)/shard_map/ppermute | solution.py:459
  190.7 45.6 %collective-permute-start.25 = (f32[3,144,1152]{2,1,0:T(8,128)}, f32[3,144,1152]{2,1,0:T(8,128)}, u32[]{:S(2)}, u32[]{:S(2)}) collective-permute-start(f32[3,144,1152]{2,1,0:T(8,128)} %fusion.14.refs_1_), channel_id=1, source_target_pairs={{0,8},{4,12},{8,0},{12,4},{16,24},{20,28},{24,16},{28,20},{1,9},{5... | collective-permute-start | bytes 5971976 | tf_op jit(solution)/shard_map/ppermute | solution.py:463
  192.1 45.3 %collective-permute-start.26 = (f32[3,144,1152]{2,1,0:T(8,128)}, f32[3,144,1152]{2,1,0:T(8,128)}, u32[]{:S(2)}, u32[]{:S(2)}) collective-permute-start(f32[3,144,1152]{2,1,0:T(8,128)} %fusion.14.refs_1_), channel_id=1, source_target_pairs={{0,16},{4,20},{8,24},{12,28},{16,0},{20,4},{24,8},{28,12},{1,17},{... | collective-permute-start | bytes 5971976 | tf_op jit(solution)/shard_map/ppermute | solution.py:467
  259.8 43.8 %collective-permute-start.27 = (f32[516,1152]{1,0:T(8,128)}, f32[516,1152]{1,0:T(8,128)}, u32[]{:S(2)}, u32[]{:S(2)}) collective-permute-start(f32[516,1152]{1,0:T(8,128)} %get-tuple-element.300), channel_id=1, source_target_pairs={{0,4},{4,0},{8,12},{12,8},{16,20},{20,16},{24,28},{28,24},{1,5},{5... | collective-permute-start | bytes 7133192 | tf_op jit(solution)/shard_map/ppermute | solution.py:459
  265.1 32.4 %collective-permute-start.28 = (f32[2,144,1152]{2,1,0:T(8,128)}, f32[2,144,1152]{2,1,0:T(8,128)}, u32[]{:S(2)}, u32[]{:S(2)}) collective-permute-start(f32[2,144,1152]{2,1,0:T(8,128)} %slice.333), channel_id=1, source_target_pairs={{0,8},{4,12},{8,0},{12,4},{16,24},{20,28},{24,16},{28,20},{1,9},{5... | collective-permute-start | bytes 3981320 | tf_op jit(solution)/shard_map/ppermute | solution.py:463
  272.6 66.1 %collective-permute-start.30 = (f32[3,144,1152]{2,1,0:T(8,128)S(1)}, f32[3,144,1152]{2,1,0:T(8,128)S(1)}, u32[]{:S(2)}, u32[]{:S(2)}) collective-permute-start(f32[3,144,1152]{2,1,0:T(8,128)S(1)} %fusion.13.refs_1_), channel_id=1, source_target_pairs={{0,8},{4,12},{8,0},{12,4},{16,24},{20,28},{24,16},{28,20},{1,9},{5... | collective-permute-start | bytes 5971976 | tf_op jit(solution)/shard_map/ppermute | solution.py:463
  273.2 65.4 %collective-permute-start.31 = (f32[3,144,1152]{2,1,0:T(8,128)S(1)}, f32[3,144,1152]{2,1,0:T(8,128)S(1)}, u32[]{:S(2)}, u32[]{:S(2)}) collective-permute-start(f32[3,144,1152]{2,1,0:T(8,128)S(1)} %fusion.13.refs_1_), channel_id=1, source_target_pairs={{0,16},{4,20},{8,24},{12,28},{16,0},{20,4},{24,8},{28,12},{1,17},{... | collective-permute-start | bytes 5971976 | tf_op jit(solution)/shard_map/ppermute | solution.py:467
  340.3 32.1 %collective-permute-start.33 = (f32[2,144,1152]{2,1,0:T(8,128)S(1)}, f32[2,144,1152]{2,1,0:T(8,128)S(1)}, u32[]{:S(2)}, u32[]{:S(2)}) collective-permute-start(f32[2,144,1152]{2,1,0:T(8,128)S(1)} %slice.336), channel_id=1, source_target_pairs={{0,16},{4,20},{8,24},{12,28},{16,0},{20,4},{24,8},{28,12},{1,17},{... | collective-permute-start | bytes 3981320 | tf_op jit(solution)/shard_map/ppermute | solution.py:467
  357.3 44.8 %collective-permute-start.35 = (f32[2,144,1152]{2,1,0:T(8,128)}, f32[2,144,1152]{2,1,0:T(8,128)S(1)}, u32[]{:S(2)}, u32[]{:S(2)}) collective-permute-start(f32[2,144,1152]{2,1,0:T(8,128)} %get-tuple-element.321), channel_id=1, source_target_pairs={{0,8},{4,12},{8,0},{12,4},{16,24},{20,28},{24,16},{28,20},{1,9},{5... | collective-permute-start | bytes 3981320 | tf_op jit(solution)/shard_map/ppermute | solution.py:463
  357.9 44.2 %collective-permute-start.36 = (f32[2,144,1152]{2,1,0:T(8,128)}, f32[2,144,1152]{2,1,0:T(8,128)S(1)}, u32[]{:S(2)}, u32[]{:S(2)}) collective-permute-start(f32[2,144,1152]{2,1,0:T(8,128)} %get-tuple-element.322), channel_id=1, source_target_pairs={{0,16},{4,20},{8,24},{12,28},{16,0},{20,4},{24,8},{28,12},{1,17},{... | collective-permute-start | bytes 3981320 | tf_op jit(solution)/shard_map/ppermute | solution.py:467
  436.2 377.3 %reduce-scatter.9.cloned.1.call-start = ((), (), s32[]{:S(2)}) async-start(), calls=%async_computation.5 | async-start | bytes 3317760 | tf_op jit(solution)/shard_map/reduce_scatter | solution.py:653
  443.1 88.7 %collective-permute-start.38 = (f32[4,144,1152]{2,1,0:T(8,128)}, f32[4,144,1152]{2,1,0:T(8,128)}, u32[]{:S(2)}, u32[]{:S(2)}) collective-permute-start(f32[4,144,1152]{2,1,0:T(8,128)} %pad_maximum_fusion.5), channel_id=1, source_target_pairs={{0,8},{4,12},{8,0},{12,4},{16,24},{20,28},{24,16},{28,20},{1,9},{5... | collective-permute-start | bytes 7962632 | tf_op jit(solution)/shard_map/ppermute | solution.py:463
  443.6 88.1 %collective-permute-start.39 = (f32[4,144,1152]{2,1,0:T(8,128)}, f32[4,144,1152]{2,1,0:T(8,128)}, u32[]{:S(2)}, u32[]{:S(2)}) collective-permute-start(f32[4,144,1152]{2,1,0:T(8,128)} %pad_maximum_fusion.6), channel_id=1, source_target_pairs={{0,16},{4,20},{8,24},{12,28},{16,0},{20,4},{24,8},{28,12},{1,17},{... | collective-permute-start | bytes 7962632 | tf_op jit(solution)/shard_map/ppermute | solution.py:467
  450.5 80.9 %collective-permute-start.40 = (f32[2,144,1152]{2,1,0:T(8,128)}, f32[2,144,1152]{2,1,0:T(8,128)}, u32[]{:S(2)}, u32[]{:S(2)}) collective-permute-start(f32[2,144,1152]{2,1,0:T(8,128)} %get-tuple-element.339), channel_id=1, source_target_pairs={{0,8},{4,12},{8,0},{12,4},{16,24},{20,28},{24,16},{28,20},{1,9},{5... | collective-permute-start | bytes 3981320 | tf_op jit(solution)/shard_map/ppermute | solution.py:463
  452.0 79.8 %collective-permute-start.41 = (f32[2,144,1152]{2,1,0:T(8,128)}, f32[2,144,1152]{2,1,0:T(8,128)}, u32[]{:S(2)}, u32[]{:S(2)}) collective-permute-start(f32[2,144,1152]{2,1,0:T(8,128)} %get-tuple-element.340), channel_id=1, source_target_pairs={{0,16},{4,20},{8,24},{12,28},{16,0},{20,4},{24,8},{28,12},{1,17},{... | collective-permute-start | bytes 3981320 | tf_op jit(solution)/shard_map/ppermute | solution.py:467
  541.7 53.8 %collective-permute-start.42 = (f32[1728,1152]{1,0:T(8,128)}, f32[1728,1152]{1,0:T(8,128)}, u32[]{:S(2)}, u32[]{:S(2)}) collective-permute-start(f32[1728,1152]{1,0:T(8,128)} %fusion.84), channel_id=1, source_target_pairs={{0,4},{4,0},{8,12},{12,8},{16,20},{20,16},{24,28},{28,24},{1,5},{5... | collective-permute-start | bytes 23887880 | tf_op jit(solution)/shard_map/ppermute | solution.py:459
  558.5 37.0 %collective-permute-start.43 = (f32[576,1152]{1,0:T(8,128)}, f32[576,1152]{1,0:T(8,128)}, u32[]{:S(2)}, u32[]{:S(2)}) collective-permute-start(f32[576,1152]{1,0:T(8,128)} %fusion.85), channel_id=1, source_target_pairs={{0,4},{4,0},{8,12},{12,8},{16,20},{20,16},{24,28},{28,24},{1,5},{5... | collective-permute-start | bytes 7962632 | tf_op jit(solution)/shard_map/ppermute | solution.py:459
  580.9 55.7 %collective-permute-start.49 = (f32[1152,1152]{1,0:T(8,128)}, f32[1152,1152]{1,0:T(8,128)}, u32[]{:S(2)}, u32[]{:S(2)}) collective-permute-start(f32[1152,1152]{1,0:T(8,128)} %fusion.88), channel_id=1, source_target_pairs={{0,4},{4,0},{8,12},{12,8},{16,20},{20,16},{24,28},{28,24},{1,5},{5... | collective-permute-start | bytes 15925256 | tf_op jit(solution)/shard_map/ppermute | solution.py:459
  587.3 60.7 %collective-permute-start.47 = (f32[4,144,1152]{2,1,0:T(8,128)}, f32[4,144,1152]{2,1,0:T(8,128)}, u32[]{:S(2)}, u32[]{:S(2)}) collective-permute-start(f32[4,144,1152]{2,1,0:T(8,128)} %pad_maximum_fusion.7), channel_id=1, source_target_pairs={{0,8},{4,12},{8,0},{12,4},{16,24},{20,28},{24,16},{28,20},{1,9},{5... | collective-permute-start | bytes 7962632 | tf_op jit(solution)/shard_map/ppermute | solution.py:463
  588.8 60.7 %collective-permute-start.48 = (f32[4,144,1152]{2,1,0:T(8,128)}, f32[4,144,1152]{2,1,0:T(8,128)}, u32[]{:S(2)}, u32[]{:S(2)}) collective-permute-start(f32[4,144,1152]{2,1,0:T(8,128)} %pad_maximum_fusion.8), channel_id=1, source_target_pairs={{0,16},{4,20},{8,24},{12,28},{16,0},{20,4},{24,8},{28,12},{1,17},{... | collective-permute-start | bytes 7962632 | tf_op jit(solution)/shard_map/ppermute | solution.py:467
  595.5 239.4 %reduce-scatter.7.cloned.1.call-start = ((), (), s32[]{:S(2)}) async-start(), calls=%async_computation.4 | async-start | bytes 3317760 | tf_op jit(solution)/shard_map/reduce_scatter | solution.py:653
  621.0 54.8 %collective-permute-start.45 = (f32[2,144,1152]{2,1,0:T(8,128)S(1)}, f32[2,144,1152]{2,1,0:T(8,128)S(1)}, u32[]{:S(2)}, u32[]{:S(2)}) collective-permute-start(f32[2,144,1152]{2,1,0:T(8,128)S(1)} %get-tuple-element.357), channel_id=1, source_target_pairs={{0,8},{4,12},{8,0},{12,4},{16,24},{20,28},{24,16},{28,20},{1,9},{5... | collective-permute-start | bytes 3981320 | tf_op jit(solution)/shard_map/ppermute | solution.py:463
  621.6 55.3 %collective-permute-start.46 = (f32[2,144,1152]{2,1,0:T(8,128)S(1)}, f32[2,144,1152]{2,1,0:T(8,128)S(1)}, u32[]{:S(2)}, u32[]{:S(2)}) collective-permute-start(f32[2,144,1152]{2,1,0:T(8,128)S(1)} %get-tuple-element.358), channel_id=1, source_target_pairs={{0,16},{4,20},{8,24},{12,28},{16,0},{20,4},{24,8},{28,12},{1,17},{... | collective-permute-start | bytes 3981320 | tf_op jit(solution)/shard_map/ppermute | solution.py:467
  636.6 60.5 %collective-permute-start.44 = (f32[516,576]{1,0:T(8,128)}, f32[516,576]{1,0:T(8,128)}, u32[]{:S(2)}, u32[]{:S(2)}) collective-permute-start(f32[516,576]{1,0:T(8,128)} %fusion.27), channel_id=1, source_target_pairs={{0,1},{1,2},{2,3},{3,0},{4,5},{5,6},{6,7},{7,4},{8,9},{9,10},{10,1... | collective-permute-start | bytes 3566600 | tf_op jit(solution)/shard_map/ppermute | solution.py:472
  682.5 80.7 %collective-permute-start.52 = (f32[4,144,1152]{2,1,0:T(8,128)}, f32[4,144,1152]{2,1,0:T(8,128)}, u32[]{:S(2)}, u32[]{:S(2)}) collective-permute-start(f32[4,144,1152]{2,1,0:T(8,128)} %pad_maximum_fusion.9), channel_id=1, source_target_pairs={{0,8},{4,12},{8,0},{12,4},{16,24},{20,28},{24,16},{28,20},{1,9},{5... | collective-permute-start | bytes 7962632 | tf_op jit(solution)/shard_map/ppermute | solution.py:463
  683.1 80.1 %collective-permute-start.53 = (f32[4,144,1152]{2,1,0:T(8,128)}, f32[4,144,1152]{2,1,0:T(8,128)}, u32[]{:S(2)}, u32[]{:S(2)}) collective-permute-start(f32[4,144,1152]{2,1,0:T(8,128)} %pad_maximum_fusion.10), channel_id=1, source_target_pairs={{0,16},{4,20},{8,24},{12,28},{16,0},{20,4},{24,8},{28,12},{1,17},{... | collective-permute-start | bytes 7962632 | tf_op jit(solution)/shard_map/ppermute | solution.py:467
  689.7 238.4 %reduce-scatter.11.cloned.1.call-start = ((), (), s32[]{:S(2)}) async-start(), calls=%async_computation.6 | async-start | bytes 3317760 | tf_op jit(solution)/shard_map/reduce_scatter | solution.py:653
  695.2 60.6 %collective-permute-start.54 = (f32[2,72,1152]{2,1,0:T(8,128)}, f32[2,72,1152]{2,1,0:T(8,128)}, u32[]{:S(2)}, u32[]{:S(2)}) collective-permute-start(f32[2,72,1152]{2,1,0:T(8,128)} %get-tuple-element.376), channel_id=1, source_target_pairs={{0,8},{4,12},{8,0},{12,4},{16,24},{20,28},{24,16},{28,20},{1,9},{5... | collective-permute-start | bytes 1990664 | tf_op jit(solution)/shard_map/ppermute | solution.py:463
  696.6 59.5 %collective-permute-start.55 = (f32[2,72,1152]{2,1,0:T(8,128)}, f32[2,72,1152]{2,1,0:T(8,128)}, u32[]{:S(2)}, u32[]{:S(2)}) collective-permute-start(f32[2,72,1152]{2,1,0:T(8,128)} %get-tuple-element.377), channel_id=1, source_target_pairs={{0,16},{4,20},{8,24},{12,28},{16,0},{20,4},{24,8},{28,12},{1,17},{... | collective-permute-start | bytes 1990664 | tf_op jit(solution)/shard_map/ppermute | solution.py:467
  698.9 97.9 %collective-permute-start.50 = (f32[516,576]{1,0:T(8,128)}, f32[516,576]{1,0:T(8,128)}, u32[]{:S(2)}, u32[]{:S(2)}) collective-permute-start(f32[516,576]{1,0:T(8,128)} %fusion.29), channel_id=1, source_target_pairs={{0,2},{1,3},{2,0},{3,1},{4,6},{5,7},{6,4},{7,5},{8,10},{9,11},{10,... | collective-permute-start | bytes 3566600 | tf_op jit(solution)/shard_map/ppermute | solution.py:472
  760.3 61.6 %collective-permute-start.60 = (f32[4,72,1152]{2,1,0:T(8,128)}, f32[4,72,1152]{2,1,0:T(8,128)}, u32[]{:S(2)}, u32[]{:S(2)}) collective-permute-start(f32[4,72,1152]{2,1,0:T(8,128)} %pad_maximum_fusion.15), channel_id=1, source_target_pairs={{0,8},{4,12},{8,0},{12,4},{16,24},{20,28},{24,16},{28,20},{1,9},{5... | collective-permute-start | bytes 3981320 | tf_op jit(solution)/shard_map/ppermute | solution.py:463
  761.7 61.6 %collective-permute-start.61 = (f32[4,72,1152]{2,1,0:T(8,128)}, f32[4,72,1152]{2,1,0:T(8,128)}, u32[]{:S(2)}, u32[]{:S(2)}) collective-permute-start(f32[4,72,1152]{2,1,0:T(8,128)} %pad_maximum_fusion.16), channel_id=1, source_target_pairs={{0,16},{4,20},{8,24},{12,28},{16,0},{20,4},{24,8},{28,12},{1,17},{... | collective-permute-start | bytes 3981320 | tf_op jit(solution)/shard_map/ppermute | solution.py:467
  821.9 54.9 %collective-permute-start.56 = (f32[516,576]{1,0:T(8,128)}, f32[516,576]{1,0:T(8,128)}, u32[]{:S(2)}, u32[]{:S(2)}) collective-permute-start(f32[516,576]{1,0:T(8,128)} %fusion.23), channel_id=1, source_target_pairs={{0,3},{1,0},{2,1},{3,2},{4,7},{5,4},{6,5},{7,6},{8,11},{9,8},{10,9... | collective-permute-start | bytes 3566600 | tf_op jit(solution)/shard_map/ppermute | solution.py:472
  834.9 41.1 %collective-permute-start.62 = (f32[144,1152]{1,0:T(8,128)}, f32[144,1152]{1,0:T(8,128)S(1)}, u32[]{:S(2)}, u32[]{:S(2)}) collective-permute-start(f32[144,1152]{1,0:T(8,128)} %bitcast.108), channel_id=1, source_target_pairs={{0,8},{4,12},{8,0},{12,4},{16,24},{20,28},{24,16},{28,20},{1,9},{5... | collective-permute-start | bytes 1990664 | tf_op jit(solution)/shard_map/ppermute | solution.py:463
  842.5 33.6 %collective-permute-start.63 = (f32[144,1152]{1,0:T(8,128)}, f32[144,1152]{1,0:T(8,128)}, u32[]{:S(2)}, u32[]{:S(2)}) collective-permute-start(f32[144,1152]{1,0:T(8,128)} %bitcast.108), channel_id=1, source_target_pairs={{0,16},{4,20},{8,24},{12,28},{16,0},{20,4},{24,8},{28,12},{1,17},{... | collective-permute-start | bytes 1990664 | tf_op jit(solution)/shard_map/ppermute | solution.py:467
  865.7 108.9 %reduce-scatter.13.cloned.1.call-start = ((), (), s32[]{:S(2)}) async-start(), calls=%async_computation.12 | async-start | bytes 1658880
  871.4 37.3 %collective-permute-start.72 = (f32[4,144,1152]{2,1,0:T(8,128)}, f32[4,144,1152]{2,1,0:T(8,128)}, u32[]{:S(2)}, u32[]{:S(2)}) collective-permute-start(f32[4,144,1152]{2,1,0:T(8,128)} %fusion.42), channel_id=1, source_target_pairs={{0,4},{4,0},{8,12},{12,8},{16,20},{20,16},{24,28},{28,24},{1,5},{5... | collective-permute-start | bytes 7962632 | tf_op jit(solution)/shard_map/ppermute | solution.py:459
  (152 other events, 1513.1 us)
Sparse Core Ops, SparseCore 0:
  10.2 36.1 all-gather.11
  48.5 54.5 all-gather.13
  105.3 54.1 all-gather.15
  161.4 54.1 all-gather.17
  436.3 167.5 all-gather.19
  606.0 64.7 reduce-scatter.8
  689.9 88.6 reduce-scatter.6
  865.8 49.9 reduce-scatter.10
  928.3 31.3 reduce-scatter.12

commit v2 on v1

--- a/solution.py
+++ b/solution.py
@@ -1,3 +1,4 @@
+import functools
 import math
 
 import jax
@@ -455,6 +456,9 @@
     return body_tensor(*operands)
 
 
+small_cost = pl.CostEstimate(flops=0, bytes_accessed=1024, transcendentals=0)
+
+
 def to_core(array):
     return lax.ppermute(array, "dp", [(i, i ^ 1) for i in range(8)])
 
@@ -558,7 +562,7 @@
             pltpu.SemaphoreType.DMA((depth,)),
         ],
         compiler_params=pltpu.CompilerParams(vmem_limit_bytes=32 * 1024 * 1024),
-        cost_estimate=pl.CostEstimate(flops=0, bytes_accessed=blocks * rows * D * 6, transcendentals=0),
+        cost_estimate=small_cost,
     )(table, *arrays)
 
 
@@ -610,13 +614,13 @@
     return lax.dynamic_slice_in_dim(twice, lax.axis_index("mp") + 1, count - 1, 0)
 
 
-def assemble_weight(shard, parts, swapped, core, shard_major, split):
+def assemble_weight(shard, parts, swapped, core, split):
     count = lax.axis_size("mp")
     rows = shard.shape[0] // 8
 
     def spot(shard_index, quarter):
         shard_index = lax.rem(lax.axis_index("mp") + shard_index, count)
-        return shard_index * 4 + quarter if shard_major else quarter * count + shard_index
+        return quarter * count + shard_index
 
     if swapped is None:
         mine = pick(shard.reshape(4, 2, rows, D), core, 1)
@@ -649,80 +653,236 @@
 
 
 def sum_deep(order, grad, quarter, from_x, from_y):
-    own = pick(grad, quarter, 0) + from_x + from_y
-    return lax.psum_scatter(order.after(own), "mp", scatter_dimension=0, tiled=False)
-
-
-def hold(parts, quarter):
-    own, from_x, from_y, corner_one, corner_two = parts
-    held = jnp.zeros((4,) + own.shape, jnp.float32)
-    corner = jnp.concatenate([corner_one, corner_two], 0)
-    for turn, array in enumerate((own, from_x, from_y, corner)):
-        held = lax.dynamic_update_slice(held, array[None], (quarter ^ turn, jnp.int32(0), jnp.int32(0)))
-    return held
-
-
-def interleave(held, other, core):
-    low_core = jnp.where(core == 0, held, other)
-    high_core = jnp.where(core == 0, other, held)
-    return jnp.stack([low_core, high_core], 1).reshape(-1, D)
-
-
-class Tensor:
-    def __init__(self, grad, weight, row_state, col_state, axis):
-        self.grad, self.weight, self.axis = grad, weight, axis
-        self.row_state, self.col_state = row_state, col_state
-        self.leading = grad.shape[0]
-        self.rows_full = row_state.shape[1]
-        self.cols_full = col_state.shape[1]
-        squares = grad * grad + moment_eps
-        row_sum, col_sum = jnp.sum(squares, 2), jnp.sum(squares, 1)
-        start = lax.axis_index("mp") * grad.shape[axis]
-        if axis == 1:
-            state = lax.dynamic_slice_in_dim(row_state, start, grad.shape[1], 1)
-            self.near = 0.5 * state + 0.5 * (row_sum / self.cols_full)
-            self.partial = col_sum
+    own = order.mark(pick(grad, quarter, 0) + from_x + from_y)
+    return lax.psum_scatter(own, "mp", scatter_dimension=0, tiled=False)
+
+
+def place_rows(pieces, rows, near_state=None):
+    arrays = []
+    for array, *_ in pieces:
+        if not any(array is other for other in arrays):
+            arrays.append(array)
+    steps = [
+        (next(n for n, other in enumerate(arrays) if other is array), first, amount)
+        for array, first, amount, _ in pieces
+    ]
+    table = jnp.stack([jnp.asarray(spot, jnp.int32) for *_, spot in pieces])
+
+    def kernel(table_ref, *refs):
+        sources = refs[: len(arrays)]
+        sems = refs[-1]
+        if near_state is None:
+            out_ref = refs[len(arrays)]
         else:
-            state = lax.dynamic_slice_in_dim(col_state, start, grad.shape[2], 1)
-            self.near = 0.5 * state + 0.5 * (col_sum / self.rows_full)
-            self.partial = row_sum
-
-    def sent(self):
-        return [self.near.reshape(-1), self.partial.reshape(-1)]
-
-    def received(self, near, partial):
-        near = near.reshape(near.shape[0], self.leading, -1).transpose(1, 0, 2)
-        near = near.reshape(self.leading, -1)
-        total = jnp.sum(partial, 0).reshape(self.leading, -1)
-        if self.axis == 1:
-            self.row_new = near
-            self.col_new = 0.5 * self.col_state + 0.5 * (total / self.rows_full)
-            row_piece, col_piece = self.near, self.col_new
-        else:
-            self.col_new = near
-            self.row_new = 0.5 * self.row_state + 0.5 * (total / self.cols_full)
-            row_piece, col_piece = self.row_new, self.near
-        row_mean = jnp.mean(self.row_new, 1)
-        self.row_scale = lax.rsqrt(row_piece / row_mean[:, None])
-        self.col_scale = lax.rsqrt(col_piece)
-        update = self.update()
-        self.step_sq = jnp.sum(update * update)
-
-    def update(self):
-        return self.grad * self.row_scale[:, :, None] * self.col_scale[:, None, :]
-
-
-def exchange(tensors, extra):
-    pieces = [part for tensor in tensors for part in tensor.sent()]
-    whole = gather_deep(jnp.concatenate(pieces + [extra]))
-    offset = 0
-    for tensor in tensors:
-        parts = []
-        for part in tensor.sent():
-            parts.append(whole[:, offset : offset + part.shape[0]])
-            offset = offset + part.shape[0]
-        tensor.received(*parts)
-    return whole[:, offset:]
+            state_ref, out_ref, moment_ref = refs[len(arrays) : -1]
+        copies = []
+        for step, (n, first, amount) in enumerate(steps):
+            spot = pl.multiple_of(table_ref[step], 8)
+            source = sources[n].at[pl.ds(first, amount)]
+            copies.append(
+                pltpu.make_async_copy(source, out_ref.at[pl.ds(spot, amount)], sems.at[step])
+            )
+        for copy in copies:
+            copy.start()
+        for copy in copies:
+            copy.wait()
+        if near_state is None:
+            return
+        leading, length = near_state.shape
+        chunk = length if length < 384 else 384
+        for lead in range(leading):
+            total = jnp.zeros((1, D), jnp.float32)
+            for first in range(0, length, chunk):
+                grad = out_ref[lead * length + first : lead * length + first + chunk]
+                squares = grad * grad + moment_eps
+                total = total + jnp.sum(squares, 0, keepdims=True)
+                near = 0.5 * state_ref[lead, :1, first : first + chunk]
+                near = near + 0.5 * (as_row(lanes_of(squares)) / D)
+                moment_ref[lead, 1:2, first : first + chunk] = near
+            moment_ref[lead, :1] = total
+            if length < D:
+                moment_ref[lead, 1:2, length:] = jnp.zeros((1, D - length), jnp.float32)
+
+    vmem = pl.BlockSpec(memory_space=pltpu.VMEM)
+    in_specs = [pl.BlockSpec(memory_space=pltpu.SMEM)]
+    in_specs = in_specs + [pl.BlockSpec(memory_space=pl.ANY)] * len(arrays)
+    out_specs, shapes = [vmem], [jax.ShapeDtypeStruct((rows, D), jnp.float32)]
+    operands = [table, *arrays]
+    if near_state is not None:
+        leading, length = near_state.shape
+        in_specs.append(vmem)
+        operands.append(near_state.reshape(leading, 1, length))
+        out_specs.append(vmem)
+        shapes.append(jax.ShapeDtypeStruct((leading, 2, D), jnp.float32))
+    result = pl.pallas_call(
+        kernel,
+        in_specs=in_specs,
+        out_specs=out_specs,
+        out_shape=shapes,
+        scratch_shapes=[pltpu.SemaphoreType.DMA((len(steps),))],
+        compiler_params=pltpu.CompilerParams(vmem_limit_bytes=40 * 1024 * 1024),
+        cost_estimate=small_cost,
+    )(*operands)
+    return result[0] if near_state is None else result
+
+
+def add_half(grads, given, core):
+    rows = grads[0].shape[2]
+    amounts = [array.shape[0] for array in grads]
+    firsts = [sum(amounts[:n]) for n in range(len(amounts))]
+
+    def kernel(core_ref, *refs):
+        for n, (first, amount) in enumerate(zip(firsts, amounts)):
+
+            @pl.when((pl.program_id(0) >= first) & (pl.program_id(0) < first + amount))
+            def _():
+                refs[-1][...] = refs[n][0] + refs[len(grads) + n][...]
+
+    def at(first, amount):
+        return lambda step: jnp.clip(step - first, 0, amount - 1)
+
+    spots = [at(*pair) for pair in zip(firsts, amounts)]
+    own_specs = [
+        pl.BlockSpec((1, 1, rows, D), lambda step, core_ref, at=at: (at(step), core_ref[0], 0, 0))
+        for at in spots
+    ]
+    given_specs = [
+        pl.BlockSpec((1, rows, D), lambda step, core_ref, at=at: (at(step), 0, 0)) for at in spots
+    ]
+    total = sum(amounts)
+    return pl.pallas_call(
+        kernel,
+        grid_spec=pltpu.PrefetchScalarGridSpec(
+            num_scalar_prefetch=1,
+            grid=(total,),
+            in_specs=own_specs + given_specs,
+            out_specs=pl.BlockSpec((1, rows, D), lambda step, core_ref: (step, 0, 0)),
+        ),
+        out_shape=jax.ShapeDtypeStruct((total, rows, D), jnp.float32),
+        compiler_params=pltpu.CompilerParams(vmem_limit_bytes=40 * 1024 * 1024),
+        cost_estimate=small_cost,
+    )(core[None], *grads, *given)
+
+
+def lanes_of(array):
+    total = array[:, :128]
+    for tile in range(1, array.shape[1] // 128):
+        total = total + array[:, tile * 128 : (tile + 1) * 128]
+    return total
+
+
+def as_row(column):
+    return jnp.sum(column.T, 0, keepdims=True)
+
+
+def as_column(row):
+    return jnp.broadcast_to(row, (128, row.shape[1])).T
+
+
+def scale_kernel(count, by_rows, place_ref, grad_ref, state_ref, *refs):
+    sources = refs[:count]
+    far_ref, scale_ref, near_ref, step_ref = refs[count:]
+    rows = grad_ref.shape[1]
+    total = jnp.zeros((1, D), jnp.float32)
+    near_sum = jnp.zeros((1, 1), jnp.float32)
+    for index in range(count):
+        part = jnp.zeros((2, D), jnp.float32)
+        for shift in range(count):
+            part = jnp.where(place_ref[0] == (index + shift) % count, sources[shift][0], part)
+        total = total + part[:1]
+        near_sum = near_sum + jnp.sum(part[1:], 1, keepdims=True)
+    far = 0.5 * state_ref[0] + 0.5 * (total / (count * rows))
+    far_ref[0] = far
+    lead = pl.program_id(0)
+    near_mean = near_sum / (count * rows)
+    far_mean = jnp.sum(far, 1, keepdims=True) / D
+    if all(by_rows):
+        mean = near_mean
+    elif not any(by_rows):
+        mean = far_mean
+    else:
+        split = by_rows.index(True)
+        mean = jnp.where(lead >= split, near_mean, far_mean)
+    far_scale = lax.rsqrt(far)
+    near_scale = as_column(lax.rsqrt(sources[0][0][1:2, :rows] / mean))
+    scale_ref[0] = far_scale
+    near_ref[0] = near_scale
+    step = grad_ref[0] * far_scale
+    step = lanes_of(step * step) * near_scale * near_scale
+
+    @pl.when(lead == 0)
+    def _():
+        step_ref[...] = jnp.zeros_like(step_ref)
+
+    step_ref[...] += jnp.sum(step.reshape(rows // 8, 8, 128), 0)
+
+
+def scales(grad, far_state, sources, mp_index, by_rows):
+    leading, rows, _ = grad.shape
+    count = len(sources)
+    small = pl.BlockSpec((1, 2, D), lambda i: (i, 0, 0))
+    line = pl.BlockSpec((1, 1, D), lambda i: (i, 0, 0))
+    return pl.pallas_call(
+        functools.partial(scale_kernel, count, by_rows),
+        grid=(leading,),
+        in_specs=[
+            pl.BlockSpec(memory_space=pltpu.SMEM),
+            pl.BlockSpec((1, rows, D), lambda i: (i, 0, 0)),
+            line,
+        ]
+        + [small] * count,
+        out_specs=[
+            line,
+            line,
+            pl.BlockSpec((1, rows, 128), lambda i: (i, 0, 0)),
+            pl.BlockSpec((8, 128), lambda i: (0, 0)),
+        ],
+        out_shape=[
+            jax.ShapeDtypeStruct((leading, 1, D), jnp.float32),
+            jax.ShapeDtypeStruct((leading, 1, D), jnp.float32),
+            jax.ShapeDtypeStruct((leading, rows, 128), jnp.float32),
+            jax.ShapeDtypeStruct((8, 128), jnp.float32),
+        ],
+        compiler_params=pltpu.CompilerParams(vmem_limit_bytes=40 * 1024 * 1024),
+        cost_estimate=small_cost,
+    )(mp_index[None], grad, far_state.reshape(leading, 1, D), *sources)
+
+
+def renew_kernel(turned, factor_ref, weight_ref, grad_ref, far_ref, near_ref, new_ref, low_ref):
+    step = grad_ref[0] * far_ref[0] * (near_ref[0][:, :1] * factor_ref[0])
+    new = weight_ref[0] - (step.T if turned else step)
+    new_ref[0] = new
+    low_ref[0] = new.astype(jnp.bfloat16)
+
+
+def renew(weight, grad, far_scale, near_scale, factor, turned, first=0):
+    leading, rows = weight.shape[0], grad.shape[1]
+    if turned:
+        width = 384
+        grid = (leading, D // width)
+        weight_spec = pl.BlockSpec((1, width, rows), lambda i, j: (i, j, 0))
+        grad_spec = pl.BlockSpec((1, rows, width), lambda i, j: (i + first, 0, j))
+        far_spec = pl.BlockSpec((1, 1, width), lambda i, j: (i + first, 0, j))
+        near_spec = pl.BlockSpec((1, rows, 128), lambda i, j: (i + first, 0, 0))
+    else:
+        height = min(rows, 288)
+        grid = (leading, rows // height)
+        weight_spec = pl.BlockSpec((1, height, D), lambda i, j: (i, j, 0))
+        grad_spec = pl.BlockSpec((1, height, D), lambda i, j: (i + first, j, 0))
+        far_spec = pl.BlockSpec((1, 1, D), lambda i, j: (i + first, 0, 0))
+        near_spec = pl.BlockSpec((1, height, 128), lambda i, j: (i + first, j, 0))
+    return pl.pallas_call(
+        functools.partial(renew_kernel, turned),
+        grid=grid,
+        in_specs=[pl.BlockSpec(memory_space=pltpu.SMEM), weight_spec, grad_spec, far_spec, near_spec],
+        out_specs=[weight_spec, weight_spec],
+        out_shape=[
+            jax.ShapeDtypeStruct(weight.shape, jnp.float32),
+            jax.ShapeDtypeStruct(weight.shape, jnp.bfloat16),
+        ],
+        compiler_params=pltpu.CompilerParams(vmem_limit_bytes=40 * 1024 * 1024),
+        cost_estimate=small_cost,
+    )(factor[None], weight, grad, far_scale, near_scale)
 
 
 def head_windows():
@@ -770,11 +930,7 @@
         out_shape=jax.ShapeDtypeStruct((images, SEQ, D), jnp.bfloat16),
         scratch_shapes=[pltpu.VMEM((SEQ, D), jnp.float32)],
         compiler_params=pltpu.CompilerParams(vmem_limit_bytes=40 * 1024 * 1024),
-        cost_estimate=pl.CostEstimate(
-            flops=images * 4 * SEQ * SEQ * 256 * 16,
-            bytes_accessed=images * SEQ * D * 8,
-            transcendentals=images * 16 * SEQ * SEQ,
-        ),
+        cost_estimate=small_cost,
     )(qkv)
 
 
@@ -821,11 +977,7 @@
         out_shape=jax.ShapeDtypeStruct((images, SEQ, 3 * D), jnp.bfloat16),
         scratch_shapes=[pltpu.VMEM((SEQ, D), jnp.float32)] * 3,
         compiler_params=pltpu.CompilerParams(vmem_limit_bytes=40 * 1024 * 1024),
-        cost_estimate=pl.CostEstimate(
-            flops=images * 10 * SEQ * SEQ * 256 * 16,
-            bytes_accessed=images * SEQ * D * 14,
-            transcendentals=images * 16 * SEQ * SEQ,
-        ),
+        cost_estimate=small_cost,
     )(qkv, grad)
 
 
@@ -898,13 +1050,13 @@
     start = mp_index * tokens
     block_local = lax.dynamic_slice_in_dim(block_input, start, tokens, 0)
     skip_local = lax.dynamic_slice_in_dim(skip_input, start, tokens, 0)
-    both_inputs = jnp.stack(
+    both_inputs = jnp.concatenate(
         [
-            block_local.reshape(tokens, mp_count, width_local),
-            skip_local.reshape(tokens, mp_count, width_local),
+            array.reshape(tokens, mp_count, 2, -1).transpose(0, 2, 1, 3).reshape(tokens, D)
+            for array in (block_local, skip_local)
         ],
-        2,
-    ).reshape(tokens, -1)
+        1,
+    )
     both_inputs = order.mark(both_inputs)
     batch = order.mark(batch + batch_y)
 
@@ -933,6 +1085,7 @@
     attn_own = others(order.mark(attn_whole))
     attn_x, attn_y = swap_plane(order, attn_own, attn_own)
     fc2_whole = bring(order, fc2_shard, quarter, core)
+    fc2_across = bring(order, fc2_shard, quarter ^ 3, core)
     skip_swapped = order.mark(*skip_swapped)
     attn_swapped = [to_core(order.after(attn_own))]
     skip_parts = [
@@ -942,7 +1095,7 @@
         (skip_one, quarter ^ 3, 1),
         (skip_two, quarter ^ 3, 3),
     ]
-    (skip_low,) = assemble_weight(skip_shard, skip_parts, skip_swapped, core, True, 0)
+    (skip_low,) = assemble_weight(skip_shard, skip_parts, skip_swapped, core, 0)
     joined = matmul(both_inputs, skip_low) + vectors[4]
     normed, normal_one, inverse_one = norm_forward(joined, vectors[0], vectors[1])
     normed_low = normed.astype(jnp.bfloat16)
@@ -969,7 +1122,7 @@
     ]
     attn_swapped = order.mark(*attn_swapped)
     qkv_low, proj_low = assemble_weight(
-        attn_shard, attn_parts, attn_swapped, core, False, 3 * mp_count
+        attn_shard, attn_parts, attn_swapped, core, 3 * mp_count
     )
     qkv_all = jnp.einsum(
         "itd,ed->ite",
@@ -978,14 +1131,18 @@
         preferred_element_type=jnp.float32,
     ).astype(jnp.bfloat16)
     qkv_all = order.mark(qkv_all)
+    attended = attend(qkv_all).reshape(tokens, D)
+    residual = joined + matmul(attended, proj_low) + vectors[5]
+    residual = order.mark(residual)
+    fc1_x, fc1_y = order.mark(fc1_x, fc1_y)
+    fc1_cut = order.mark(fc1_y[:2], fc1_x[2:])
+    fc1_one, fc1_two = swap_plane(order, *fc1_cut)
     fc2_own = others(order.mark(fc2_whole))
-    fc1_x, fc1_y = order.mark(fc1_x, fc1_y)
-    fc1_one, fc1_two = swap_plane(order, fc1_y[:2], fc1_x[2:])
     fc2_x, fc2_y = swap_plane(order, fc2_own, fc2_own)
-    attended = attend(order.after(qkv_all)).reshape(tokens, D)
-    residual = joined + matmul(attended, proj_low) + vectors[5]
-    normed_two, normal_two, inverse_two = norm_forward(residual, vectors[2], vectors[3])
-    residual, normed_two, normal_two = order.mark(residual, normed_two, normal_two)
+    normed_two, normal_two, inverse_two = norm_forward(
+        order.after(residual), vectors[2], vectors[3]
+    )
+    normed_two, normal_two = order.mark(normed_two, normal_two)
     normed_two_other = to_core(normal_two)
     fc1_one, fc1_two = order.mark(fc1_one, fc1_two)
     fc1_parts = [
@@ -995,13 +1152,11 @@
         (fc1_one, quarter ^ 3, 1),
         (fc1_two, quarter ^ 3, 3),
     ]
-    (fc1_low,) = assemble_weight(fc1_shard, fc1_parts, None, core, False, 0)
+    (fc1_low,) = assemble_weight(fc1_shard, fc1_parts, None, core, 0)
     fc1_low = order.mark(fc1_low)
     normed_two_other = order.mark(normed_two_other) * vectors[2] + vectors[3]
     normed_two_low = jnp.concatenate([normed_two, normed_two_other], 0).astype(jnp.bfloat16)
     normed_two_low = order.mark(normed_two_low)
-    fc2_x, fc2_y = order.mark(fc2_x, fc2_y)
-    fc2_one, fc2_two = swap_plane(order, fc2_y[:1], fc2_x[1:])
     pre_act = (
         jnp.einsum("td,fd->tf", normed_two_low, fc1_low, preferred_element_type=jnp.float32)
         + hidden_own
@@ -1012,26 +1167,33 @@
         "tf,td->fd", activated_low, upstream_low, preferred_element_type=jnp.float32
     ).reshape(4, mp_count, hidden_slice, D)
     fc2_grad = order.mark(fc2_grad)
-    fc2_add = swap_plane(order, *cut_corner(fc2_grad, quarter))
-
-    fc2_one, fc2_two = order.mark(fc2_one, fc2_two)
+    fc2_add = swap_plane(order, *order.mark(*cut_corner(fc2_grad, quarter)))
+
+    fc2_x, fc2_y = order.mark(fc2_x, fc2_y)
+    fc2_corner = others(order.mark(fc2_across))
     fc2_parts = [
         (fc2_own, quarter, 1),
         (fc2_x, quarter ^ 1, 1),
         (fc2_y, quarter ^ 2, 1),
-        (fc2_one, quarter ^ 3, 1),
-        (fc2_two, quarter ^ 3, 2),
+        (fc2_corner, quarter ^ 3, 1),
     ]
-    (fc2_low,) = assemble_weight(fc2_shard, fc2_parts, None, core, False, 0)
+    (fc2_low,) = assemble_weight(fc2_shard, fc2_parts, None, core, 0)
     fc2_low = order.mark(fc2_low)
-    act_grad = jnp.einsum("td,fd->tf", upstream_low, fc2_low, preferred_element_type=jnp.float32)
+    forward_part = order.mark(matmul(activated_low, fc2_low))
+    forward_other = to_core(forward_part[tokens:])
+    act_grad = jnp.einsum(
+        "td,fd->tf", order.after(upstream_low), fc2_low, preferred_element_type=jnp.float32
+    )
     pre_grad = gelu_pull(act_grad)[0]
     hidden_grad = jnp.sum(pre_grad, 0)
     pre_low, hidden_grad = order.mark(pre_grad.astype(jnp.bfloat16), hidden_grad)
-    back_part = order.mark(matmul(pre_low, fc1_low))
+    block_own = residual + forward_part[:tokens] + order.mark(forward_other)
+    block_own = order.mark(block_own.reshape(images, SEQ, D))
+    block_all = lax.all_gather(block_own, "mp")
+    fc2_add = order.mark(*fc2_add)
+    fc2_sides = swap_plane(order, *order.mark(*cut_sides(fc2_grad, quarter, *fc2_add)))
+    back_part = order.mark(matmul(order.after(pre_low), fc1_low))
     back_other = to_core(back_part[tokens:])
-    fc2_add = order.mark(*fc2_add)
-    fc2_sides = swap_plane(order, *cut_sides(fc2_grad, quarter, *fc2_add))
     fc1_grad = jnp.einsum(
         "tf,td->fd",
         order.after(pre_low),
@@ -1039,7 +1201,7 @@
         preferred_element_type=jnp.float32,
     ).reshape(4, mp_count, hidden_slice, D)
     fc1_grad = order.mark(fc1_grad)
-    fc1_add = swap_plane(order, *cut_corner(fc1_grad, quarter))
+    fc1_add = swap_plane(order, *order.mark(*cut_corner(fc1_grad, quarter)))
     norm_two_in = back_part[:tokens] + order.mark(back_other)
     back_two, gain_two_grad, bias_two_grad = norm_backward(
         norm_two_in, normal_two, inverse_two, vectors[2]
@@ -1047,35 +1209,25 @@
     residual_grad = upstream + back_two
     residual_low = residual_grad.astype(jnp.bfloat16)
     residual_grad, residual_low = order.mark(residual_grad, residual_low)
-    forward_part = order.mark(matmul(order.after(activated_low), fc2_low))
-    forward_other = to_core(forward_part[tokens:])
     attended_grad = jnp.einsum(
         "td,ed->te", residual_low, proj_low, preferred_element_type=jnp.float32
     ).astype(jnp.bfloat16)
-    attended_grad = order.mark(attended_grad)
-    block_own = residual + forward_part[:tokens] + order.mark(forward_other)
-    block_all = lax.all_gather(order.mark(block_own), "mp")
     qkv_grad_low = attend_back(
-        qkv_all, order.after(attended_grad).reshape(images, SEQ, D)
+        qkv_all, order.mark(attended_grad.reshape(images, SEQ, D))
     ).reshape(tokens, 3 * D)
     qkv_grad_low = order.mark(qkv_grad_low)
-    fc1_add = order.mark(*fc1_add)
-    fc1_sides = swap_plane(order, *cut_sides(fc1_grad, quarter, *fc1_add))
     fc2_sides = order.mark(*fc2_sides)
     fc2_piece = sum_deep(order, fc2_grad, quarter, *fc2_sides)
-
-    def by_core(array, leading):
-        return array.reshape(tokens, leading, mp_count, 2, -1)
-
-    def attn_half(which):
-        left = pick(by_core(qkv_grad_low, 3), which, 3).reshape(tokens, -1)
-        first = jnp.einsum("te,td->ed", left, normed_low, preferred_element_type=jnp.float32)
-        left = pick(by_core(attended, 1), which, 3).reshape(tokens, -1)
-        second = jnp.einsum("te,td->ed", left, residual_low, preferred_element_type=jnp.float32)
-        return first, second
-
-    attn_given = order.mark(*attn_half(1 - core))
+    qkv_grad = jnp.einsum(
+        "te,td->ed", order.after(qkv_grad_low), normed_low, preferred_element_type=jnp.float32
+    ).reshape(3 * mp_count, 2, hidden_slice, D)
+    proj_grad = jnp.einsum(
+        "te,td->ed", attended, order.after(residual_low), preferred_element_type=jnp.float32
+    ).reshape(mp_count, 2, hidden_slice, D)
+    attn_given = order.mark(pick(qkv_grad, 1 - core, 1), pick(proj_grad, 1 - core, 1))
     attn_given = [to_core(array) for array in attn_given]
+    fc1_add = order.mark(*fc1_add)
+    fc1_sides = swap_plane(order, *order.mark(*cut_sides(fc1_grad, quarter, *fc1_add)))
     norm_one_in = matmul(order.after(qkv_grad_low), qkv_low)
     back_one, gain_one_grad, bias_one_grad = norm_backward(
         norm_one_in, normal_one, inverse_one, vectors[0]
@@ -1083,39 +1235,32 @@
     joined_grad = residual_grad + back_one
     joined_low = joined_grad.astype(jnp.bfloat16)
     joined_grad, joined_low = order.mark(joined_grad, joined_low)
-    attn_kept = order.mark(*attn_half(core))
-
-    inputs_view = both_inputs.reshape(tokens, mp_count, 4, 2, -1).transpose(0, 2, 1, 3, 4)
-
-    def skip_half(which):
-        left = pick(inputs_view, which, 3).reshape(tokens, -1)
-        return jnp.einsum("te,td->ed", left, joined_low, preferred_element_type=jnp.float32)
-
-    skip_given = order.mark(skip_half(1 - core))
+    skip_grad = jnp.einsum(
+        "tc,td->cd", both_inputs, joined_low, preferred_element_type=jnp.float32
+    ).reshape(4 * mp_count, 2, -1, D)
+    skip_given = order.mark(pick(skip_grad, 1 - core, 1))
     skip_given = to_core(skip_given)
+    block_all = order.mark(block_all)
     attn_given = order.mark(*attn_given)
-    attn_grad = jnp.concatenate(
-        [kept + given for kept, given in zip(attn_kept, attn_given)], 0
-    ).reshape(4, mp_count, hidden_slice, D)
-    attn_grad = order.mark(attn_grad)
-    attn_add = swap_plane(order, *cut_corner(attn_grad, quarter))
-    skip_shards = skip_low.reshape(mp_count, 2 * width_local, D)
+    attn_grad = add_half([qkv_grad, proj_grad], attn_given, core)
+    attn_grad = order.mark(attn_grad.reshape(4, mp_count, hidden_slice, D))
+    attn_add = swap_plane(order, *order.mark(*cut_corner(attn_grad, quarter)))
+    fc1_sides = order.mark(*fc1_sides)
+    fc1_piece = sum_deep(order, fc1_grad, quarter, *fc1_sides)
+    skip_shards = skip_low.reshape(4, mp_count, -1, D)
     both_grads = []
     for shift in (1, 2, 3, 0):
-        shard_low = pick(skip_shards, lax.rem(mp_index + shift, mp_count), 0)
+        shard_low = pick(skip_shards, lax.rem(mp_index + shift, mp_count), 1).reshape(-1, D)
         both = jnp.einsum("td,cd->tc", joined_low, shard_low, preferred_element_type=jnp.float32)
         both = order.mark(both)
-        both_grads.append(turn_mp(both, shift) if shift == 1 else both)
-    skip_kept = order.mark(skip_half(core))
-    skip_grad = order.mark((skip_kept + order.mark(skip_given)).reshape(4, mp_count, -1, D))
-
-    fc1_sides = order.mark(*fc1_sides)
-    fc1_piece = sum_deep(order, fc1_grad, quarter, *fc1_sides)
+        both_grads.append(both)
     attn_add = order.mark(*attn_add)
-    attn_sides = swap_plane(order, *cut_sides(attn_grad, quarter, *attn_add))
-    skip_add = swap_plane(order, *cut_corner(skip_grad, quarter))
-    both_grads[0] = order.mark(both_grads[0])
-    both_grads[1] = turn_mp(order.after(both_grads[1]), 2)
+    attn_sides = swap_plane(order, *order.mark(*cut_sides(attn_grad, quarter, *attn_add)))
+    skip_given = order.mark(skip_given)
+    skip_grad = add_half([skip_grad], [skip_given], core)
+    skip_grad = order.mark(skip_grad.reshape(4, mp_count, -1, D))
+    skip_add = swap_plane(order, *order.mark(*cut_corner(skip_grad, quarter)))
+    fc2_piece = order.mark(fc2_piece)
     vector_grad = jnp.stack(
         [
             gain_one_grad,
@@ -1130,87 +1275,133 @@
     hidden_grad = hidden_grad.reshape(4, mp_count, 1, hidden_slice).transpose(1, 0, 2, 3)
     hidden_grad = jnp.where(jnp.arange(2)[None, None, :, None] == core, hidden_grad, 0.0)
     small = order.mark(jnp.concatenate([vector_grad.reshape(-1), hidden_grad.reshape(-1)]))
-    skip_add = order.mark(*skip_add)
-    skip_sides = swap_plane(order, *cut_sides(skip_grad, quarter, *skip_add))
-    attn_sides = order.mark(*attn_sides)
-    attn_piece = sum_deep(order, attn_grad, quarter, *attn_sides)
-    small = order.mark(small + to_core(small))
-    both_grads[1] = order.mark(both_grads[1])
-    both_grads[2] = turn_mp(order.after(both_grads[2]), 3)
-    block_all = order.mark(block_all)
-    block_output = (block_all.reshape(-1, D) + vectors[6]).astype(jnp.bfloat16)
-    block_output = order.mark(block_output)
-    half = hidden_slice // 2
-
-    def spread(piece):
-        return swap_plane(order, piece, piece)
-
-    def spread_far(near):
-        half = near[0].shape[0] // 2
-        return swap_plane(order, near[1][:half], near[0][half:])
-
-    fc2_piece = order.mark(fc2_piece)
-    fc2_near = spread(fc2_piece)
-    small_x = to_x(order.after(small))
-    skip_sides = order.mark(*skip_sides)
-    skip_piece = sum_deep(order, skip_grad, quarter, *skip_sides)
-    fc2_near = order.mark(*fc2_near)
-    fc2_far = spread_far(fc2_near)
-    small = order.mark(small + small_x)
-    small_y = to_y(small)
-    fc1_piece = order.mark(fc1_piece)
-    fc1_near = spread(fc1_piece)
-    fc2_far = order.mark(*fc2_far)
-    fc2_held = order.mark(hold((fc2_piece, *fc2_near, *fc2_far), quarter))
-    fc2_other = to_core(fc2_held)
-    small = order.mark(small + small_y)
-    small = order.mark(jnp.sum(gather_deep(small), 0))
-    fc1_near = order.mark(*fc1_near)
-    fc1_far = spread_far(fc1_near)
-    both_grads[2] = order.mark(both_grads[2])
-    input_grads = in_turn([both_grads[3]] + both_grads[:3])
-    input_grad = input_grads[:, :, :width_local].reshape(-1, width_local)
-    skip_input_grad = input_grads[:, :, width_local:].reshape(-1, width_local)
-    input_grad, skip_input_grad = order.mark(input_grad, skip_input_grad)
-    fc2_sum = interleave(fc2_held, order.mark(fc2_other), core)
-    fc2_part = Tensor(fc2_sum[None], fc2_weight[None], fc2_rows[None], fc2_cols[None], 1)
-    fc1_far = order.mark(*fc1_far)
-    fc1_held = order.mark(hold((fc1_piece, *fc1_near, *fc1_far), quarter))
-    fc1_other = to_core(fc1_held)
-    attn_piece = order.mark(attn_piece)
-    attn_near = spread(attn_piece)
-    fc1_sum = interleave(fc1_held, order.mark(fc1_other), core).T
-    fc1_part = Tensor(fc1_sum[None], fc1_weight[None], fc1_rows[None], fc1_cols[None], 2)
     weight_sq = jnp.stack(
         [
             jnp.sum(array * array)
             for array in (skip_weight, qkv_weight, proj_weight, fc1_weight, fc2_weight, hidden_bias)
         ]
     )
+    small_core = to_core(small)
     weight_sq = order.mark(weight_sq)
-    weight_sq = jnp.sum(exchange([fc2_part, fc1_part], weight_sq), 0)
-    fc2_part.step_sq, fc1_part.step_sq = order.mark(fc2_part.step_sq, fc1_part.step_sq)
+    fc1_piece = order.mark(fc1_piece)
+    both_grads[0] = turn_mp(order.after(both_grads[0]), 1)
+    attn_sides = order.mark(*attn_sides)
+    attn_piece = sum_deep(order, attn_grad, quarter, *attn_sides)
+    skip_add = order.mark(*skip_add)
+    skip_sides = swap_plane(order, *order.mark(*cut_sides(skip_grad, quarter, *skip_add)))
+    small = order.mark(small + order.mark(small_core))
+    small_x = to_x(small)
+    skip_sides = order.mark(*skip_sides)
+    small = order.mark(small + order.mark(small_x))
+    small_y = to_y(small)
+    skip_piece = sum_deep(order, skip_grad, quarter, *skip_sides)
+
+    def spread(piece):
+        return swap_plane(order, piece, piece)
+
+    def half_of(rows):
+        return (rows // 2 + 7) // 8 * 8
+
+    def spread_far(near):
+        half = half_of(near[0].shape[0])
+        return swap_plane(order, near[1][:half], near[0][half:])
+
+    def hold(piece, near, far):
+        rows, half = piece.shape[0], far[0].shape[0]
+        return place_rows(
+            [
+                (piece, 0, rows, quarter * rows),
+                (near[0], 0, rows, (quarter ^ 1) * rows),
+                (near[1], 0, rows, (quarter ^ 2) * rows),
+                (far[0], 0, half, (quarter ^ 3) * rows),
+                (far[1], 0, rows - half, (quarter ^ 3) * rows + half),
+            ],
+            4 * rows,
+        )
+
+    def interleave(held, other, near_state):
+        rows = held.shape[0] // 4
+        pieces = []
+        for n in range(4):
+            pieces.append((held, n * rows, rows, (2 * n + core) * rows))
+            pieces.append((other, n * rows, rows, (2 * n + 1 - core) * rows))
+        whole, sent = place_rows(pieces, 8 * rows, near_state)
+        return whole.reshape(near_state.shape + (D,)), sent
+
+    def own_state(state):
+        width = state.shape[-1] // mp_count
+        return lax.dynamic_slice_in_dim(state, mp_index * width, width, state.ndim - 1)
+
+    def everywhere(array):
+        return [array] + [turn_mp(array, shift) for shift in range(1, mp_count)]
+
+    fc2_near, fc1_near = spread(fc2_piece), spread(fc1_piece)
+    attn_piece = order.mark(attn_piece)
+    fc2_near = order.mark(*fc2_near)
+    both_grads[0] = order.mark(both_grads[0])
+    fc2_far = spread_far(fc2_near)
+    small = order.mark(small + order.mark(small_y))
+    fc1_near = order.mark(*fc1_near)
+    fc1_far = spread_far(fc1_near)
+    fc2_far = order.mark(*fc2_far)
+    attn_near = spread(attn_piece)
+    fc2_held = order.mark(hold(fc2_piece, fc2_near, fc2_far))
+    skip_piece = order.mark(skip_piece)
+    both_grads[1] = turn_mp(order.after(both_grads[1]), 2)
+    fc1_far = order.mark(*fc1_far)
+    skip_near = spread(skip_piece)
+    fc1_held = order.mark(hold(fc1_piece, fc1_near, fc1_far))
     attn_near = order.mark(*attn_near)
+    fc2_other = to_core(order.after(fc2_held))
     attn_far = spread_far(attn_near)
-    skip_piece = order.mark(skip_piece)
-    skip_near = spread(skip_piece)
-    attn_far = order.mark(*attn_far)
-    attn_held = order.mark(hold((attn_piece, *attn_near, *attn_far), quarter))
-    attn_other = to_core(attn_held)
     skip_near = order.mark(*skip_near)
     skip_far = spread_far(skip_near)
-    attn_sum = interleave(attn_held, order.mark(attn_other), core)
-    qkv_sum = attn_sum[: 3 * width_local].reshape(3, width_local, D).transpose(0, 2, 1)
-    proj_sum = attn_sum[3 * width_local :]
-    qkv_sum, proj_sum = order.mark(qkv_sum, proj_sum)
+    fc2_sum, fc2_moments = order.mark(
+        *interleave(fc2_held, order.mark(fc2_other), own_state(fc2_rows)[None])
+    )
+    fc1_other = to_core(order.after(fc1_held))
+    attn_far = order.mark(*attn_far)
+    attn_held = order.mark(hold(attn_piece, attn_near, attn_far))
+    attn_other = to_core(attn_held)
     skip_far = order.mark(*skip_far)
-    skip_held = order.mark(hold((skip_piece, *skip_near, *skip_far), quarter))
+    skip_held = order.mark(hold(skip_piece, skip_near, skip_far))
     skip_other = to_core(skip_held)
-    qkv_part = Tensor(qkv_sum, qkv_weight, qkv_rows, qkv_cols, 2)
-    proj_part = Tensor(proj_sum[None], proj_weight[None], proj_rows[None], proj_cols[None], 1)
-    skip_sum = interleave(skip_held, order.mark(skip_other), core).reshape(2, width_local, D)
-    skip_part = Tensor(skip_sum, skip_weight, skip_rows, skip_cols, 1)
-    exchange([qkv_part, proj_part, skip_part], jnp.zeros((128,), jnp.float32))
+    both_grads[1] = order.mark(both_grads[1])
+    both_grads[2] = turn_mp(order.after(both_grads[2]), 3)
+    fc1_sum, fc1_moments = order.mark(
+        *interleave(fc1_held, order.mark(fc1_other), own_state(fc1_cols)[None])
+    )
+    hidden_sent = everywhere(order.mark(jnp.concatenate([fc2_moments, fc1_moments], 0)))
+    attn_state = jnp.concatenate([own_state(qkv_cols), own_state(proj_rows)[None]], 0)
+    attn_sum, attn_moments = order.mark(
+        *interleave(attn_held, order.mark(attn_other), attn_state)
+    )
+    skip_sum, skip_moments = order.mark(
+        *interleave(skip_held, order.mark(skip_other), own_state(skip_rows))
+    )
+    hidden_sent = order.mark(*hidden_sent)
+    both_grads[2] = order.mark(both_grads[2])
+    token_sent = everywhere(order.mark(jnp.concatenate([attn_moments, skip_moments], 0)))
+    small_all = everywhere(order.after(small))
+    fc2_sent = [array[:1] for array in hidden_sent]
+    fc1_sent = [array[1:] for array in hidden_sent]
+    fc2_far_new, *fc2_scales, fc2_step = order.mark(
+        *scales(fc2_sum, fc2_cols[None], fc2_sent, mp_index, (True,))
+    )
+    fc1_far_new, *fc1_scales, fc1_step = order.mark(
+        *scales(fc1_sum, fc1_rows[None], fc1_sent, mp_index, (False,))
+    )
+    token_sent = order.mark(*token_sent)
+    small = jnp.sum(in_turn(order.mark(*small_all)), 0)
+    attn_sent = [array[:4] for array in token_sent]
+    skip_sent = [array[4:] for array in token_sent]
+    attn_state = jnp.concatenate([qkv_rows, proj_cols[None]], 0)
+    attn_far_new, *attn_scales, attn_step = order.mark(
+        *scales(attn_sum, attn_state, attn_sent, mp_index, (False, False, False, True))
+    )
+    skip_far_new, *skip_scales, skip_step = order.mark(
+        *scales(skip_sum, skip_cols, skip_sent, mp_index, (True, True))
+    )
 
     vector_sum = small[: 7 * D].reshape(7, D)
     hidden_sum = lax.dynamic_slice_in_dim(small[7 * D :], mp_index * hidden_local, hidden_local, 0)
@@ -1218,70 +1409,88 @@
     vector_update = vector_sum * lax.rsqrt(vector_new)
     hidden_new = 0.5 * hidden_moments + 0.5 * (hidden_sum * hidden_sum + moment_eps)
     hidden_update = hidden_sum * lax.rsqrt(hidden_new)
-    parts = [skip_part, qkv_part, proj_part, fc1_part, fc2_part]
     step_sq = jnp.sum(hidden_update * hidden_update)
-    for part in parts:
-        step_sq = step_sq + part.step_sq
-    step_total = jnp.sum(gather_deep(jnp.broadcast_to(step_sq, (128,)))[:, 0])
-    step_total = step_total + jnp.sum(vector_update * vector_update)
+    step_sq = step_sq + jnp.sum(skip_step + attn_step + fc1_step + fc2_step)
+    sent = jnp.concatenate([step_sq[None], weight_sq, jnp.zeros((121,), jnp.float32)])
+    sent = everywhere(order.mark(sent))
+    input_grads = in_turn([both_grads[3]] + both_grads[:3])
+    input_grad = input_grads[:, :, :width_local].reshape(-1, width_local)
+    skip_input_grad = input_grads[:, :, width_local:].reshape(-1, width_local)
+    input_grad, skip_input_grad = order.mark(input_grad, skip_input_grad)
+    sent = jnp.sum(in_turn(order.mark(*sent)), 0)
+    weight_sq = sent[1:]
+    step_total = sent[0] + jnp.sum(vector_update * vector_update)
     param_count = 6.0 * D * D + 2.0 * D * FF + 7.0 * D + FF
     update_rms = jnp.sqrt(step_total / param_count)
     divisor = jnp.maximum(1.0, update_rms / clip_level)
-    tensor_sizes = (2.0 * D * D, 3.0 * D * D, 1.0 * D * D, 1.0 * D * FF, 1.0 * FF * D)
-    new_weights = []
-    for position, part in enumerate(parts):
+    tensor_sizes = (2.0 * D * D, 3.0 * D * D, 1.0 * D * D, 1.0 * D * FF, 1.0 * FF * D, 1.0 * FF)
+
+    def factor_of(position):
         weight_rms = jnp.sqrt(weight_sq[position] / tensor_sizes[position])
-        factor = step_rate * jnp.maximum(0.001, weight_rms) / divisor
-        new_weights.append(part.weight - factor * part.update())
+        return step_rate * jnp.maximum(0.001, weight_rms) / divisor
+
+    skip_new, skip_new_low = renew(skip_weight, skip_sum, *skip_scales, factor_of(0), False)
+    qkv_turned = qkv_weight.transpose(0, 2, 1)
+    qkv_new, qkv_new_low = renew(qkv_turned, attn_sum, *attn_scales, factor_of(1), False)
+    qkv_new, qkv_new_low = qkv_new.transpose(0, 2, 1), qkv_new_low.transpose(0, 2, 1)
+    proj_new, proj_new_low = renew(
+        proj_weight[None], attn_sum, *attn_scales, factor_of(2), False, first=3
+    )
+    fc1_new, fc1_new_low = renew(fc1_weight[None], fc1_sum, *fc1_scales, factor_of(3), True)
+    fc2_new, fc2_new_low = renew(fc2_weight[None], fc2_sum, *fc2_scales, factor_of(4), False)
+    block_output = (block_all + vectors[6]).astype(jnp.bfloat16).reshape(-1, D)
     vector_rms = jnp.sqrt(jnp.mean(vectors * vectors, 1, keepdims=True))
     vectors_new = vectors - step_rate * jnp.maximum(0.001, vector_rms) * vector_update / divisor
-    hidden_rms = jnp.sqrt(weight_sq[5] / FF)
-    hidden_bias_new = (
-        hidden_bias - step_rate * jnp.maximum(0.001, hidden_rms) * hidden_update / divisor
-    )
-    skip_new, qkv_new = new_weights[0], new_weights[1]
-    proj_new, fc1_new, fc2_new = (array[0] for array in new_weights[2:])
+    hidden_bias_new = hidden_bias - factor_of(5) * hidden_update
     piece_width = D // dp_count
     dp_start = dp_index * piece_width
 
     def own_piece(array, axis):
         return lax.dynamic_slice_in_dim(array, dp_start, piece_width, axis)
 
+    def near_whole(sent, width):
+        near = in_turn([array[:, 1, :width] for array in sent])
+        return near.transpose(1, 0, 2).reshape(near.shape[1], -1)
+
+    skip_near_new = near_whole(skip_sent, width_local)
+    attn_near_new = near_whole(attn_sent, width_local)
+    fc1_near_new = near_whole(fc1_sent, hidden_local)
+    fc2_near_new = near_whole(fc2_sent, hidden_local)
     return (
         block_output,
         input_grad,
         skip_input_grad,
         own_piece(skip_sum, 2),
-        own_piece(qkv_sum, 1),
-        own_piece(proj_sum, 1),
-        own_piece(fc1_sum, 0),
-        own_piece(fc2_sum, 1),
+        own_piece(attn_sum[:3], 2).transpose(0, 2, 1),
+        own_piece(attn_sum[3], 1),
+        own_piece(fc1_sum[0], 1).T,
+        own_piece(fc2_sum[0], 1),
         own_piece(vector_sum, 1),
         hidden_sum,
-        skip_part.row_new,
-        skip_part.col_new,
-        qkv_part.row_new,
-        qkv_part.col_new,
-        proj_part.row_new[0],
-        proj_part.col_new[0],
-        fc1_part.row_new[0],
-        fc1_part.col_new[0],
-        fc2_part.row_new[0],
-        fc2_part.col_new[0],
+        skip_near_new,
+        skip_far_new[:, 0],
+        attn_far_new[:3, 0],
+        attn_near_new[:3],
+        attn_near_new[3],
+        attn_far_new[3, 0],
+        fc1_far_new[0, 0],
+        fc1_near_new[0],
+        fc2_near_new[0],
+        fc2_far_new[0, 0],
         vector_new,
         hidden_new,
         skip_new,
         qkv_new,
-        proj_new,
-        fc1_new,
-        fc2_new,
+        proj_new[0],
+        fc1_new[0],
+        fc2_new[0],
         vectors_new,
         hidden_bias_new,
-        skip_new.astype(jnp.bfloat16),
-        qkv_new.astype(jnp.bfloat16),
-        proj_new.astype(jnp.bfloat16),
-        fc1_new.astype(jnp.bfloat16),
-        fc2_new.astype(jnp.bfloat16),
+        skip_new_low,
+        qkv_new_low,
+        proj_new_low[0],
+        fc1_new_low[0],
+        fc2_new_low[0],
         update_rms,
     )
 

time: 1160 us -> 1080 us (0.931)
  other arithmetic: 238 us -> 115 us
  Pallas kernels: 55.4 us -> 128 us
  local copies, waits for them, and re-layouts: 260 us -> 235 us
  matrix products: 130 us -> 113 us
    pallas_call x0 -> x19, Pallas kernels: none -> 71.7 us  [the longest x8 29 us: place_rows(): pl.pallas_call(kernel, in_specs=in_specs, out_specs=out_specs, out_shape=...]
    ppermute x18, waiting for transfers between devices: 35.5 us -> 77.8 us  [turn_mp(): lax.ppermute(array, 'mp', [(i, (i + shift) % count) for i in range(count)])]
    ppermute x26 -> x25, waiting for transfers between devices: 257 us -> 227 us  [to_x(): return lax.ppermute(array, 'dp', [(i, i ^ 2) for i in range(8)])]
    reduce_sum x23 -> x5, other arithmetic: 33.1 us -> 4.64 us  [the longest x1 1.99 us: body_data(): step_total = sent[0] + jnp.sum(vector_update * vector_update)]
    convert_element_type x6 -> x1, other arithmetic: 34.9 us -> 6.77 us  [body_data(): block_output = (block_all + vectors[6]).astype(jnp.bfloat16).reshape(-1, D)]
    unnamed x215 -> x310, local copies, waits for them, and re-layouts: 73.3 us -> 100 us
    add x12 -> x7, other arithmetic: 40.5 us -> 18.9 us  [the longest x4 18.2 us: sum_deep(): own = order.mark(pick(grad, quarter, 0) + from_x + from_y)]
    another operation x12 -> x3, other arithmetic: 27.1 us -> 7.48 us  [the longest x8 18 us: interleave(): return jnp.stack([low_core, high_core], 1).reshape(-1, D)]
  transfers between devices with their start and end apart: 102 -> 101, of which waited for: 37 -> 45; matrix products, arithmetic and copies ran while one was open for 44% -> 33% of each run, Pallas kernels for 4% -> 10%
where the time goes in v2:
time: 1080 us; the launch traced here: 1070 us
  waiting for transfers between devices  360 us (33%)
  local copies, waits for them, and re-layouts  235 us (22%)
  Pallas kernels  128 us (12%)
  other arithmetic  115 us (11%)
  matrix products  113 us (10%)
  starting transfers between devices  91.2 us (8%)
  between operations  25.8 us (2%)
    ppermute x25, waiting for transfers between devices, to_x(): return lax.ppermute(array, 'dp', [(i, i ^ 2) for i in range(8)])  227 us
    unnamed x310, local copies, waits for them, and re-layouts  100 us
    ppermute x18, waiting for transfers between devices, turn_mp(): lax.ppermute(array, 'mp', [(i, (i + shift) % count) for i in range(count)])  77.8 us
    ppermute x25, waiting for transfers between devices, to_y(): return lax.ppermute(array, 'dp', [(i, i ^ 4) for i in range(8)])  39.6 us
    dot_general x5, matrix products, matmul(): return jnp.dot(left_side, right_side, preferred_element_type=jnp.float32)  36.1 us
    ppermute x25, starting transfers between devices, to_y(): return lax.ppermute(array, 'dp', [(i, i ^ 4) for i in range(8)])  32.4 us
    pallas_call x4, Pallas kernels, assemble(): pl.pallas_call(kernel, in_specs=[pl.BlockSpec(memory_space=pltpu.SMEM)] +...  30.2 us
    pallas_call x8, Pallas kernels, place_rows(): pl.pallas_call(kernel, in_specs=in_specs, out_specs=out_specs, out_shape=...  29 us
  transfers between devices with their start and end apart: 101, of which 45 were waited for; matrix products, arithmetic and copies ran while one was open for 33% of the time, Pallas kernels for 10%

profile of v2, /device:TPU:0, one launch (start us, length us, event | category | flops | bytes accessed | tf_op | source)
XLA Modules:
  0.0 1067.2 jit_solution(165096742207924767)
XLA Ops:
  34.7 6.9 copy.137
  55.4 17.5 %collective-permute-done.4.refs_3_ = f32[3,72,1152]{2,1,0:T(8,128)} collective-permute-done((f32[3,72,1152]{2,1,0:T(8,128)}, f32[3,72,1152]{2,1,0:T(8,128)}, u32[]{:S(2)}, u32[]{:S(2)}) %collective-permute-start.4) | collective-permute-done | bytes 995360 | tf_op jit(solution)/shard_map/ppermute | solution.py:467
  78.9 6.2 collective-permute-done.12.refs_9_
  85.2 6.7 collective-permute-done.11.refs_7_
  95.3 7.7 all-gather.15.cloned.1.call-done
  109.0 6.5 shard_map.512
  125.5 25.9 %collective-permute-done.16.refs_3_ = f32[3,144,1152]{2,1,0:T(8,128)} collective-permute-done((f32[3,144,1152]{2,1,0:T(8,128)}, f32[3,144,1152]{2,1,0:T(8,128)}, u32[]{:S(2)}, u32[]{:S(2)}) %collective-permute-start.16) | collective-permute-done | bytes 1990688 | tf_op jit(solution)/shard_map/ppermute | solution.py:467
  164.3 13.3 %collective-permute-done.20.refs_7_ = f32[1,144,1152]{2,1,0:T(8,128)} collective-permute-done((f32[1,144,1152]{2,1,0:T(8,128)S(1)}, f32[1,144,1152]{2,1,0:T(8,128)}, u32[]{:S(2)}, u32[]{:S(2)}) %collective-permute-start.20) | collective-permute-done | bytes 663584 | tf_op jit(solution)/shard_map/ppermute | solution.py:467
  177.6 8.4 collective-permute-done.21.refs_9_
  195.8 10.9 %shard_map.513 = (bf16[12,288,1152]{2,1,0:T(8,128)(2,1)}, bf16[4,288,1152]{2,1,0:T(8,128)(2,1)S(1)}) custom-call(s32[17]{0:T(128)S(1)} %stack.378.table_ref, f32[4,288,1152]{2,1,0:T(8,128)} %bitcast.396, f32[3,144,1152]{2,1,0:T(8,128)} %fusion.7.refs_1_, f32[3,144,1152]{2,1,0:T(8,128)} %collective-permute-done.15.refs_2_, ...), custom_call_target="tpu_custom_call" | custom-call | bytes 1024 | tf_op jit(solution)/shard_map/pallas_call | solution.py:553
  208.2 8.6 convolution_convert_fusion.qkv_ref
  216.8 9.2 shard_map.514
  229.1 6.2 fusion
  260.1 6.0 collective-permute-done.29.refs_5_
  266.1 13.7 %collective-permute-done.28.refs_4_ = f32[2,144,1152]{2,1,0:T(8,128)} collective-permute-done((f32[2,144,1152]{2,1,0:T(8,128)}, f32[2,144,1152]{2,1,0:T(8,128)}, u32[]{:S(2)}, u32[]{:S(2)}) %collective-permute-start.28) | collective-permute-done | bytes 1327136 | tf_op jit(solution)/shard_map/ppermute | solution.py:467
  279.8 6.2 shard_map.515
  290.3 9.4 multiply_convert_fusion
  299.7 8.0 fusion.39
  313.3 8.6 collective-permute-done.30.refs_2_
  329.8 6.6 shard_map.516
  336.4 8.5 fusion.40
  347.3 13.3 %fusion.30 = (f32[2304]{0:T(1024)S(1)}, bf16[1032,2304]{1,0:T(8,128)(2,1)}) fusion(f32[1032,2304]{1,0:T(8,128)S(1)} %bitcast.450, bf16[1032,1152]{1,0:T(8,128)(2,1)S(1)} %copy-done.84, bf16[2304,1152]{1,0:T(8,128)(2,1)S(1)} %bitcast.381), kind=kOutput, calls=%fused_computation.225 | convolution fusion | flops 5511571456 | bytes 21961728 | tf_op jit(solution)/shard_map/td,fd->tf/dot_general | solution.py:1184
  362.8 13.4 %collective-permute-done.33 = f32[2,144,1152]{2,1,0:T(8,128)} collective-permute-done((f32[2,144,1152]{2,1,0:T(8,128)}, f32[2,144,1152]{2,1,0:T(8,128)}, u32[]{:S(2)}, u32[]{:S(2)}) %collective-permute-start.33) | collective-permute-done | bytes 1327136 | tf_op jit(solution)/shard_map/ppermute | solution.py:467
  383.1 9.3 fusion.41
  395.6 7.9 fusion.42
  423.7 16.6 %shard_map.517 = bf16[2,258,3456]{2,1,0:T(8,128)(2,1)S(1)} custom-call(bf16[2,258,3456]{2,1,0:T(8,128)(2,1)S(1)} %copy-done.16, bf16[2,258,1152]{2,1,0:T(8,128)(2,1)S(1)} %reshape.395.grad_ref), custom_call_target="tpu_custom_call" | custom-call | bytes 1024 | tf_op jit(solution)/shard_map/pallas_call | solution.py:969
  446.7 6.2 collective-permute-done.38
  454.1 5.2 fusion.3
  468.2 7.0 fusion.43
  485.2 5.0 constant_dynamic-slice_fusion.13
  490.7 24.3 %collective-permute-done.36 = f32[2,144,1152]{2,1,0:T(8,128)} collective-permute-done((f32[2,144,1152]{2,1,0:T(8,128)}, f32[2,144,1152]{2,1,0:T(8,128)}, u32[]{:S(2)}, u32[]{:S(2)}) %collective-permute-start.36) | collective-permute-done | bytes 1327136 | tf_op jit(solution)/shard_map/ppermute | solution.py:467
  524.5 8.7 multiply_reduce_fusion.5
  548.8 14.2 %shard_map.518 = f32[16,144,1152]{2,1,0:T(8,128)} custom-call(s32[1]{0:T(128)} %bitcast.26.core_ref, f32[12,2,144,1152]{3,2,1,0:T(8,128)} %bitcast.394, f32[4,2,144,1152]{3,2,1,0:T(8,128)S(1)} %copy-done.24, f32[12,144,1152]{2,1,0:T(8,128)} %collective-permute-done.42.refs_2_, f32[4,144,1152]{2,1,0:T(8,128)S(1)} %collective-permute-done.43.refs_3_), custom_call_target="tpu_custom_call" | custom-call | bytes 1024 | tf_op jit(solution)/shard_map/pallas_call | solution.py:753
  563.0 5.1 dynamic-slice_bitcast_fusion.5
  568.0 12.8 %collective-permute-done.40 = f32[4,144,1152]{2,1,0:T(8,128)} collective-permute-done((f32[4,144,1152]{2,1,0:T(8,128)}, f32[4,144,1152]{2,1,0:T(8,128)}, u32[]{:S(2)}, u32[]{:S(2)}) %collective-permute-start.40) | collective-permute-done | bytes 2654240 | tf_op jit(solution)/shard_map/ppermute | solution.py:467
  584.0 5.2 fusion.2
  601.3 10.1 collective-permute-done.45
  636.3 9.6 shard_map.519
  648.8 27.1 %collective-permute-done.49 = f32[4,144,1152]{2,1,0:T(8,128)} collective-permute-done((f32[4,144,1152]{2,1,0:T(8,128)}, f32[4,144,1152]{2,1,0:T(8,128)}, u32[]{:S(2)}, u32[]{:S(2)}) %collective-permute-start.49) | collective-permute-done | bytes 2654240 | tf_op jit(solution)/shard_map/ppermute | solution.py:467
  676.4 5.2 fusion.1
  684.5 10.3 collective-permute-done.47
  702.7 21.7 %collective-permute-done.51 = f32[4,72,1152]{2,1,0:T(8,128)S(1)} collective-permute-done((f32[4,72,1152]{2,1,0:T(8,128)S(1)}, f32[4,72,1152]{2,1,0:T(8,128)S(1)}, u32[]{:S(2)}, u32[]{:S(2)}) %collective-permute-start.51) | collective-permute-done | bytes 1327136 | tf_op jit(solution)/shard_map/ppermute | solution.py:467
  737.0 9.2 collective-permute-done.55.refs_1_
  748.0 27.9 %collective-permute-done.57 = f32[516,576]{1,0:T(8,128)} collective-permute-done((f32[516,576]{1,0:T(8,128)}, f32[516,576]{1,0:T(8,128)}, u32[]{:S(2)}, u32[]{:S(2)}) %collective-permute-start.57) | collective-permute-done | bytes 1188896 | tf_op jit(solution)/shard_map/ppermute | solution.py:476
  780.1 7.3 collective-permute-done.62
  851.8 6.8 add_convert_fusion
  863.1 42.4 %collective-permute-done.63 = f32[516,576]{1,0:T(8,128)} collective-permute-done((f32[516,576]{1,0:T(8,128)}, f32[516,576]{1,0:T(8,128)}, u32[]{:S(2)}, u32[]{:S(2)}) %collective-permute-start.63) | collective-permute-done | bytes 1188896 | tf_op jit(solution)/shard_map/ppermute | solution.py:476
  993.3 5.2 collective-permute-done.82
  (763 shorter events, 503.6 us)
Async XLA Ops:
  7.2 39.2 %all-gather.13.cloned.1.call-start = ((), (), s32[]{:S(2)}) async-start(), calls=%async_computation.7 | async-start | bytes 1658880 | tf_op jit(solution)/shard_map/all_gather | solution.py:608
  9.1 93.9 %all-gather.15.cloned.1.call-start = ((), (), s32[]{:S(2)}) async-start(), calls=%async_computation.8 | async-start | bytes 3317760 | tf_op jit(solution)/shard_map/all_gather | solution.py:608
  15.3 149.0 %all-gather.17.cloned.1.call-start = ((), (), s32[]{:S(2)}) async-start(), calls=%async_computation.9 | async-start | bytes 3317760 | tf_op jit(solution)/shard_map/all_gather | solution.py:608
  78.3 30.6 %collective-permute-start.10 = (f32[3,72,1152]{2,1,0:T(8,128)}, f32[3,72,1152]{2,1,0:T(8,128)}, u32[]{:S(2)}, u32[]{:S(2)}) collective-permute-start(f32[3,72,1152]{2,1,0:T(8,128)} %collective-permute-done.5.refs_5_), channel_id=1, source_target_pairs={{0,4},{4,0},{8,12},{12,8},{16,20},{20,16},{24,28},{28,24},{1,5},{5... | collective-permute-start | bytes 2985992 | tf_op jit(solution)/shard_map/ppermute | solution.py:463
  78.8 30.1 %collective-permute-start.9 = (f32[3,72,1152]{2,1,0:T(8,128)}, f32[3,72,1152]{2,1,0:T(8,128)}, u32[]{:S(2)}, u32[]{:S(2)}) collective-permute-start(f32[3,72,1152]{2,1,0:T(8,128)} %collective-permute-done.4.refs_3_), channel_id=1, source_target_pairs={{0,4},{4,0},{8,12},{12,8},{16,20},{20,16},{24,28},{28,24},{1,5},{5... | collective-permute-start | bytes 2985992 | tf_op jit(solution)/shard_map/ppermute | solution.py:463
  95.0 146.0 %all-gather.19.cloned.1.call-start = ((), (), s32[]{:S(2)}) async-start(), calls=%async_computation.10 | async-start | bytes 3317760 | tf_op jit(solution)/shard_map/all_gather | solution.py:608
  106.0 45.4 %collective-permute-start.16 = (f32[3,144,1152]{2,1,0:T(8,128)}, f32[3,144,1152]{2,1,0:T(8,128)}, u32[]{:S(2)}, u32[]{:S(2)}) collective-permute-start(f32[3,144,1152]{2,1,0:T(8,128)} %fusion.7.refs_1_), channel_id=1, source_target_pairs={{0,8},{4,12},{8,0},{12,4},{16,24},{20,28},{24,16},{28,20},{1,9},{5... | collective-permute-start | bytes 5971976 | tf_op jit(solution)/shard_map/ppermute | solution.py:467
  107.5 45.1 %collective-permute-start.17 = (f32[3,144,1152]{2,1,0:T(8,128)}, f32[3,144,1152]{2,1,0:T(8,128)}, u32[]{:S(2)}, u32[]{:S(2)}) collective-permute-start(f32[3,144,1152]{2,1,0:T(8,128)} %fusion.7.refs_1_), channel_id=1, source_target_pairs={{0,16},{4,20},{8,24},{12,28},{16,0},{20,4},{24,8},{28,12},{1,17},{... | collective-permute-start | bytes 5971976 | tf_op jit(solution)/shard_map/ppermute | solution.py:471
  121.8 38.4 %collective-permute-start.22 = (f32[516,1152]{1,0:T(8,128)}, f32[516,1152]{1,0:T(8,128)}, u32[]{:S(2)}, u32[]{:S(2)}) collective-permute-start(f32[516,1152]{1,0:T(8,128)} %convert_multiply_fusion), channel_id=1, source_target_pairs={{0,4},{4,0},{8,12},{12,8},{16,20},{20,16},{24,28},{28,24},{1,5},{5... | collective-permute-start | bytes 7133192 | tf_op jit(solution)/shard_map/ppermute | solution.py:463
  159.5 165.0 %all-gather.21.cloned.1.call-start = ((), (), s32[]{:S(2)}) async-start(), calls=%async_computation.11 | async-start | bytes 3317760 | tf_op jit(solution)/shard_map/all_gather | solution.py:608
  159.6 35.1 %collective-permute-start.19 = (f32[3,144,1152]{2,1,0:T(8,128)}, f32[3,144,1152]{2,1,0:T(8,128)}, u32[]{:S(2)}, u32[]{:S(2)}) collective-permute-start(f32[3,144,1152]{2,1,0:T(8,128)} %collective-permute-done.17.refs_5_), channel_id=1, source_target_pairs={{0,4},{4,0},{8,12},{12,8},{16,20},{20,16},{24,28},{28,24},{1,5},{5... | collective-permute-start | bytes 5971976 | tf_op jit(solution)/shard_map/ppermute | solution.py:463
  160.1 34.6 %collective-permute-start.18 = (f32[3,144,1152]{2,1,0:T(8,128)}, f32[3,144,1152]{2,1,0:T(8,128)}, u32[]{:S(2)}, u32[]{:S(2)}) collective-permute-start(f32[3,144,1152]{2,1,0:T(8,128)} %collective-permute-done.16.refs_3_), channel_id=1, source_target_pairs={{0,4},{4,0},{8,12},{12,8},{16,20},{20,16},{24,28},{28,24},{1,5},{5... | collective-permute-start | bytes 5971976 | tf_op jit(solution)/shard_map/ppermute | solution.py:463
  188.3 47.0 %collective-permute-start.25 = (f32[3,144,1152]{2,1,0:T(8,128)S(1)}, f32[3,144,1152]{2,1,0:T(8,128)}, u32[]{:S(2)}, u32[]{:S(2)}) collective-permute-start(f32[3,144,1152]{2,1,0:T(8,128)S(1)} %fusion.6.refs_1_), channel_id=1, source_target_pairs={{0,8},{4,12},{8,0},{12,4},{16,24},{20,28},{24,16},{28,20},{1,9},{5... | collective-permute-start | bytes 5971976 | tf_op jit(solution)/shard_map/ppermute | solution.py:467
  190.7 45.7 %collective-permute-start.26 = (f32[3,144,1152]{2,1,0:T(8,128)S(1)}, f32[3,144,1152]{2,1,0:T(8,128)}, u32[]{:S(2)}, u32[]{:S(2)}) collective-permute-start(f32[3,144,1152]{2,1,0:T(8,128)S(1)} %fusion.6.refs_1_), channel_id=1, source_target_pairs={{0,16},{4,20},{8,24},{12,28},{16,0},{20,4},{24,8},{28,12},{1,17},{... | collective-permute-start | bytes 5971976 | tf_op jit(solution)/shard_map/ppermute | solution.py:471
  247.5 38.5 %collective-permute-start.27 = (f32[516,1152]{1,0:T(8,128)}, f32[516,1152]{1,0:T(8,128)}, u32[]{:S(2)}, u32[]{:S(2)}) collective-permute-start(f32[516,1152]{1,0:T(8,128)} %get-tuple-element.394), channel_id=1, source_target_pairs={{0,4},{4,0},{8,12},{12,8},{16,20},{20,16},{24,28},{28,24},{1,5},{5... | collective-permute-start | bytes 7133192 | tf_op jit(solution)/shard_map/ppermute | solution.py:463
  247.5 32.2 %collective-permute-start.28 = (f32[2,144,1152]{2,1,0:T(8,128)}, f32[2,144,1152]{2,1,0:T(8,128)}, u32[]{:S(2)}, u32[]{:S(2)}) collective-permute-start(f32[2,144,1152]{2,1,0:T(8,128)} %slice.423), channel_id=1, source_target_pairs={{0,8},{4,12},{8,0},{12,4},{16,24},{20,28},{24,16},{28,20},{1,9},{5... | collective-permute-start | bytes 3981320 | tf_op jit(solution)/shard_map/ppermute | solution.py:467
  253.2 293.0 %all-gather.23.cloned.1.call-start = ((), (), s32[]{:S(2)}) async-start(), calls=%async_computation.12 | async-start | bytes 12165120 | tf_op jit(solution)/shard_map/all_gather | solution.py:1192
  258.0 63.9 %collective-permute-start.30 = (f32[3,144,1152]{2,1,0:T(8,128)S(1)}, f32[3,144,1152]{2,1,0:T(8,128)S(1)}, u32[]{:S(2)}, u32[]{:S(2)}) collective-permute-start(f32[3,144,1152]{2,1,0:T(8,128)S(1)} %fusion.5.refs_1_), channel_id=1, source_target_pairs={{0,8},{4,12},{8,0},{12,4},{16,24},{20,28},{24,16},{28,20},{1,9},{5... | collective-permute-start | bytes 5971976 | tf_op jit(solution)/shard_map/ppermute | solution.py:467
  259.5 63.7 %collective-permute-start.31 = (f32[3,144,1152]{2,1,0:T(8,128)S(1)}, f32[3,144,1152]{2,1,0:T(8,128)S(1)}, u32[]{:S(2)}, u32[]{:S(2)}) collective-permute-start(f32[3,144,1152]{2,1,0:T(8,128)S(1)} %fusion.5.refs_1_), channel_id=1, source_target_pairs={{0,16},{4,20},{8,24},{12,28},{16,0},{20,4},{24,8},{28,12},{1,17},{... | collective-permute-start | bytes 5971976 | tf_op jit(solution)/shard_map/ppermute | solution.py:471
  345.1 31.1 %collective-permute-start.33 = (f32[2,144,1152]{2,1,0:T(8,128)}, f32[2,144,1152]{2,1,0:T(8,128)}, u32[]{:S(2)}, u32[]{:S(2)}) collective-permute-start(f32[2,144,1152]{2,1,0:T(8,128)} %get-tuple-element.418), channel_id=1, source_target_pairs={{0,8},{4,12},{8,0},{12,4},{16,24},{20,28},{24,16},{28,20},{1,9},{5... | collective-permute-start | bytes 3981320 | tf_op jit(solution)/shard_map/ppermute | solution.py:467
  345.8 30.8 %collective-permute-start.34 = (f32[2,144,1152]{2,1,0:T(8,128)}, f32[2,144,1152]{2,1,0:T(8,128)}, u32[]{:S(2)}, u32[]{:S(2)}) collective-permute-start(f32[2,144,1152]{2,1,0:T(8,128)} %get-tuple-element.419), channel_id=1, source_target_pairs={{0,16},{4,20},{8,24},{12,28},{16,0},{20,4},{24,8},{28,12},{1,17},{... | collective-permute-start | bytes 3981320 | tf_op jit(solution)/shard_map/ppermute | solution.py:471
  362.8 286.0 %reduce-scatter.9.cloned.1.call-start = ((), (), s32[]{:S(2)}) async-start(), calls=%async_computation.5 | async-start | bytes 3317760 | tf_op jit(solution)/shard_map/reduce_scatter | solution.py:657
  392.6 60.3 %collective-permute-start.38 = (f32[4,144,1152]{2,1,0:T(8,128)}, f32[4,144,1152]{2,1,0:T(8,128)}, u32[]{:S(2)}, u32[]{:S(2)}) collective-permute-start(f32[4,144,1152]{2,1,0:T(8,128)} %pad_maximum_fusion.2), channel_id=1, source_target_pairs={{0,8},{4,12},{8,0},{12,4},{16,24},{20,28},{24,16},{28,20},{1,9},{5... | collective-permute-start | bytes 7962632 | tf_op jit(solution)/shard_map/ppermute | solution.py:467
  394.1 60.0 %collective-permute-start.39 = (f32[4,144,1152]{2,1,0:T(8,128)}, f32[4,144,1152]{2,1,0:T(8,128)}, u32[]{:S(2)}, u32[]{:S(2)}) collective-permute-start(f32[4,144,1152]{2,1,0:T(8,128)} %pad_maximum_fusion.3), channel_id=1, source_target_pairs={{0,16},{4,20},{8,24},{12,28},{16,0},{20,4},{24,8},{28,12},{1,17},{... | collective-permute-start | bytes 7962632 | tf_op jit(solution)/shard_map/ppermute | solution.py:471
  483.2 63.1 %collective-permute-start.42 = (f32[12,144,1152]{2,1,0:T(8,128)}, f32[12,144,1152]{2,1,0:T(8,128)}, u32[]{:S(2)}, u32[]{:S(2)}) collective-permute-start(f32[12,144,1152]{2,1,0:T(8,128)} %dynamic-slice_bitcast_fusion), channel_id=1, source_target_pairs={{0,4},{4,0},{8,12},{12,8},{16,20},{20,16},{24,28},{28,24},{1,5},{5... | collective-permute-start | bytes 23887880 | tf_op jit(solution)/shard_map/ppermute | solution.py:463
  483.2 31.9 %collective-permute-start.36 = (f32[2,144,1152]{2,1,0:T(8,128)}, f32[2,144,1152]{2,1,0:T(8,128)}, u32[]{:S(2)}, u32[]{:S(2)}) collective-permute-start(f32[2,144,1152]{2,1,0:T(8,128)} %get-tuple-element.434), channel_id=1, source_target_pairs={{0,8},{4,12},{8,0},{12,4},{16,24},{20,28},{24,16},{28,20},{1,9},{5... | collective-permute-start | bytes 3981320 | tf_op jit(solution)/shard_map/ppermute | solution.py:467
  483.7 31.6 %collective-permute-start.37 = (f32[2,144,1152]{2,1,0:T(8,128)}, f32[2,144,1152]{2,1,0:T(8,128)}, u32[]{:S(2)}, u32[]{:S(2)}) collective-permute-start(f32[2,144,1152]{2,1,0:T(8,128)} %get-tuple-element.435), channel_id=1, source_target_pairs={{0,16},{4,20},{8,24},{12,28},{16,0},{20,4},{24,8},{28,12},{1,17},{... | collective-permute-start | bytes 3981320 | tf_op jit(solution)/shard_map/ppermute | solution.py:471
  490.2 158.6 %reduce-scatter.7.cloned.1.call-start = ((), (), s32[]{:S(2)}) async-start(), calls=%async_computation.4 | async-start | bytes 3317760 | tf_op jit(solution)/shard_map/reduce_scatter | solution.py:657
  521.5 59.2 %collective-permute-start.40 = (f32[4,144,1152]{2,1,0:T(8,128)}, f32[4,144,1152]{2,1,0:T(8,128)}, u32[]{:S(2)}, u32[]{:S(2)}) collective-permute-start(f32[4,144,1152]{2,1,0:T(8,128)} %pad_maximum_fusion.4), channel_id=1, source_target_pairs={{0,8},{4,12},{8,0},{12,4},{16,24},{20,28},{24,16},{28,20},{1,9},{5... | collective-permute-start | bytes 7962632 | tf_op jit(solution)/shard_map/ppermute | solution.py:467
  523.0 58.9 %collective-permute-start.41 = (f32[4,144,1152]{2,1,0:T(8,128)}, f32[4,144,1152]{2,1,0:T(8,128)}, u32[]{:S(2)}, u32[]{:S(2)}) collective-permute-start(f32[4,144,1152]{2,1,0:T(8,128)} %pad_maximum_fusion.5), channel_id=1, source_target_pairs={{0,16},{4,20},{8,24},{12,28},{16,0},{20,4},{24,8},{28,12},{1,17},{... | collective-permute-start | bytes 7962632 | tf_op jit(solution)/shard_map/ppermute | solution.py:471
  545.7 90.6 %collective-permute-start.44 = (f32[16,72,1152]{2,1,0:T(8,128)}, f32[16,72,1152]{2,1,0:T(8,128)}, u32[]{:S(2)}, u32[]{:S(2)}) collective-permute-start(f32[16,72,1152]{2,1,0:T(8,128)} %dynamic-slice_bitcast_fusion.1), channel_id=1, source_target_pairs={{0,4},{4,0},{8,12},{12,8},{16,20},{20,16},{24,28},{28,24},{1,5},{5... | collective-permute-start | bytes 15925256 | tf_op jit(solution)/shard_map/ppermute | solution.py:463
  589.3 147.7 %reduce-scatter.11.cloned.1.call-start = ((), (), s32[]{:S(2)}) async-start(), calls=%async_computation.6 | async-start | bytes 3317760 | tf_op jit(solution)/shard_map/reduce_scatter | solution.py:657
  618.8 57.1 %collective-permute-start.49 = (f32[4,144,1152]{2,1,0:T(8,128)}, f32[4,144,1152]{2,1,0:T(8,128)}, u32[]{:S(2)}, u32[]{:S(2)}) collective-permute-start(f32[4,144,1152]{2,1,0:T(8,128)} %pad_maximum_fusion.6), channel_id=1, source_target_pairs={{0,8},{4,12},{8,0},{12,4},{16,24},{20,28},{24,16},{28,20},{1,9},{5... | collective-permute-start | bytes 7962632 | tf_op jit(solution)/shard_map/ppermute | solution.py:467
  619.6 56.8 %collective-permute-start.50 = (f32[4,144,1152]{2,1,0:T(8,128)}, f32[4,144,1152]{2,1,0:T(8,128)}, u32[]{:S(2)}, u32[]{:S(2)}) collective-permute-start(f32[4,144,1152]{2,1,0:T(8,128)} %pad_maximum_fusion.7), channel_id=1, source_target_pairs={{0,16},{4,20},{8,24},{12,28},{16,0},{20,4},{24,8},{28,12},{1,17},{... | collective-permute-start | bytes 7962632 | tf_op jit(solution)/shard_map/ppermute | solution.py:471
  681.6 121.9 %reduce-scatter.13.cloned.1.call-start = ((), (), s32[]{:S(2)}) async-start(), calls=%async_computation.13 | async-start | bytes 1658880
  727.7 48.1 %collective-permute-start.57 = (f32[516,576]{1,0:T(8,128)}, f32[516,576]{1,0:T(8,128)}, u32[]{:S(2)}, u32[]{:S(2)}) collective-permute-start(f32[516,576]{1,0:T(8,128)} %fusion.47), channel_id=1, source_target_pairs={{0,1},{1,2},{2,3},{3,0},{4,5},{5,6},{6,7},{7,4},{8,9},{9,10},{10,1... | collective-permute-start | bytes 3566600 | tf_op jit(solution)/shard_map/ppermute | solution.py:476
  730.2 57.9 %collective-permute-start.60 = (f32[144,1152]{1,0:T(8,128)}, f32[144,1152]{1,0:T(8,128)S(1)}, u32[]{:S(2)}, u32[]{:S(2)}) collective-permute-start(f32[144,1152]{1,0:T(8,128)} %bitcast.382), channel_id=1, source_target_pairs={{0,8},{4,12},{8,0},{12,4},{16,24},{20,28},{24,16},{28,20},{1,9},{5... | collective-permute-start | bytes 1990664 | tf_op jit(solution)/shard_map/ppermute | solution.py:467
  731.5 56.6 %collective-permute-start.61 = (f32[144,1152]{1,0:T(8,128)}, f32[144,1152]{1,0:T(8,128)}, u32[]{:S(2)}, u32[]{:S(2)}) collective-permute-start(f32[144,1152]{1,0:T(8,128)} %bitcast.383), channel_id=1, source_target_pairs={{0,16},{4,20},{8,24},{12,28},{16,0},{20,4},{24,8},{28,12},{1,17},{... | collective-permute-start | bytes 1990664 | tf_op jit(solution)/shard_map/ppermute | solution.py:471
  831.6 82.8 %collective-permute-start.76 = (f32[576,1152]{1,0:T(8,128)}, f32[576,1152]{1,0:T(8,128)}, u32[]{:S(2)}, u32[]{:S(2)}) collective-permute-start(f32[576,1152]{1,0:T(8,128)} %shard_map.521.refs_0_), channel_id=1, source_target_pairs={{0,4},{4,0},{8,12},{12,8},{16,20},{20,16},{24,28},{28,24},{1,5},{5... | collective-permute-start | bytes 7962632 | tf_op jit(solution)/shard_map/ppermute | solution.py:463
  835.5 83.1 %collective-permute-start.81 = (f32[576,1152]{1,0:T(8,128)}, f32[576,1152]{1,0:T(8,128)}, u32[]{:S(2)}, u32[]{:S(2)}) collective-permute-start(f32[576,1152]{1,0:T(8,128)} %shard_map.523.refs_0_), channel_id=1, source_target_pairs={{0,4},{4,0},{8,12},{12,8},{16,20},{20,16},{24,28},{28,24},{1,5},{5... | collective-permute-start | bytes 7962632 | tf_op jit(solution)/shard_map/ppermute | solution.py:463
  843.7 61.8 %collective-permute-start.63 = (f32[516,576]{1,0:T(8,128)}, f32[516,576]{1,0:T(8,128)}, u32[]{:S(2)}, u32[]{:S(2)}) collective-permute-start(f32[516,576]{1,0:T(8,128)} %fusion.46), channel_id=1, source_target_pairs={{0,2},{1,3},{2,0},{3,1},{4,6},{5,7},{6,4},{7,5},{8,10},{9,11},{10,... | collective-permute-start | bytes 3566600 | tf_op jit(solution)/shard_map/ppermute | solution.py:476
  851.7 76.7 %collective-permute-start.80 = (f32[288,1152]{1,0:T(8,128)}, f32[288,1152]{1,0:T(8,128)}, u32[]{:S(2)}, u32[]{:S(2)}) collective-permute-start(f32[288,1152]{1,0:T(8,128)} %shard_map.524.refs_0_), channel_id=1, source_target_pairs={{0,4},{4,0},{8,12},{12,8},{16,20},{20,16},{24,28},{28,24},{1,5},{5... | collective-permute-start | bytes 3981320 | tf_op jit(solution)/shard_map/ppermute | solution.py:463
  910.8 34.4 %collective-permute-start.75 = (f32[516,576]{1,0:T(8,128)}, f32[516,576]{1,0:T(8,128)}, u32[]{:S(2)}, u32[]{:S(2)}) collective-permute-start(f32[516,576]{1,0:T(8,128)} %fusion.45), channel_id=1, source_target_pairs={{0,3},{1,0},{2,1},{3,2},{4,7},{5,4},{6,5},{7,6},{8,11},{9,8},{10,9... | collective-permute-start | bytes 3566600 | tf_op jit(solution)/shard_map/ppermute | solution.py:476
  945.2 48.1 %collective-permute-start.84 = (f32[12672]{0:T(1024)}, f32[12672]{0:T(1024)S(1)}, u32[]{:S(2)}, u32[]{:S(2)}) collective-permute-start(f32[12672]{0:T(1024)} %add.606), channel_id=1, source_target_pairs={{0,3},{1,0},{2,1},{3,2},{4,7},{5,4},{6,5},{7,6},{8,11},{9,8},{10,9... | collective-permute-start | bytes 152072 | tf_op jit(solution)/shard_map/ppermute | solution.py:476
  948.9 44.4 %collective-permute-start.83 = (f32[12672]{0:T(1024)}, f32[12672]{0:T(1024)S(1)}, u32[]{:S(2)}, u32[]{:S(2)}) collective-permute-start(f32[12672]{0:T(1024)} %add.606), channel_id=1, source_target_pairs={{0,2},{1,3},{2,0},{3,1},{4,6},{5,7},{6,4},{7,5},{8,10},{9,11},{10,... | collective-permute-start | bytes 152072 | tf_op jit(solution)/shard_map/ppermute | solution.py:476
  948.9 43.4 %collective-permute-start.87 = (f32[6,2,1152]{2,1,0:T(2,128)S(1)}, f32[6,2,1152]{2,1,0:T(2,128)S(1)}, u32[]{:S(2)}, u32[]{:S(2)}) collective-permute-start(f32[6,2,1152]{2,1,0:T(2,128)S(1)} %pad_maximum_fusion.12), channel_id=1, source_target_pairs={{0,3},{1,0},{2,1},{3,2},{4,7},{5,4},{6,5},{7,6},{8,11},{9,8},{10,9... | collective-permute-start | bytes 165896 | tf_op jit(solution)/shard_map/ppermute | solution.py:476
  949.8 42.6 %collective-permute-start.86 = (f32[6,2,1152]{2,1,0:T(2,128)S(1)}, f32[6,2,1152]{2,1,0:T(2,128)S(1)}, u32[]{:S(2)}, u32[]{:S(2)}) collective-permute-start(f32[6,2,1152]{2,1,0:T(2,128)S(1)} %pad_maximum_fusion.12), channel_id=1, source_target_pairs={{0,2},{1,3},{2,0},{3,1},{4,6},{5,7},{6,4},{7,5},{8,10},{9,11},{10,... | collective-permute-start | bytes 165896 | tf_op jit(solution)/shard_map/ppermute | solution.py:476
  951.9 40.5 %collective-permute-start.85 = (f32[6,2,1152]{2,1,0:T(2,128)S(1)}, f32[6,2,1152]{2,1,0:T(2,128)S(1)}, u32[]{:S(2)}, u32[]{:S(2)}) collective-permute-start(f32[6,2,1152]{2,1,0:T(2,128)S(1)} %pad_maximum_fusion.12), channel_id=1, source_target_pairs={{0,1},{1,2},{2,3},{3,0},{4,5},{5,6},{6,7},{7,4},{8,9},{9,10},{10,1... | collective-permute-start | bytes 165896 | tf_op jit(solution)/shard_map/ppermute | solution.py:476
  (197 other events, 2692.6 us)
Sparse Core Ops, SparseCore 0:
  10.2 36.1 all-gather.12
  48.6 54.3 all-gather.14
  105.1 54.1 all-gather.16
  161.2 54.1 all-gather.18
  253.4 53.5 all-gather.20
  362.9 169.9 all-gather.22
  535.8 50.7 reduce-scatter.8
  589.5 52.3 reduce-scatter.6
  681.7 55.2 reduce-scatter.10
  739.7 45.2 reduce-scatter.12

commit v3 on v2

--- a/solution.py
+++ b/solution.py
@@ -764,6 +764,46 @@
     )(core[None], *grads, *given)
 
 
+def order_tokens(arrays, mp_index):
+    count = len(arrays)
+    tokens, width = arrays[0].shape[0], arrays[0].shape[1] // 2
+
+    def kernel(place_ref, *refs):
+        left_ref, right_ref, held, sems = refs[count:]
+
+        def copy(n, index):
+            return pltpu.make_async_copy(refs[n], held.at[index], sems.at[index])
+
+        for index in range(count):
+            for n in range(count):
+
+                @pl.when(lax.rem(place_ref[0] + count - index, count) == n)
+                def _():
+                    copy(n, index).start()
+
+        for index in range(count):
+            copy(0, index).wait()
+            rows = slice(index * tokens, (index + 1) * tokens)
+            left_ref[rows] = held[index, :, :width]
+            right_ref[rows] = held[index, :, width:]
+
+    vmem = pl.BlockSpec(memory_space=pltpu.VMEM)
+    shape = jax.ShapeDtypeStruct((count * tokens, width), jnp.float32)
+    return pl.pallas_call(
+        kernel,
+        in_specs=[pl.BlockSpec(memory_space=pltpu.SMEM)]
+        + [pl.BlockSpec(memory_space=pl.ANY)] * count,
+        out_specs=[vmem, vmem],
+        out_shape=[shape, shape],
+        scratch_shapes=[
+            pltpu.VMEM((count, tokens, 2 * width), jnp.float32),
+            pltpu.SemaphoreType.DMA((count,)),
+        ],
+        compiler_params=pltpu.CompilerParams(vmem_limit_bytes=40 * 1024 * 1024),
+        cost_estimate=small_cost,
+    )(mp_index[None], *arrays)
+
+
 def lanes_of(array):
     total = array[:, :128]
     for tile in range(1, array.shape[1] // 128):
@@ -779,7 +819,7 @@
     return jnp.broadcast_to(row, (128, row.shape[1])).T
 
 
-def scale_kernel(count, by_rows, place_ref, grad_ref, state_ref, *refs):
+def scale_kernel(count, by_rows, place_ref, grad_ref, state_ref, before_ref, *refs):
     sources = refs[:count]
     far_ref, scale_ref, near_ref, step_ref = refs[count:]
     rows = grad_ref.shape[1]
@@ -812,15 +852,15 @@
 
     @pl.when(lead == 0)
     def _():
-        step_ref[...] = jnp.zeros_like(step_ref)
+        step_ref[...] = before_ref[...]
 
     step_ref[...] += jnp.sum(step.reshape(rows // 8, 8, 128), 0)
 
 
-def scales(grad, far_state, sources, mp_index, by_rows):
+def scales(grad, far_state, before, sources, first, mp_index, by_rows):
     leading, rows, _ = grad.shape
     count = len(sources)
-    small = pl.BlockSpec((1, 2, D), lambda i: (i, 0, 0))
+    small = pl.BlockSpec((1, 2, D), lambda i: (i + first, 0, 0))
     line = pl.BlockSpec((1, 1, D), lambda i: (i, 0, 0))
     return pl.pallas_call(
         functools.partial(scale_kernel, count, by_rows),
@@ -829,6 +869,7 @@
             pl.BlockSpec(memory_space=pltpu.SMEM),
             pl.BlockSpec((1, rows, D), lambda i: (i, 0, 0)),
             line,
+            pl.BlockSpec((8, 128), lambda i: (0, 0)),
         ]
         + [small] * count,
         out_specs=[
@@ -845,17 +886,26 @@
         ],
         compiler_params=pltpu.CompilerParams(vmem_limit_bytes=40 * 1024 * 1024),
         cost_estimate=small_cost,
-    )(mp_index[None], grad, far_state.reshape(leading, 1, D), *sources)
-
-
-def renew_kernel(turned, factor_ref, weight_ref, grad_ref, far_ref, near_ref, new_ref, low_ref):
-    step = grad_ref[0] * far_ref[0] * (near_ref[0][:, :1] * factor_ref[0])
+    )(mp_index[None], grad, far_state.reshape(leading, 1, D), before, *sources)
+
+
+param_count = 6.0 * D * D + 2.0 * D * FF + 7.0 * D + FF
+
+
+def renew_kernel(turned, count, rate_ref, weight_ref, grad_ref, far_ref, near_ref, *refs):
+    new_ref, low_ref = refs[count:]
+    total = refs[0][...]
+    for ref in refs[1:count]:
+        total = total + ref[...]
+    total = jnp.sum(jnp.sum(total, 0, keepdims=True), 1, keepdims=True) + rate_ref[1]
+    divisor = jnp.maximum(1.0, jnp.sqrt(total / param_count) / clip_level)
+    step = grad_ref[0] * far_ref[0] * (near_ref[0][:, :1] * (rate_ref[0] / divisor))
     new = weight_ref[0] - (step.T if turned else step)
     new_ref[0] = new
     low_ref[0] = new.astype(jnp.bfloat16)
 
 
-def renew(weight, grad, far_scale, near_scale, factor, turned, first=0):
+def renew(weight, grad, far_scale, near_scale, rate, steps, turned, first=0):
     leading, rows = weight.shape[0], grad.shape[1]
     if turned:
         width = 384
@@ -872,9 +922,10 @@
         far_spec = pl.BlockSpec((1, 1, D), lambda i, j: (i + first, 0, 0))
         near_spec = pl.BlockSpec((1, height, 128), lambda i, j: (i + first, j, 0))
     return pl.pallas_call(
-        functools.partial(renew_kernel, turned),
+        functools.partial(renew_kernel, turned, len(steps)),
         grid=grid,
-        in_specs=[pl.BlockSpec(memory_space=pltpu.SMEM), weight_spec, grad_spec, far_spec, near_spec],
+        in_specs=[pl.BlockSpec(memory_space=pltpu.SMEM), weight_spec, grad_spec, far_spec, near_spec]
+        + [pl.BlockSpec((8, 128), lambda i, j: (0, 0))] * len(steps),
         out_specs=[weight_spec, weight_spec],
         out_shape=[
             jax.ShapeDtypeStruct(weight.shape, jnp.float32),
@@ -882,7 +933,7 @@
         ],
         compiler_params=pltpu.CompilerParams(vmem_limit_bytes=40 * 1024 * 1024),
         cost_estimate=small_cost,
-    )(factor[None], weight, grad, far_scale, near_scale)
+    )(rate, weight, grad, far_scale, near_scale, *steps)
 
 
 def head_windows():
@@ -1025,6 +1076,7 @@
     skip_shard = skip_weight.reshape(-1, D)
     skip_whole = bring(order, skip_shard, quarter, core)
     hidden_all = gather_deep(hidden_bias)
+    hidden_state = gather_deep(hidden_moments).reshape(-1)
 
     angles = (timesteps.astype(jnp.float32) + 0.5) * (0.5 * math.pi / total_steps)
     alpha_sq = jnp.square(jnp.cos(angles))
@@ -1109,6 +1161,13 @@
     upstream = upstream * batch_scale
     upstream_low = jnp.concatenate([upstream, upstream_other], 0).astype(jnp.bfloat16)
     upstream_low = order.mark(upstream_low)
+    weight_sq = jnp.stack(
+        [
+            jnp.sum(array * array)
+            for array in (skip_weight, qkv_weight, proj_weight, fc1_weight, fc2_weight, hidden_bias)
+        ]
+    )
+    weight_sq = order.mark(weight_sq)
     fc1_own = others(order.mark(fc1_whole))
     fc1_x, fc1_y = swap_plane(order, fc1_own, fc1_own)
     attn_one, attn_two = order.mark(attn_one, attn_two)
@@ -1221,13 +1280,14 @@
     qkv_grad = jnp.einsum(
         "te,td->ed", order.after(qkv_grad_low), normed_low, preferred_element_type=jnp.float32
     ).reshape(3 * mp_count, 2, hidden_slice, D)
+    qkv_grad = order.mark(qkv_grad)
+    fc1_add = order.mark(*fc1_add)
+    fc1_sides = swap_plane(order, *order.mark(*cut_sides(fc1_grad, quarter, *fc1_add)))
     proj_grad = jnp.einsum(
         "te,td->ed", attended, order.after(residual_low), preferred_element_type=jnp.float32
     ).reshape(mp_count, 2, hidden_slice, D)
     attn_given = order.mark(pick(qkv_grad, 1 - core, 1), pick(proj_grad, 1 - core, 1))
     attn_given = [to_core(array) for array in attn_given]
-    fc1_add = order.mark(*fc1_add)
-    fc1_sides = swap_plane(order, *order.mark(*cut_sides(fc1_grad, quarter, *fc1_add)))
     norm_one_in = matmul(order.after(qkv_grad_low), qkv_low)
     back_one, gain_one_grad, bias_one_grad = norm_backward(
         norm_one_in, normal_one, inverse_one, vectors[0]
@@ -1248,12 +1308,15 @@
     fc1_sides = order.mark(*fc1_sides)
     fc1_piece = sum_deep(order, fc1_grad, quarter, *fc1_sides)
     skip_shards = skip_low.reshape(4, mp_count, -1, D)
-    both_grads = []
-    for shift in (1, 2, 3, 0):
+
+    def input_product(shift):
         shard_low = pick(skip_shards, lax.rem(mp_index + shift, mp_count), 1).reshape(-1, D)
-        both = jnp.einsum("td,cd->tc", joined_low, shard_low, preferred_element_type=jnp.float32)
-        both = order.mark(both)
-        both_grads.append(both)
+        return order.mark(
+            jnp.einsum("td,cd->tc", joined_low, shard_low, preferred_element_type=jnp.float32)
+        )
+
+    turn_two = turn_mp(input_product(2), 2)
+    turn_one, stay, turn_three = input_product(1), input_product(0), input_product(3)
     attn_add = order.mark(*attn_add)
     attn_sides = swap_plane(order, *order.mark(*cut_sides(attn_grad, quarter, *attn_add)))
     skip_given = order.mark(skip_given)
@@ -1275,16 +1338,9 @@
     hidden_grad = hidden_grad.reshape(4, mp_count, 1, hidden_slice).transpose(1, 0, 2, 3)
     hidden_grad = jnp.where(jnp.arange(2)[None, None, :, None] == core, hidden_grad, 0.0)
     small = order.mark(jnp.concatenate([vector_grad.reshape(-1), hidden_grad.reshape(-1)]))
-    weight_sq = jnp.stack(
-        [
-            jnp.sum(array * array)
-            for array in (skip_weight, qkv_weight, proj_weight, fc1_weight, fc2_weight, hidden_bias)
-        ]
-    )
     small_core = to_core(small)
-    weight_sq = order.mark(weight_sq)
     fc1_piece = order.mark(fc1_piece)
-    both_grads[0] = turn_mp(order.after(both_grads[0]), 1)
+    turn_two = order.mark(turn_two)
     attn_sides = order.mark(*attn_sides)
     attn_piece = sum_deep(order, attn_grad, quarter, *attn_sides)
     skip_add = order.mark(*skip_add)
@@ -1336,42 +1392,48 @@
         return [array] + [turn_mp(array, shift) for shift in range(1, mp_count)]
 
     fc2_near, fc1_near = spread(fc2_piece), spread(fc1_piece)
-    attn_piece = order.mark(attn_piece)
+    block_output = (block_all + vectors[6]).astype(jnp.bfloat16).reshape(-1, D)
+    block_output = order.mark(block_output)
     fc2_near = order.mark(*fc2_near)
-    both_grads[0] = order.mark(both_grads[0])
     fc2_far = spread_far(fc2_near)
     small = order.mark(small + order.mark(small_y))
     fc1_near = order.mark(*fc1_near)
     fc1_far = spread_far(fc1_near)
     fc2_far = order.mark(*fc2_far)
+    attn_piece = order.mark(attn_piece)
     attn_near = spread(attn_piece)
     fc2_held = order.mark(hold(fc2_piece, fc2_near, fc2_far))
+    fc2_other = to_core(fc2_held)
+    fc1_far = order.mark(*fc1_far)
     skip_piece = order.mark(skip_piece)
-    both_grads[1] = turn_mp(order.after(both_grads[1]), 2)
-    fc1_far = order.mark(*fc1_far)
     skip_near = spread(skip_piece)
+    turn_one = turn_mp(order.after(turn_one), 1)
     fc1_held = order.mark(hold(fc1_piece, fc1_near, fc1_far))
     attn_near = order.mark(*attn_near)
-    fc2_other = to_core(order.after(fc2_held))
     attn_far = spread_far(attn_near)
+    fc1_other = to_core(order.after(fc1_held))
     skip_near = order.mark(*skip_near)
     skip_far = spread_far(skip_near)
+    small = jnp.concatenate(
+        [small, weight_sq, jnp.zeros((D - 6,), jnp.float32)], 0
+    ).reshape(6, 2, D)
     fc2_sum, fc2_moments = order.mark(
         *interleave(fc2_held, order.mark(fc2_other), own_state(fc2_rows)[None])
     )
-    fc1_other = to_core(order.after(fc1_held))
     attn_far = order.mark(*attn_far)
     attn_held = order.mark(hold(attn_piece, attn_near, attn_far))
     attn_other = to_core(attn_held)
+    turn_one = order.mark(turn_one)
+    turn_three = turn_mp(order.after(turn_three), 3)
     skip_far = order.mark(*skip_far)
     skip_held = order.mark(hold(skip_piece, skip_near, skip_far))
     skip_other = to_core(skip_held)
-    both_grads[1] = order.mark(both_grads[1])
-    both_grads[2] = turn_mp(order.after(both_grads[2]), 3)
     fc1_sum, fc1_moments = order.mark(
         *interleave(fc1_held, order.mark(fc1_other), own_state(fc1_cols)[None])
     )
-    hidden_sent = everywhere(order.mark(jnp.concatenate([fc2_moments, fc1_moments], 0)))
+    hidden_sent = jnp.concatenate([fc2_moments, fc1_moments, small], 0)
+    turn_three = order.mark(turn_three)
+    hidden_sent = everywhere(order.mark(hidden_sent))
     attn_state = jnp.concatenate([own_state(qkv_cols), own_state(proj_rows)[None]], 0)
     attn_sum, attn_moments = order.mark(
         *interleave(attn_held, order.mark(attn_other), attn_state)
@@ -1380,82 +1442,77 @@
         *interleave(skip_held, order.mark(skip_other), own_state(skip_rows))
     )
     hidden_sent = order.mark(*hidden_sent)
-    both_grads[2] = order.mark(both_grads[2])
     token_sent = everywhere(order.mark(jnp.concatenate([attn_moments, skip_moments], 0)))
-    small_all = everywhere(order.after(small))
-    fc2_sent = [array[:1] for array in hidden_sent]
-    fc1_sent = [array[1:] for array in hidden_sent]
-    fc2_far_new, *fc2_scales, fc2_step = order.mark(
-        *scales(fc2_sum, fc2_cols[None], fc2_sent, mp_index, (True,))
-    )
-    fc1_far_new, *fc1_scales, fc1_step = order.mark(
-        *scales(fc1_sum, fc1_rows[None], fc1_sent, mp_index, (False,))
+    input_grad, skip_input_grad = order.mark(
+        *order_tokens([stay, turn_one, turn_two, turn_three], mp_index)
+    )
+    step = jnp.zeros((8, 128), jnp.float32)
+    fc2_far_new, *fc2_scales, step = order.mark(
+        *scales(fc2_sum, fc2_cols[None], step, hidden_sent, 0, mp_index, (True,))
+    )
+    fc1_far_new, *fc1_scales, step = order.mark(
+        *scales(fc1_sum, fc1_rows[None], step, hidden_sent, 1, mp_index, (False,))
     )
     token_sent = order.mark(*token_sent)
-    small = jnp.sum(in_turn(order.mark(*small_all)), 0)
-    attn_sent = [array[:4] for array in token_sent]
-    skip_sent = [array[4:] for array in token_sent]
     attn_state = jnp.concatenate([qkv_rows, proj_cols[None]], 0)
-    attn_far_new, *attn_scales, attn_step = order.mark(
-        *scales(attn_sum, attn_state, attn_sent, mp_index, (False, False, False, True))
-    )
-    skip_far_new, *skip_scales, skip_step = order.mark(
-        *scales(skip_sum, skip_cols, skip_sent, mp_index, (True, True))
-    )
-
+    attn_far_new, *attn_scales, step = order.mark(
+        *scales(attn_sum, attn_state, step, token_sent, 0, mp_index, (False, False, False, True))
+    )
+    skip_far_new, *skip_scales, step = order.mark(
+        *scales(skip_sum, skip_cols, step, token_sent, 4, mp_index, (True, True))
+    )
+    steps = everywhere(step)
+    small = jnp.sum(in_turn([array[2:] for array in hidden_sent]), 0).reshape(-1)
     vector_sum = small[: 7 * D].reshape(7, D)
-    hidden_sum = lax.dynamic_slice_in_dim(small[7 * D :], mp_index * hidden_local, hidden_local, 0)
+    hidden_whole = small[7 * D : 7 * D + mp_count * hidden_local]
+    weight_sq = small[11 * D : 11 * D + 6]
     vector_new = 0.5 * vector_moments + 0.5 * (vector_sum * vector_sum + moment_eps)
     vector_update = vector_sum * lax.rsqrt(vector_new)
-    hidden_new = 0.5 * hidden_moments + 0.5 * (hidden_sum * hidden_sum + moment_eps)
-    hidden_update = hidden_sum * lax.rsqrt(hidden_new)
-    step_sq = jnp.sum(hidden_update * hidden_update)
-    step_sq = step_sq + jnp.sum(skip_step + attn_step + fc1_step + fc2_step)
-    sent = jnp.concatenate([step_sq[None], weight_sq, jnp.zeros((121,), jnp.float32)])
-    sent = everywhere(order.mark(sent))
-    input_grads = in_turn([both_grads[3]] + both_grads[:3])
-    input_grad = input_grads[:, :, :width_local].reshape(-1, width_local)
-    skip_input_grad = input_grads[:, :, width_local:].reshape(-1, width_local)
-    input_grad, skip_input_grad = order.mark(input_grad, skip_input_grad)
-    sent = jnp.sum(in_turn(order.mark(*sent)), 0)
-    weight_sq = sent[1:]
-    step_total = sent[0] + jnp.sum(vector_update * vector_update)
-    param_count = 6.0 * D * D + 2.0 * D * FF + 7.0 * D + FF
+    hidden_new = 0.5 * hidden_state + 0.5 * (hidden_whole * hidden_whole + moment_eps)
+    hidden_update = hidden_whole * lax.rsqrt(hidden_new)
+    vector_step = jnp.sum(vector_update * vector_update) + jnp.sum(hidden_update * hidden_update)
+
+    def own_hidden(array):
+        return lax.dynamic_slice_in_dim(array, mp_index * hidden_local, hidden_local, 0)
+
+    hidden_sum, hidden_new = own_hidden(hidden_whole), own_hidden(hidden_new)
+    hidden_update = own_hidden(hidden_update)
+    tensor_sizes = (2.0 * D * D, 3.0 * D * D, 1.0 * D * D, 1.0 * D * FF, 1.0 * FF * D, 1.0 * FF)
+    weight_rms = jnp.sqrt(weight_sq / jnp.array(tensor_sizes, jnp.float32))
+    rates = step_rate * jnp.maximum(0.001, weight_rms)
+    pairs = jnp.stack([rates, jnp.broadcast_to(vector_step, (6,))], 1)
+    pairs = order.mark(pairs)
+    steps = order.mark(*steps)
+
+    qkv_turned = qkv_weight.transpose(0, 2, 1)
+    skip_new, skip_new_low = renew(skip_weight, skip_sum, *skip_scales, pairs[0], steps, False)
+    qkv_new, qkv_new_low = renew(qkv_turned, attn_sum, *attn_scales, pairs[1], steps, False)
+    qkv_new, qkv_new_low = qkv_new.transpose(0, 2, 1), qkv_new_low.transpose(0, 2, 1)
+    proj_new, proj_new_low = renew(
+        proj_weight[None], attn_sum, *attn_scales, pairs[2], steps, False, first=3
+    )
+    fc1_new, fc1_new_low = renew(fc1_weight[None], fc1_sum, *fc1_scales, pairs[3], steps, True)
+    fc2_new, fc2_new_low = renew(fc2_weight[None], fc2_sum, *fc2_scales, pairs[4], steps, False)
+    step_total = jnp.sum(jnp.sum(in_turn(steps), 0)) + vector_step
     update_rms = jnp.sqrt(step_total / param_count)
     divisor = jnp.maximum(1.0, update_rms / clip_level)
-    tensor_sizes = (2.0 * D * D, 3.0 * D * D, 1.0 * D * D, 1.0 * D * FF, 1.0 * FF * D, 1.0 * FF)
-
-    def factor_of(position):
-        weight_rms = jnp.sqrt(weight_sq[position] / tensor_sizes[position])
-        return step_rate * jnp.maximum(0.001, weight_rms) / divisor
-
-    skip_new, skip_new_low = renew(skip_weight, skip_sum, *skip_scales, factor_of(0), False)
-    qkv_turned = qkv_weight.transpose(0, 2, 1)
-    qkv_new, qkv_new_low = renew(qkv_turned, attn_sum, *attn_scales, factor_of(1), False)
-    qkv_new, qkv_new_low = qkv_new.transpose(0, 2, 1), qkv_new_low.transpose(0, 2, 1)
-    proj_new, proj_new_low = renew(
-        proj_weight[None], attn_sum, *attn_scales, factor_of(2), False, first=3
-    )
-    fc1_new, fc1_new_low = renew(fc1_weight[None], fc1_sum, *fc1_scales, factor_of(3), True)
-    fc2_new, fc2_new_low = renew(fc2_weight[None], fc2_sum, *fc2_scales, factor_of(4), False)
-    block_output = (block_all + vectors[6]).astype(jnp.bfloat16).reshape(-1, D)
     vector_rms = jnp.sqrt(jnp.mean(vectors * vectors, 1, keepdims=True))
     vectors_new = vectors - step_rate * jnp.maximum(0.001, vector_rms) * vector_update / divisor
-    hidden_bias_new = hidden_bias - factor_of(5) * hidden_update
+    hidden_bias_new = hidden_bias - rates[5] / divisor * hidden_update
     piece_width = D // dp_count
     dp_start = dp_index * piece_width
 
     def own_piece(array, axis):
         return lax.dynamic_slice_in_dim(array, dp_start, piece_width, axis)
 
-    def near_whole(sent, width):
-        near = in_turn([array[:, 1, :width] for array in sent])
+    def near_whole(sent, first, amount, width):
+        near = in_turn([array[first : first + amount, 1, :width] for array in sent])
         return near.transpose(1, 0, 2).reshape(near.shape[1], -1)
 
-    skip_near_new = near_whole(skip_sent, width_local)
-    attn_near_new = near_whole(attn_sent, width_local)
-    fc1_near_new = near_whole(fc1_sent, hidden_local)
-    fc2_near_new = near_whole(fc2_sent, hidden_local)
+    skip_near_new = near_whole(token_sent, 4, 2, width_local)
+    attn_near_new = near_whole(token_sent, 0, 4, width_local)
+    fc1_near_new = near_whole(hidden_sent, 1, 1, hidden_local)
+    fc2_near_new = near_whole(hidden_sent, 0, 1, hidden_local)
     return (
         block_output,
         input_grad,

time: 1080 us -> 1040 us (0.963)
  local copies, waits for them, and re-layouts: 235 us -> 210 us
    reduce_scatter x3, waiting for transfers between devices: 4.9 us -> 55.7 us  [sum_deep(): return lax.psum_scatter(own, 'mp', scatter_dimension=0, tiled=False)]
    ppermute x25, waiting for transfers between devices: 227 us -> 190 us  [to_x(): return lax.ppermute(array, 'dp', [(i, i ^ 2) for i in range(8)])]
    ppermute x18, waiting for transfers between devices: 77.8 us -> 51 us  [turn_mp(): lax.ppermute(array, 'mp', [(i, (i + shift) % count) for i in range(count)])]
    reshape x4 -> x3, local copies, waits for them, and re-layouts: 13.6 us -> 0.09 us  [the longest x1 0.05 us: body_data(): jnp.sum(in_turn([array[2:] for array in hidden_sent]), 0).reshape(-1)]
    unnamed x310 -> x321, local copies, waits for them, and re-layouts: 100 us -> 100 us
  transfers between devices with their start and end apart: 101 -> 101, of which waited for: 45 -> 40; matrix products, arithmetic and copies ran while one was open for 33% -> 33% of each run, Pallas kernels for 10% -> 10%
where the time goes in v3:
time: 1040 us
  waiting for transfers between devices  353 us (34%)
  local copies, waits for them, and re-layouts  210 us (20%)
  Pallas kernels  132 us (13%)
  other arithmetic  121 us (12%)
  matrix products  113 us (11%)
  starting transfers between devices  85.9 us (8%)
  between operations  21.3 us (2%)
    ppermute x25, waiting for transfers between devices, to_x(): return lax.ppermute(array, 'dp', [(i, i ^ 2) for i in range(8)])  190 us
    unnamed x321, local copies, waits for them, and re-layouts  100 us
    reduce_scatter x3, waiting for transfers between devices, sum_deep(): return lax.psum_scatter(own, 'mp', scatter_dimension=0, tiled=False)  55.7 us
    ppermute x18, waiting for transfers between devices, turn_mp(): lax.ppermute(array, 'mp', [(i, (i + shift) % count) for i in range(count)])  51 us
    ppermute x25, waiting for transfers between devices, to_y(): return lax.ppermute(array, 'dp', [(i, i ^ 4) for i in range(8)])  40.9 us
    dot_general x5, matrix products, matmul(): return jnp.dot(left_side, right_side, preferred_element_type=jnp.float32)  35.9 us
    ppermute x25, starting transfers between devices, to_y(): return lax.ppermute(array, 'dp', [(i, i ^ 4) for i in range(8)])  31.2 us
    pallas_call x4, Pallas kernels, assemble(): pl.pallas_call(kernel, in_specs=[pl.BlockSpec(memory_space=pltpu.SMEM)] +...  30 us
  transfers between devices with their start and end apart: 101, of which 40 were waited for; matrix products, arithmetic and copies ran while one was open for 33% of the time, Pallas kernels for 10%

profile of v3, /device:TPU:0, one launch (start us, length us, event | category | flops | bytes accessed | tf_op | source)
XLA Modules:
  0.0 1036.2 jit_solution(4643503388655432840)
XLA Ops:
  34.8 6.9 copy.138
  57.9 16.4 %collective-permute-done.4.refs_3_ = f32[3,72,1152]{2,1,0:T(8,128)} collective-permute-done((f32[3,72,1152]{2,1,0:T(8,128)}, f32[3,72,1152]{2,1,0:T(8,128)}, u32[]{:S(2)}, u32[]{:S(2)}) %collective-permute-start.4) | collective-permute-done | bytes 995360 | tf_op jit(solution)/shard_map/ppermute | solution.py:467
  79.7 5.8 collective-permute-done.12.refs_9_
  85.5 5.4 collective-permute-done.11.refs_7_
  94.7 8.9 all-gather.15.cloned.1.call-done
  109.6 6.5 shard_map.521
  145.8 6.3 collective-permute-done.16.refs_3_
  164.9 13.3 %collective-permute-done.20.refs_7_ = f32[1,144,1152]{2,1,0:T(8,128)} collective-permute-done((f32[1,144,1152]{2,1,0:T(8,128)S(1)}, f32[1,144,1152]{2,1,0:T(8,128)}, u32[]{:S(2)}, u32[]{:S(2)}) %collective-permute-start.20) | collective-permute-done | bytes 663584 | tf_op jit(solution)/shard_map/ppermute | solution.py:467
  178.2 8.4 collective-permute-done.21.refs_9_
  196.5 10.5 %shard_map.522 = (bf16[12,288,1152]{2,1,0:T(8,128)(2,1)}, bf16[4,288,1152]{2,1,0:T(8,128)(2,1)S(1)}) custom-call(s32[17]{0:T(128)S(1)} %stack.384.table_ref, f32[4,288,1152]{2,1,0:T(8,128)} %bitcast.394, f32[3,144,1152]{2,1,0:T(8,128)} %fusion.7.refs_1_, f32[3,144,1152]{2,1,0:T(8,128)} %collective-permute-done.15.refs_2_, ...), custom_call_target="tpu_custom_call" | custom-call | bytes 1024 | tf_op jit(solution)/shard_map/pallas_call | solution.py:553
  208.5 8.6 convolution_convert_fusion.qkv_ref
  217.0 9.2 shard_map.523
  229.4 6.2 fusion
  260.7 6.0 collective-permute-done.29.refs_5_
  266.7 13.7 %collective-permute-done.28.refs_4_ = f32[2,144,1152]{2,1,0:T(8,128)} collective-permute-done((f32[2,144,1152]{2,1,0:T(8,128)}, f32[2,144,1152]{2,1,0:T(8,128)}, u32[]{:S(2)}, u32[]{:S(2)}) %collective-permute-start.28) | collective-permute-done | bytes 1327136 | tf_op jit(solution)/shard_map/ppermute | solution.py:467
  280.4 6.2 shard_map.524
  290.9 9.4 multiply_convert_fusion
  300.3 8.0 fusion.35
  314.0 8.6 collective-permute-done.30.refs_2_
  330.5 6.8 shard_map.525
  337.3 8.5 fusion.36
  348.2 13.3 %fusion.31 = (f32[2304]{0:T(1024)S(1)}, bf16[1032,2304]{1,0:T(8,128)(2,1)}) fusion(f32[1032,2304]{1,0:T(8,128)S(1)} %bitcast.441, bf16[1032,1152]{1,0:T(8,128)(2,1)S(1)} %copy-done.82, bf16[2304,1152]{1,0:T(8,128)(2,1)S(1)} %bitcast.376), kind=kOutput, calls=%fused_computation.237 | convolution fusion | flops 5511571456 | bytes 21961728 | tf_op jit(solution)/shard_map/td,fd->tf/dot_general | solution.py:1243
  363.7 13.4 %collective-permute-done.33 = f32[2,144,1152]{2,1,0:T(8,128)} collective-permute-done((f32[2,144,1152]{2,1,0:T(8,128)}, f32[2,144,1152]{2,1,0:T(8,128)}, u32[]{:S(2)}, u32[]{:S(2)}) %collective-permute-start.33) | collective-permute-done | bytes 1327136 | tf_op jit(solution)/shard_map/ppermute | solution.py:467
  384.0 9.0 fusion.37
  396.3 7.9 fusion.38
  425.7 16.9 %shard_map.526 = bf16[2,258,3456]{2,1,0:T(8,128)(2,1)S(1)} custom-call(bf16[2,258,3456]{2,1,0:T(8,128)(2,1)S(1)} %copy-done.15, bf16[2,258,1152]{2,1,0:T(8,128)(2,1)S(1)} %reshape.350.grad_ref), custom_call_target="tpu_custom_call" | custom-call | bytes 1024 | tf_op jit(solution)/shard_map/pallas_call | solution.py:1020
  455.5 5.3 fusion.3
  460.8 9.0 fusion.39
  469.8 12.2 %collective-permute-done.38 = f32[2,144,1152]{2,1,0:T(8,128)} collective-permute-done((f32[2,144,1152]{2,1,0:T(8,128)}, f32[2,144,1152]{2,1,0:T(8,128)}, u32[]{:S(2)}, u32[]{:S(2)}) %collective-permute-start.38) | collective-permute-done | bytes 1327136 | tf_op jit(solution)/shard_map/ppermute | solution.py:467
  500.9 5.2 constant_dynamic-slice_fusion.10
  508.2 8.7 multiply_reduce_fusion.5
  536.3 14.4 %shard_map.527 = f32[16,144,1152]{2,1,0:T(8,128)} custom-call(s32[1]{0:T(128)} %bitcast.26.core_ref, f32[12,2,144,1152]{3,2,1,0:T(8,128)} %bitcast.392, f32[4,2,144,1152]{3,2,1,0:T(8,128)S(1)} %copy-done.22, f32[12,144,1152]{2,1,0:T(8,128)} %collective-permute-done.41.refs_2_, f32[4,144,1152]{2,1,0:T(8,128)S(1)} %collective-permute-done.42.refs_3_), custom_call_target="tpu_custom_call" | custom-call | bytes 1024 | tf_op jit(solution)/shard_map/pallas_call | solution.py:753
  555.1 11.3 %collective-permute-done.45 = f32[4,144,1152]{2,1,0:T(8,128)} collective-permute-done((f32[4,144,1152]{2,1,0:T(8,128)}, f32[4,144,1152]{2,1,0:T(8,128)}, u32[]{:S(2)}, u32[]{:S(2)}) %collective-permute-start.45) | collective-permute-done | bytes 2654240 | tf_op jit(solution)/shard_map/ppermute | solution.py:467
  569.6 5.2 fusion.2
  586.3 11.2 %collective-permute-done.43 = f32[2,144,1152]{2,1,0:T(8,128)} collective-permute-done((f32[2,144,1152]{2,1,0:T(8,128)}, f32[2,144,1152]{2,1,0:T(8,128)}, u32[]{:S(2)}, u32[]{:S(2)}) %collective-permute-start.43) | collective-permute-done | bytes 1327136 | tf_op jit(solution)/shard_map/ppermute | solution.py:467
  610.6 9.5 shard_map.528
  622.7 55.7 %reduce-scatter.7.cloned.1.call-done = f32[1,144,1152]{2,1,0:T(8,128)} async-done(((f32[4,144,1152]{2,1,0:T(8,128)}), f32[1,144,1152]{2,1,0:T(8,128)}) %reduce-scatter.7.cloned.1.call-update) | async-done | bytes 663568 | tf_op jit(solution)/shard_map/reduce_scatter | solution.py:657
  678.4 20.3 %collective-permute-done.51.refs_2_ = f32[516,576]{1,0:T(8,128)S(1)} collective-permute-done((f32[516,576]{1,0:T(8,128)}, f32[516,576]{1,0:T(8,128)S(1)}, u32[]{:S(2)}, u32[]{:S(2)}) %collective-permute-start.51) | collective-permute-done | bytes 1188896 | tf_op jit(solution)/shard_map/ppermute | solution.py:476
  698.7 5.7 fusion.1
  708.5 13.6 %collective-permute-done.47 = f32[2,72,1152]{2,1,0:T(8,128)S(1)} collective-permute-done((f32[2,72,1152]{2,1,0:T(8,128)S(1)}, f32[2,72,1152]{2,1,0:T(8,128)S(1)}, u32[]{:S(2)}, u32[]{:S(2)}) %collective-permute-start.47) | collective-permute-done | bytes 663584 | tf_op jit(solution)/shard_map/ppermute | solution.py:467
  730.1 25.2 %collective-permute-done.52 = f32[4,72,1152]{2,1,0:T(8,128)S(1)} collective-permute-done((f32[4,72,1152]{2,1,0:T(8,128)S(1)}, f32[4,72,1152]{2,1,0:T(8,128)S(1)}, u32[]{:S(2)}, u32[]{:S(2)}) %collective-permute-start.52) | collective-permute-done | bytes 1327136 | tf_op jit(solution)/shard_map/ppermute | solution.py:467
  762.8 7.0 add_convert_fusion
  774.3 13.4 %collective-permute-done.59.refs_1_ = f32[144,1152]{1,0:T(8,128)S(1)} collective-permute-done((f32[144,1152]{1,0:T(8,128)S(1)}, f32[144,1152]{1,0:T(8,128)S(1)}, u32[]{:S(2)}, u32[]{:S(2)}) %collective-permute-start.59) | collective-permute-done | bytes 663584 | tf_op jit(solution)/shard_map/ppermute | solution.py:467
  793.7 5.9 collective-permute-done.58
  807.9 20.4 %collective-permute-done.61.refs_3_ = f32[72,1152]{1,0:T(8,128)S(1)} collective-permute-done((f32[72,1152]{1,0:T(8,128)S(1)}, f32[72,1152]{1,0:T(8,128)S(1)}, u32[]{:S(2)}, u32[]{:S(2)}) %collective-permute-start.61) | collective-permute-done | bytes 331808 | tf_op jit(solution)/shard_map/ppermute | solution.py:467
  864.0 16.4 %collective-permute-done.65.refs_1_ = f32[516,576]{1,0:T(8,128)} collective-permute-done((f32[516,576]{1,0:T(8,128)}, f32[516,576]{1,0:T(8,128)}, u32[]{:S(2)}, u32[]{:S(2)}) %collective-permute-start.65) | collective-permute-done | bytes 1188896 | tf_op jit(solution)/shard_map/ppermute | solution.py:476
  897.2 13.2 %collective-permute-done.73.refs_3_ = f32[516,576]{1,0:T(8,128)} collective-permute-done((f32[516,576]{1,0:T(8,128)}, f32[516,576]{1,0:T(8,128)}, u32[]{:S(2)}, u32[]{:S(2)}) %collective-permute-start.73) | collective-permute-done | bytes 1188896 | tf_op jit(solution)/shard_map/ppermute | solution.py:476
  1022.8 5.3 shard_map.545
  (762 shorter events, 480.7 us)
Async XLA Ops:
  7.2 42.1 %all-gather.13.cloned.1.call-start = ((), (), s32[]{:S(2)}) async-start(), calls=%async_computation.7 | async-start | bytes 1658880 | tf_op jit(solution)/shard_map/all_gather | solution.py:608
  9.1 94.5 %all-gather.15.cloned.1.call-start = ((), (), s32[]{:S(2)}) async-start(), calls=%async_computation.8 | async-start | bytes 3317760 | tf_op jit(solution)/shard_map/all_gather | solution.py:608
  15.3 149.6 %all-gather.17.cloned.1.call-start = ((), (), s32[]{:S(2)}) async-start(), calls=%async_computation.9 | async-start | bytes 3317760 | tf_op jit(solution)/shard_map/all_gather | solution.py:608
  17.4 31.8 %collective-permute-start.86 = (f32[1152]{0:T(1024)S(1)}, f32[1152]{0:T(1024)S(1)}, u32[]{:S(2)}, u32[]{:S(2)}) collective-permute-start(f32[1152]{0:T(1024)S(1)} %copy-done.117), channel_id=1, source_target_pairs={{0,2},{1,3},{2,0},{3,1},{4,6},{5,7},{6,4},{7,5},{8,10},{9,11},{10,... | collective-permute-start | bytes 13832 | tf_op jit(solution)/shard_map/ppermute | solution.py:476
  94.1 147.5 %all-gather.19.cloned.1.call-start = ((), (), s32[]{:S(2)}) async-start(), calls=%async_computation.10 | async-start | bytes 3317760 | tf_op jit(solution)/shard_map/all_gather | solution.py:608
  106.6 45.4 %collective-permute-start.16 = (f32[3,144,1152]{2,1,0:T(8,128)}, f32[3,144,1152]{2,1,0:T(8,128)}, u32[]{:S(2)}, u32[]{:S(2)}) collective-permute-start(f32[3,144,1152]{2,1,0:T(8,128)} %fusion.7.refs_1_), channel_id=1, source_target_pairs={{0,8},{4,12},{8,0},{12,4},{16,24},{20,28},{24,16},{28,20},{1,9},{5... | collective-permute-start | bytes 5971976 | tf_op jit(solution)/shard_map/ppermute | solution.py:467
  108.1 45.1 %collective-permute-start.17 = (f32[3,144,1152]{2,1,0:T(8,128)}, f32[3,144,1152]{2,1,0:T(8,128)}, u32[]{:S(2)}, u32[]{:S(2)}) collective-permute-start(f32[3,144,1152]{2,1,0:T(8,128)} %fusion.7.refs_1_), channel_id=1, source_target_pairs={{0,16},{4,20},{8,24},{12,28},{16,0},{20,4},{24,8},{28,12},{1,17},{... | collective-permute-start | bytes 5971976 | tf_op jit(solution)/shard_map/ppermute | solution.py:471
  122.4 38.4 %collective-permute-start.22 = (f32[516,1152]{1,0:T(8,128)}, f32[516,1152]{1,0:T(8,128)}, u32[]{:S(2)}, u32[]{:S(2)}) collective-permute-start(f32[516,1152]{1,0:T(8,128)} %convert_multiply_fusion), channel_id=1, source_target_pairs={{0,4},{4,0},{8,12},{12,8},{16,20},{20,16},{24,28},{28,24},{1,5},{5... | collective-permute-start | bytes 7133192 | tf_op jit(solution)/shard_map/ppermute | solution.py:463
  160.1 165.1 %all-gather.21.cloned.1.call-start = ((), (), s32[]{:S(2)}) async-start(), calls=%async_computation.11 | async-start | bytes 3317760 | tf_op jit(solution)/shard_map/all_gather | solution.py:608
  160.3 35.1 %collective-permute-start.19 = (f32[3,144,1152]{2,1,0:T(8,128)}, f32[3,144,1152]{2,1,0:T(8,128)}, u32[]{:S(2)}, u32[]{:S(2)}) collective-permute-start(f32[3,144,1152]{2,1,0:T(8,128)} %collective-permute-done.17.refs_5_), channel_id=1, source_target_pairs={{0,4},{4,0},{8,12},{12,8},{16,20},{20,16},{24,28},{28,24},{1,5},{5... | collective-permute-start | bytes 5971976 | tf_op jit(solution)/shard_map/ppermute | solution.py:463
  160.8 34.6 %collective-permute-start.18 = (f32[3,144,1152]{2,1,0:T(8,128)}, f32[3,144,1152]{2,1,0:T(8,128)}, u32[]{:S(2)}, u32[]{:S(2)}) collective-permute-start(f32[3,144,1152]{2,1,0:T(8,128)} %collective-permute-done.16.refs_3_), channel_id=1, source_target_pairs={{0,4},{4,0},{8,12},{12,8},{16,20},{20,16},{24,28},{28,24},{1,5},{5... | collective-permute-start | bytes 5971976 | tf_op jit(solution)/shard_map/ppermute | solution.py:463
  189.0 46.6 %collective-permute-start.25 = (f32[3,144,1152]{2,1,0:T(8,128)S(1)}, f32[3,144,1152]{2,1,0:T(8,128)}, u32[]{:S(2)}, u32[]{:S(2)}) collective-permute-start(f32[3,144,1152]{2,1,0:T(8,128)S(1)} %fusion.6.refs_1_), channel_id=1, source_target_pairs={{0,8},{4,12},{8,0},{12,4},{16,24},{20,28},{24,16},{28,20},{1,9},{5... | collective-permute-start | bytes 5971976 | tf_op jit(solution)/shard_map/ppermute | solution.py:467
  191.3 45.7 %collective-permute-start.26 = (f32[3,144,1152]{2,1,0:T(8,128)S(1)}, f32[3,144,1152]{2,1,0:T(8,128)}, u32[]{:S(2)}, u32[]{:S(2)}) collective-permute-start(f32[3,144,1152]{2,1,0:T(8,128)S(1)} %fusion.6.refs_1_), channel_id=1, source_target_pairs={{0,16},{4,20},{8,24},{12,28},{16,0},{20,4},{24,8},{28,12},{1,17},{... | collective-permute-start | bytes 5971976 | tf_op jit(solution)/shard_map/ppermute | solution.py:471
  248.2 38.5 %collective-permute-start.27 = (f32[516,1152]{1,0:T(8,128)}, f32[516,1152]{1,0:T(8,128)}, u32[]{:S(2)}, u32[]{:S(2)}) collective-permute-start(f32[516,1152]{1,0:T(8,128)} %get-tuple-element.392), channel_id=1, source_target_pairs={{0,4},{4,0},{8,12},{12,8},{16,20},{20,16},{24,28},{28,24},{1,5},{5... | collective-permute-start | bytes 7133192 | tf_op jit(solution)/shard_map/ppermute | solution.py:463
  248.2 32.2 %collective-permute-start.28 = (f32[2,144,1152]{2,1,0:T(8,128)}, f32[2,144,1152]{2,1,0:T(8,128)}, u32[]{:S(2)}, u32[]{:S(2)}) collective-permute-start(f32[2,144,1152]{2,1,0:T(8,128)} %slice.351), channel_id=1, source_target_pairs={{0,8},{4,12},{8,0},{12,4},{16,24},{20,28},{24,16},{28,20},{1,9},{5... | collective-permute-start | bytes 3981320 | tf_op jit(solution)/shard_map/ppermute | solution.py:467
  253.9 279.9 %all-gather.23.cloned.1.call-start = ((), (), s32[]{:S(2)}) async-start(), calls=%async_computation.12 | async-start | bytes 12165120 | tf_op jit(solution)/shard_map/all_gather | solution.py:1251
  258.6 63.9 %collective-permute-start.30 = (f32[3,144,1152]{2,1,0:T(8,128)S(1)}, f32[3,144,1152]{2,1,0:T(8,128)S(1)}, u32[]{:S(2)}, u32[]{:S(2)}) collective-permute-start(f32[3,144,1152]{2,1,0:T(8,128)S(1)} %fusion.5.refs_1_), channel_id=1, source_target_pairs={{0,8},{4,12},{8,0},{12,4},{16,24},{20,28},{24,16},{28,20},{1,9},{5... | collective-permute-start | bytes 5971976 | tf_op jit(solution)/shard_map/ppermute | solution.py:467
  260.1 63.7 %collective-permute-start.31 = (f32[3,144,1152]{2,1,0:T(8,128)S(1)}, f32[3,144,1152]{2,1,0:T(8,128)S(1)}, u32[]{:S(2)}, u32[]{:S(2)}) collective-permute-start(f32[3,144,1152]{2,1,0:T(8,128)S(1)} %fusion.5.refs_1_), channel_id=1, source_target_pairs={{0,16},{4,20},{8,24},{12,28},{16,0},{20,4},{24,8},{28,12},{1,17},{... | collective-permute-start | bytes 5971976 | tf_op jit(solution)/shard_map/ppermute | solution.py:471
  346.0 31.1 %collective-permute-start.33 = (f32[2,144,1152]{2,1,0:T(8,128)}, f32[2,144,1152]{2,1,0:T(8,128)}, u32[]{:S(2)}, u32[]{:S(2)}) collective-permute-start(f32[2,144,1152]{2,1,0:T(8,128)} %get-tuple-element.416), channel_id=1, source_target_pairs={{0,8},{4,12},{8,0},{12,4},{16,24},{20,28},{24,16},{28,20},{1,9},{5... | collective-permute-start | bytes 3981320 | tf_op jit(solution)/shard_map/ppermute | solution.py:467
  346.7 30.8 %collective-permute-start.34 = (f32[2,144,1152]{2,1,0:T(8,128)}, f32[2,144,1152]{2,1,0:T(8,128)}, u32[]{:S(2)}, u32[]{:S(2)}) collective-permute-start(f32[2,144,1152]{2,1,0:T(8,128)} %get-tuple-element.417), channel_id=1, source_target_pairs={{0,16},{4,20},{8,24},{12,28},{16,0},{20,4},{24,8},{28,12},{1,17},{... | collective-permute-start | bytes 3981320 | tf_op jit(solution)/shard_map/ppermute | solution.py:471
  363.7 259.1 %reduce-scatter.9.cloned.1.call-start = ((), (), s32[]{:S(2)}) async-start(), calls=%async_computation.5 | async-start | bytes 3317760 | tf_op jit(solution)/shard_map/reduce_scatter | solution.py:657
  393.3 60.7 %collective-permute-start.36 = (f32[4,144,1152]{2,1,0:T(8,128)}, f32[4,144,1152]{2,1,0:T(8,128)}, u32[]{:S(2)}, u32[]{:S(2)}) collective-permute-start(f32[4,144,1152]{2,1,0:T(8,128)} %pad_maximum_fusion.2), channel_id=1, source_target_pairs={{0,8},{4,12},{8,0},{12,4},{16,24},{20,28},{24,16},{28,20},{1,9},{5... | collective-permute-start | bytes 7962632 | tf_op jit(solution)/shard_map/ppermute | solution.py:467
  394.8 60.7 %collective-permute-start.37 = (f32[4,144,1152]{2,1,0:T(8,128)}, f32[4,144,1152]{2,1,0:T(8,128)}, u32[]{:S(2)}, u32[]{:S(2)}) collective-permute-start(f32[4,144,1152]{2,1,0:T(8,128)} %pad_maximum_fusion.3), channel_id=1, source_target_pairs={{0,16},{4,20},{8,24},{12,28},{16,0},{20,4},{24,8},{28,12},{1,17},{... | collective-permute-start | bytes 7962632 | tf_op jit(solution)/shard_map/ppermute | solution.py:471
  409.3 72.7 %collective-permute-start.38 = (f32[2,144,1152]{2,1,0:T(8,128)}, f32[2,144,1152]{2,1,0:T(8,128)}, u32[]{:S(2)}, u32[]{:S(2)}) collective-permute-start(f32[2,144,1152]{2,1,0:T(8,128)} %get-tuple-element.440), channel_id=1, source_target_pairs={{0,8},{4,12},{8,0},{12,4},{16,24},{20,28},{24,16},{28,20},{1,9},{5... | collective-permute-start | bytes 3981320 | tf_op jit(solution)/shard_map/ppermute | solution.py:467
  409.9 73.3 %collective-permute-start.39 = (f32[2,144,1152]{2,1,0:T(8,128)}, f32[2,144,1152]{2,1,0:T(8,128)}, u32[]{:S(2)}, u32[]{:S(2)}) collective-permute-start(f32[2,144,1152]{2,1,0:T(8,128)} %get-tuple-element.441), channel_id=1, source_target_pairs={{0,16},{4,20},{8,24},{12,28},{16,0},{20,4},{24,8},{28,12},{1,17},{... | collective-permute-start | bytes 3981320 | tf_op jit(solution)/shard_map/ppermute | solution.py:471
  500.6 33.2 %collective-permute-start.41 = (f32[12,144,1152]{2,1,0:T(8,128)}, f32[12,144,1152]{2,1,0:T(8,128)}, u32[]{:S(2)}, u32[]{:S(2)}) collective-permute-start(f32[12,144,1152]{2,1,0:T(8,128)} %dynamic-slice_bitcast_fusion), channel_id=1, source_target_pairs={{0,4},{4,0},{8,12},{12,8},{16,20},{20,16},{24,28},{28,24},{1,5},{5... | collective-permute-start | bytes 23887880 | tf_op jit(solution)/shard_map/ppermute | solution.py:463
  500.7 177.7 %reduce-scatter.7.cloned.1.call-start = ((), (), s32[]{:S(2)}) async-start(), calls=%async_computation.4 | async-start | bytes 3317760 | tf_op jit(solution)/shard_map/reduce_scatter | solution.py:657
  506.1 60.3 %collective-permute-start.45 = (f32[4,144,1152]{2,1,0:T(8,128)}, f32[4,144,1152]{2,1,0:T(8,128)}, u32[]{:S(2)}, u32[]{:S(2)}) collective-permute-start(f32[4,144,1152]{2,1,0:T(8,128)} %pad_maximum_fusion.4), channel_id=1, source_target_pairs={{0,8},{4,12},{8,0},{12,4},{16,24},{20,28},{24,16},{28,20},{1,9},{5... | collective-permute-start | bytes 7962632 | tf_op jit(solution)/shard_map/ppermute | solution.py:467
  506.7 60.0 %collective-permute-start.46 = (f32[4,144,1152]{2,1,0:T(8,128)}, f32[4,144,1152]{2,1,0:T(8,128)}, u32[]{:S(2)}, u32[]{:S(2)}) collective-permute-start(f32[4,144,1152]{2,1,0:T(8,128)} %pad_maximum_fusion.5), channel_id=1, source_target_pairs={{0,16},{4,20},{8,24},{12,28},{16,0},{20,4},{24,8},{28,12},{1,17},{... | collective-permute-start | bytes 7962632 | tf_op jit(solution)/shard_map/ppermute | solution.py:471
  529.4 81.1 %collective-permute-start.40 = (f32[16,72,1152]{2,1,0:T(8,128)}, f32[16,72,1152]{2,1,0:T(8,128)}, u32[]{:S(2)}, u32[]{:S(2)}) collective-permute-start(f32[16,72,1152]{2,1,0:T(8,128)} %dynamic-slice_bitcast_fusion.1), channel_id=1, source_target_pairs={{0,4},{4,0},{8,12},{12,8},{16,20},{20,16},{24,28},{28,24},{1,5},{5... | collective-permute-start | bytes 15925256 | tf_op jit(solution)/shard_map/ppermute | solution.py:463
  566.7 30.8 %collective-permute-start.43 = (f32[2,144,1152]{2,1,0:T(8,128)}, f32[2,144,1152]{2,1,0:T(8,128)}, u32[]{:S(2)}, u32[]{:S(2)}) collective-permute-start(f32[2,144,1152]{2,1,0:T(8,128)} %get-tuple-element.459), channel_id=1, source_target_pairs={{0,8},{4,12},{8,0},{12,4},{16,24},{20,28},{24,16},{28,20},{1,9},{5... | collective-permute-start | bytes 3981320 | tf_op jit(solution)/shard_map/ppermute | solution.py:467
  574.9 228.6 %reduce-scatter.11.cloned.1.call-start = ((), (), s32[]{:S(2)}) async-start(), calls=%async_computation.6 | async-start | bytes 3317760 | tf_op jit(solution)/shard_map/reduce_scatter | solution.py:657
  604.8 93.9 %collective-permute-start.49 = (f32[4,144,1152]{2,1,0:T(8,128)}, f32[4,144,1152]{2,1,0:T(8,128)}, u32[]{:S(2)}, u32[]{:S(2)}) collective-permute-start(f32[4,144,1152]{2,1,0:T(8,128)} %pad_maximum_fusion.6), channel_id=1, source_target_pairs={{0,8},{4,12},{8,0},{12,4},{16,24},{20,28},{24,16},{28,20},{1,9},{5... | collective-permute-start | bytes 7962632 | tf_op jit(solution)/shard_map/ppermute | solution.py:467
  605.4 93.4 %collective-permute-start.50 = (f32[4,144,1152]{2,1,0:T(8,128)}, f32[4,144,1152]{2,1,0:T(8,128)}, u32[]{:S(2)}, u32[]{:S(2)}) collective-permute-start(f32[4,144,1152]{2,1,0:T(8,128)} %pad_maximum_fusion.7), channel_id=1, source_target_pairs={{0,16},{4,20},{8,24},{12,28},{16,0},{20,4},{24,8},{28,12},{1,17},{... | collective-permute-start | bytes 7962632 | tf_op jit(solution)/shard_map/ppermute | solution.py:471
  606.9 91.9 %collective-permute-start.51 = (f32[516,576]{1,0:T(8,128)}, f32[516,576]{1,0:T(8,128)S(1)}, u32[]{:S(2)}, u32[]{:S(2)}) collective-permute-start(f32[516,576]{1,0:T(8,128)} %fusion.44), channel_id=1, source_target_pairs={{0,2},{1,3},{2,0},{3,1},{4,6},{5,7},{6,4},{7,5},{8,10},{9,11},{10,... | collective-permute-start | bytes 3566600 | tf_op jit(solution)/shard_map/ppermute | solution.py:476
  704.4 125.3 %reduce-scatter.13.cloned.1.call-start = ((), (), s32[]{:S(2)}) async-start(), calls=%async_computation.13 | async-start | bytes 1658880
  758.7 41.0 %collective-permute-start.56 = (f32[144,1152]{1,0:T(8,128)}, f32[144,1152]{1,0:T(8,128)S(1)}, u32[]{:S(2)}, u32[]{:S(2)}) collective-permute-start(f32[144,1152]{1,0:T(8,128)} %bitcast.105.refs_0_), channel_id=1, source_target_pairs={{0,8},{4,12},{8,0},{12,4},{16,24},{20,28},{24,16},{28,20},{1,9},{5... | collective-permute-start | bytes 1990664 | tf_op jit(solution)/shard_map/ppermute | solution.py:467
  759.6 40.0 %collective-permute-start.57 = (f32[144,1152]{1,0:T(8,128)}, f32[144,1152]{1,0:T(8,128)S(1)}, u32[]{:S(2)}, u32[]{:S(2)}) collective-permute-start(f32[144,1152]{1,0:T(8,128)} %bitcast.105.refs_0_), channel_id=1, source_target_pairs={{0,16},{4,20},{8,24},{12,28},{16,0},{20,4},{24,8},{28,12},{1,17},{... | collective-permute-start | bytes 1990664 | tf_op jit(solution)/shard_map/ppermute | solution.py:471
  803.5 44.8 %collective-permute-start.70 = (f32[576,1152]{1,0:T(8,128)}, f32[576,1152]{1,0:T(8,128)}, u32[]{:S(2)}, u32[]{:S(2)}) collective-permute-start(f32[576,1152]{1,0:T(8,128)} %shard_map.529.refs_0_), channel_id=1, source_target_pairs={{0,4},{4,0},{8,12},{12,8},{16,20},{20,16},{24,28},{28,24},{1,5},{5... | collective-permute-start | bytes 7962632 | tf_op jit(solution)/shard_map/ppermute | solution.py:463
  803.6 32.9 %collective-permute-start.66 = (f32[144,1152]{1,0:T(8,128)}, f32[144,1152]{1,0:T(8,128)S(1)}, u32[]{:S(2)}, u32[]{:S(2)}) collective-permute-start(f32[144,1152]{1,0:T(8,128)} %bitcast.380), channel_id=1, source_target_pairs={{0,8},{4,12},{8,0},{12,4},{16,24},{20,28},{24,16},{28,20},{1,9},{5... | collective-permute-start | bytes 1990664 | tf_op jit(solution)/shard_map/ppermute | solution.py:467
  804.2 32.4 %collective-permute-start.67 = (f32[144,1152]{1,0:T(8,128)}, f32[144,1152]{1,0:T(8,128)}, u32[]{:S(2)}, u32[]{:S(2)}) collective-permute-start(f32[144,1152]{1,0:T(8,128)} %bitcast.381), channel_id=1, source_target_pairs={{0,16},{4,20},{8,24},{12,28},{16,0},{20,4},{24,8},{28,12},{1,17},{... | collective-permute-start | bytes 1990664 | tf_op jit(solution)/shard_map/ppermute | solution.py:471
  836.6 57.0 %collective-permute-start.74 = (f32[576,1152]{1,0:T(8,128)S(1)}, f32[576,1152]{1,0:T(8,128)}, u32[]{:S(2)}, u32[]{:S(2)}) collective-permute-start(f32[576,1152]{1,0:T(8,128)S(1)} %shard_map.530.refs_0_), channel_id=1, source_target_pairs={{0,4},{4,0},{8,12},{12,8},{16,20},{20,16},{24,28},{28,24},{1,5},{5... | collective-permute-start | bytes 7962632 | tf_op jit(solution)/shard_map/ppermute | solution.py:463
  847.4 33.0 %collective-permute-start.65 = (f32[516,576]{1,0:T(8,128)}, f32[516,576]{1,0:T(8,128)}, u32[]{:S(2)}, u32[]{:S(2)}) collective-permute-start(f32[516,576]{1,0:T(8,128)} %fusion.43), channel_id=1, source_target_pairs={{0,1},{1,2},{2,3},{3,0},{4,5},{5,6},{6,7},{7,4},{8,9},{9,10},{10,1... | collective-permute-start | bytes 3566600 | tf_op jit(solution)/shard_map/ppermute | solution.py:476
  858.6 65.0 %collective-permute-start.77 = (f32[576,1152]{1,0:T(8,128)}, f32[576,1152]{1,0:T(8,128)}, u32[]{:S(2)}, u32[]{:S(2)}) collective-permute-start(f32[576,1152]{1,0:T(8,128)} %shard_map.532.refs_0_), channel_id=1, source_target_pairs={{0,4},{4,0},{8,12},{12,8},{16,20},{20,16},{24,28},{28,24},{1,5},{5... | collective-permute-start | bytes 7962632 | tf_op jit(solution)/shard_map/ppermute | solution.py:463
  887.2 44.1 %collective-permute-start.78 = (f32[288,1152]{1,0:T(8,128)}, f32[288,1152]{1,0:T(8,128)}, u32[]{:S(2)}, u32[]{:S(2)}) collective-permute-start(f32[288,1152]{1,0:T(8,128)} %shard_map.533.refs_0_), channel_id=1, source_target_pairs={{0,4},{4,0},{8,12},{12,8},{16,20},{20,16},{24,28},{28,24},{1,5},{5... | collective-permute-start | bytes 3981320 | tf_op jit(solution)/shard_map/ppermute | solution.py:463
  934.3 43.9 %collective-permute-start.84 = (f32[6,2,1152]{2,1,0:T(2,128)S(1)}, f32[6,2,1152]{2,1,0:T(2,128)S(1)}, u32[]{:S(2)}, u32[]{:S(2)}) collective-permute-start(f32[6,2,1152]{2,1,0:T(2,128)S(1)} %pad_maximum_fusion.13.refs_0_), channel_id=1, source_target_pairs={{0,3},{1,0},{2,1},{3,2},{4,7},{5,4},{6,5},{7,6},{8,11},{9,8},{10,9... | collective-permute-start | bytes 165896 | tf_op jit(solution)/shard_map/ppermute | solution.py:476
  937.7 40.5 %collective-permute-start.83 = (f32[6,2,1152]{2,1,0:T(2,128)S(1)}, f32[6,2,1152]{2,1,0:T(2,128)S(1)}, u32[]{:S(2)}, u32[]{:S(2)}) collective-permute-start(f32[6,2,1152]{2,1,0:T(2,128)S(1)} %pad_maximum_fusion.13.refs_0_), channel_id=1, source_target_pairs={{0,2},{1,3},{2,0},{3,1},{4,6},{5,7},{6,4},{7,5},{8,10},{9,11},{10,... | collective-permute-start | bytes 165896 | tf_op jit(solution)/shard_map/ppermute | solution.py:476
  938.9 39.3 %collective-permute-start.82 = (f32[6,2,1152]{2,1,0:T(2,128)S(1)}, f32[6,2,1152]{2,1,0:T(2,128)S(1)}, u32[]{:S(2)}, u32[]{:S(2)}) collective-permute-start(f32[6,2,1152]{2,1,0:T(2,128)S(1)} %pad_maximum_fusion.13.refs_0_), channel_id=1, source_target_pairs={{0,1},{1,2},{2,3},{3,0},{4,5},{5,6},{6,7},{7,4},{8,9},{9,10},{10,1... | collective-permute-start | bytes 165896 | tf_op jit(solution)/shard_map/ppermute | solution.py:476
  (197 other events, 2914.0 us)
Sparse Core Ops, SparseCore 0:
  10.2 36.6 all-gather.12
  49.0 54.5 all-gather.14
  105.7 54.1 all-gather.16
  161.9 54.1 all-gather.18
  254.0 53.5 all-gather.20
  363.8 169.9 all-gather.22
  536.7 50.7 reduce-scatter.8
  590.4 87.9 reduce-scatter.6
  704.6 51.6 reduce-scatter.10
  759.0 31.3 reduce-scatter.12

commit v4 on v3

--- a/solution.py
+++ b/solution.py
@@ -1280,14 +1280,13 @@
     qkv_grad = jnp.einsum(
         "te,td->ed", order.after(qkv_grad_low), normed_low, preferred_element_type=jnp.float32
     ).reshape(3 * mp_count, 2, hidden_slice, D)
-    qkv_grad = order.mark(qkv_grad)
-    fc1_add = order.mark(*fc1_add)
-    fc1_sides = swap_plane(order, *order.mark(*cut_sides(fc1_grad, quarter, *fc1_add)))
     proj_grad = jnp.einsum(
         "te,td->ed", attended, order.after(residual_low), preferred_element_type=jnp.float32
     ).reshape(mp_count, 2, hidden_slice, D)
     attn_given = order.mark(pick(qkv_grad, 1 - core, 1), pick(proj_grad, 1 - core, 1))
-    attn_given = [to_core(array) for array in attn_given]
+    fc1_add = order.mark(*fc1_add)
+    fc1_sides = swap_plane(order, *order.mark(*cut_sides(fc1_grad, quarter, *fc1_add)))
+    attn_given = [to_core(array) for array in order.after(*attn_given)]
     norm_one_in = matmul(order.after(qkv_grad_low), qkv_low)
     back_one, gain_one_grad, bias_one_grad = norm_backward(
         norm_one_in, normal_one, inverse_one, vectors[0]
@@ -1315,8 +1314,7 @@
             jnp.einsum("td,cd->tc", joined_low, shard_low, preferred_element_type=jnp.float32)
         )
 
-    turn_two = turn_mp(input_product(2), 2)
-    turn_one, stay, turn_three = input_product(1), input_product(0), input_product(3)
+    stay, turn_one, turn_two, turn_three = [input_product(shift) for shift in range(4)]
     attn_add = order.mark(*attn_add)
     attn_sides = swap_plane(order, *order.mark(*cut_sides(attn_grad, quarter, *attn_add)))
     skip_given = order.mark(skip_given)
@@ -1339,10 +1337,9 @@
     hidden_grad = jnp.where(jnp.arange(2)[None, None, :, None] == core, hidden_grad, 0.0)
     small = order.mark(jnp.concatenate([vector_grad.reshape(-1), hidden_grad.reshape(-1)]))
     small_core = to_core(small)
-    fc1_piece = order.mark(fc1_piece)
-    turn_two = order.mark(turn_two)
     attn_sides = order.mark(*attn_sides)
     attn_piece = sum_deep(order, attn_grad, quarter, *attn_sides)
+    fc1_piece = order.mark(fc1_piece)
     skip_add = order.mark(*skip_add)
     skip_sides = swap_plane(order, *order.mark(*cut_sides(skip_grad, quarter, *skip_add)))
     small = order.mark(small + order.mark(small_core))
@@ -1396,9 +1393,9 @@
     block_output = order.mark(block_output)
     fc2_near = order.mark(*fc2_near)
     fc2_far = spread_far(fc2_near)
-    small = order.mark(small + order.mark(small_y))
     fc1_near = order.mark(*fc1_near)
     fc1_far = spread_far(fc1_near)
+    turn_two = turn_mp(order.after(turn_two), 2)
     fc2_far = order.mark(*fc2_far)
     attn_piece = order.mark(attn_piece)
     attn_near = spread(attn_piece)
@@ -1407,6 +1404,7 @@
     fc1_far = order.mark(*fc1_far)
     skip_piece = order.mark(skip_piece)
     skip_near = spread(skip_piece)
+    turn_two = order.mark(turn_two)
     turn_one = turn_mp(order.after(turn_one), 1)
     fc1_held = order.mark(hold(fc1_piece, fc1_near, fc1_far))
     attn_near = order.mark(*attn_near)
@@ -1414,6 +1412,7 @@
     fc1_other = to_core(order.after(fc1_held))
     skip_near = order.mark(*skip_near)
     skip_far = spread_far(skip_near)
+    small = order.mark(small + order.mark(small_y))
     small = jnp.concatenate(
         [small, weight_sq, jnp.zeros((D - 6,), jnp.float32)], 0
     ).reshape(6, 2, D)

time: 1040 us -> 1030 us (level)
  waiting for transfers between devices: 353 us -> 337 us
    reduce_scatter x3, waiting for transfers between devices: 55.7 us -> 0.02 us  [sum_deep(): return lax.psum_scatter(own, 'mp', scatter_dimension=0, tiled=False)]
    ppermute x25, waiting for transfers between devices: 190 us -> 211 us  [to_x(): return lax.ppermute(array, 'dp', [(i, i ^ 2) for i in range(8)])]
    ppermute x25, waiting for transfers between devices: 40.9 us -> 51.6 us  [to_y(): return lax.ppermute(array, 'dp', [(i, i ^ 4) for i in range(8)])]
    unnamed x321 -> x319, local copies, waits for them, and re-layouts: 100 us -> 99.1 us
  transfers between devices with their start and end apart: 101 -> 101, of which waited for: 40 -> 43; matrix products, arithmetic and copies ran while one was open for 33% -> 34% of each run, Pallas kernels for 10% -> 10%
where the time goes in v4:
time: 1030 us; the launch traced here: 1020 us
  waiting for transfers between devices  337 us (33%)
  local copies, waits for them, and re-layouts  209 us (20%)
  Pallas kernels  132 us (13%)
  other arithmetic  120 us (12%)
  matrix products  115 us (11%)
  starting transfers between devices  87.8 us (9%)
  between operations  21.2 us (2%)
    ppermute x25, waiting for transfers between devices, to_x(): return lax.ppermute(array, 'dp', [(i, i ^ 2) for i in range(8)])  211 us
    unnamed x319, local copies, waits for them, and re-layouts  99.1 us
    ppermute x18, waiting for transfers between devices, turn_mp(): lax.ppermute(array, 'mp', [(i, (i + shift) % count) for i in range(count)])  53.9 us
    ppermute x25, waiting for transfers between devices, to_y(): return lax.ppermute(array, 'dp', [(i, i ^ 4) for i in range(8)])  51.6 us
    dot_general x5, matrix products, matmul(): return jnp.dot(left_side, right_side, preferred_element_type=jnp.float32)  37.6 us
    ppermute x25, starting transfers between devices, to_y(): return lax.ppermute(array, 'dp', [(i, i ^ 4) for i in range(8)])  32.7 us
    pallas_call x4, Pallas kernels, assemble(): pl.pallas_call(kernel, in_specs=[pl.BlockSpec(memory_space=pltpu.SMEM)] +...  30 us
    pallas_call x8, Pallas kernels, place_rows(): pl.pallas_call(kernel, in_specs=in_specs, out_specs=out_specs, out_shape=...  27.1 us
  transfers between devices with their start and end apart: 101, of which 43 were waited for; matrix products, arithmetic and copies ran while one was open for 34% of the time, Pallas kernels for 10%

profile of v4, /device:TPU:0, one launch (start us, length us, event | category | flops | bytes accessed | tf_op | source)
XLA Modules:
  0.0 1021.2 jit_solution(1865311291282414388)
XLA Ops:
  34.8 6.9 copy.138
  58.0 16.4 %collective-permute-done.4.refs_3_ = f32[3,72,1152]{2,1,0:T(8,128)} collective-permute-done((f32[3,72,1152]{2,1,0:T(8,128)}, f32[3,72,1152]{2,1,0:T(8,128)}, u32[]{:S(2)}, u32[]{:S(2)}) %collective-permute-start.4) | collective-permute-done | bytes 995360 | tf_op jit(solution)/shard_map/ppermute | solution.py:467
  79.7 5.8 collective-permute-done.12.refs_9_
  85.5 5.4 collective-permute-done.11.refs_7_
  94.7 8.9 all-gather.15.cloned.1.call-done
  109.6 6.5 shard_map.521
  145.7 6.3 collective-permute-done.16.refs_3_
  164.9 13.3 %collective-permute-done.20.refs_7_ = f32[1,144,1152]{2,1,0:T(8,128)} collective-permute-done((f32[1,144,1152]{2,1,0:T(8,128)S(1)}, f32[1,144,1152]{2,1,0:T(8,128)}, u32[]{:S(2)}, u32[]{:S(2)}) %collective-permute-start.20) | collective-permute-done | bytes 663584 | tf_op jit(solution)/shard_map/ppermute | solution.py:467
  178.2 8.4 collective-permute-done.21.refs_9_
  196.5 10.5 %shard_map.522 = (bf16[12,288,1152]{2,1,0:T(8,128)(2,1)}, bf16[4,288,1152]{2,1,0:T(8,128)(2,1)S(1)}) custom-call(s32[17]{0:T(128)S(1)} %stack.384.table_ref, f32[4,288,1152]{2,1,0:T(8,128)} %bitcast.394, f32[3,144,1152]{2,1,0:T(8,128)} %fusion.7.refs_1_, f32[3,144,1152]{2,1,0:T(8,128)} %collective-permute-done.15.refs_2_, ...), custom_call_target="tpu_custom_call" | custom-call | bytes 1024 | tf_op jit(solution)/shard_map/pallas_call | solution.py:553
  208.5 8.6 convolution_convert_fusion.qkv_ref
  217.1 9.2 shard_map.523
  229.4 6.2 fusion
  260.7 6.0 collective-permute-done.29.refs_5_
  266.7 13.7 %collective-permute-done.28.refs_4_ = f32[2,144,1152]{2,1,0:T(8,128)} collective-permute-done((f32[2,144,1152]{2,1,0:T(8,128)}, f32[2,144,1152]{2,1,0:T(8,128)}, u32[]{:S(2)}, u32[]{:S(2)}) %collective-permute-start.28) | collective-permute-done | bytes 1327136 | tf_op jit(solution)/shard_map/ppermute | solution.py:467
  280.4 6.2 shard_map.524
  290.9 9.4 multiply_convert_fusion
  300.3 8.0 fusion.35
  314.0 8.6 collective-permute-done.30.refs_2_
  330.5 6.8 shard_map.525
  337.4 8.5 fusion.36
  348.2 13.3 %fusion.31 = (f32[2304]{0:T(1024)S(1)}, bf16[1032,2304]{1,0:T(8,128)(2,1)}) fusion(f32[1032,2304]{1,0:T(8,128)S(1)} %bitcast.441, bf16[1032,1152]{1,0:T(8,128)(2,1)S(1)} %copy-done.81, bf16[2304,1152]{1,0:T(8,128)(2,1)S(1)} %bitcast.376), kind=kOutput, calls=%fused_computation.237 | convolution fusion | flops 5511571456 | bytes 21961728 | tf_op jit(solution)/shard_map/td,fd->tf/dot_general | solution.py:1243
  363.7 13.5 %collective-permute-done.33 = f32[2,144,1152]{2,1,0:T(8,128)} collective-permute-done((f32[2,144,1152]{2,1,0:T(8,128)}, f32[2,144,1152]{2,1,0:T(8,128)}, u32[]{:S(2)}, u32[]{:S(2)}) %collective-permute-start.33) | collective-permute-done | bytes 1327136 | tf_op jit(solution)/shard_map/ppermute | solution.py:467
  384.0 9.0 fusion.37
  396.3 7.9 fusion.38
  425.7 16.9 %shard_map.526 = bf16[2,258,3456]{2,1,0:T(8,128)(2,1)S(1)} custom-call(bf16[2,258,3456]{2,1,0:T(8,128)(2,1)S(1)} %copy-done.15, bf16[2,258,1152]{2,1,0:T(8,128)(2,1)S(1)} %reshape.350.grad_ref), custom_call_target="tpu_custom_call" | custom-call | bytes 1024 | tf_op jit(solution)/shard_map/pallas_call | solution.py:1020
  455.5 5.3 fusion.3
  460.8 9.1 fusion.39
  495.4 10.4 %multiply_reduce_fusion.5 = (f32[1152]{0:T(1024)S(1)}, f32[516]{0:T(1024)S(1)}, f32[516]{0:T(1024)S(1)}, f32[1152]{0:T(1024)S(1)}, f32[516,1152]{1,0:T(8,128)S(1)}) fusion(f32[516,1152]{1,0:T(8,128)} %get-tuple-element.449, f32[1152]{0:T(1024)S(1)} %copy-done.100, bf16[516,3456]{1,0:T(8,128)(2,1)} %reshape.351, bf16[3456,1152]{1,0:T(8,128)(2,1)} %bitcast.431), kind=kOutput, calls=%fused_computation.44 | convolution fusion | flops 4112871936 | bytes 16302624 | tf_op jit(solution)/shard_map/dot_general | solution.py:30
  525.0 8.8 all-gather.23.cloned.1.call-done
  536.4 14.6 %shard_map.527 = f32[16,144,1152]{2,1,0:T(8,128)} custom-call(s32[1]{0:T(128)} %bitcast.26.core_ref, f32[12,2,144,1152]{3,2,1,0:T(8,128)} %bitcast.392, f32[4,2,144,1152]{3,2,1,0:T(8,128)S(1)} %copy-done.22, f32[12,144,1152]{2,1,0:T(8,128)} %collective-permute-done.41.refs_2_, f32[4,144,1152]{2,1,0:T(8,128)S(1)} %collective-permute-done.42.refs_3_), custom_call_target="tpu_custom_call" | custom-call | bytes 1024 | tf_op jit(solution)/shard_map/pallas_call | solution.py:753
  555.5 10.7 %collective-permute-done.45 = f32[4,144,1152]{2,1,0:T(8,128)} collective-permute-done((f32[4,144,1152]{2,1,0:T(8,128)}, f32[4,144,1152]{2,1,0:T(8,128)}, u32[]{:S(2)}, u32[]{:S(2)}) %collective-permute-start.45) | collective-permute-done | bytes 2654240 | tf_op jit(solution)/shard_map/ppermute | solution.py:467
  569.4 5.2 fusion.2
  581.2 15.9 %collective-permute-done.43 = f32[2,144,1152]{2,1,0:T(8,128)S(1)} collective-permute-done((f32[2,144,1152]{2,1,0:T(8,128)}, f32[2,144,1152]{2,1,0:T(8,128)S(1)}, u32[]{:S(2)}, u32[]{:S(2)}) %collective-permute-start.43) | collective-permute-done | bytes 1327136 | tf_op jit(solution)/shard_map/ppermute | solution.py:467
  607.2 9.5 shard_map.528
  619.1 43.4 %collective-permute-done.49 = f32[4,144,1152]{2,1,0:T(8,128)} collective-permute-done((f32[4,144,1152]{2,1,0:T(8,128)}, f32[4,144,1152]{2,1,0:T(8,128)}, u32[]{:S(2)}, u32[]{:S(2)}) %collective-permute-start.49) | collective-permute-done | bytes 2654240 | tf_op jit(solution)/shard_map/ppermute | solution.py:467
  671.1 11.7 %collective-permute-done.47 = f32[2,72,1152]{2,1,0:T(8,128)S(1)} collective-permute-done((f32[2,72,1152]{2,1,0:T(8,128)S(1)}, f32[2,72,1152]{2,1,0:T(8,128)S(1)}, u32[]{:S(2)}, u32[]{:S(2)}) %collective-permute-start.47) | collective-permute-done | bytes 663584 | tf_op jit(solution)/shard_map/ppermute | solution.py:467
  690.2 22.9 %collective-permute-done.51 = f32[4,72,1152]{2,1,0:T(8,128)S(1)} collective-permute-done((f32[4,72,1152]{2,1,0:T(8,128)S(1)}, f32[4,72,1152]{2,1,0:T(8,128)S(1)}, u32[]{:S(2)}, u32[]{:S(2)}) %collective-permute-start.51) | collective-permute-done | bytes 1327136 | tf_op jit(solution)/shard_map/ppermute | solution.py:467
  720.7 6.8 add_convert_fusion
  732.2 11.2 %collective-permute-done.57.refs_1_ = f32[144,1152]{1,0:T(8,128)S(1)} collective-permute-done((f32[144,1152]{1,0:T(8,128)S(1)}, f32[144,1152]{1,0:T(8,128)S(1)}, u32[]{:S(2)}, u32[]{:S(2)}) %collective-permute-start.57) | collective-permute-done | bytes 663584 | tf_op jit(solution)/shard_map/ppermute | solution.py:467
  748.9 5.5 collective-permute-done.62.refs_3_
  764.1 7.1 collective-permute-done.60.refs_3_
  773.4 12.9 %collective-permute-done.61.refs_4_ = f32[72,1152]{1,0:T(8,128)S(1)} collective-permute-done((f32[72,1152]{1,0:T(8,128)S(1)}, f32[72,1152]{1,0:T(8,128)S(1)}, u32[]{:S(2)}, u32[]{:S(2)}) %collective-permute-start.61) | collective-permute-done | bytes 331808 | tf_op jit(solution)/shard_map/ppermute | solution.py:471
  794.5 25.0 %collective-permute-done.59.refs_2_ = f32[516,576]{1,0:T(8,128)} collective-permute-done((f32[516,576]{1,0:T(8,128)}, f32[516,576]{1,0:T(8,128)}, u32[]{:S(2)}, u32[]{:S(2)}) %collective-permute-start.59) | collective-permute-done | bytes 1188896 | tf_op jit(solution)/shard_map/ppermute | solution.py:476
  824.1 6.8 collective-permute-done.70
  850.3 15.7 %collective-permute-done.64.refs_1_ = f32[516,576]{1,0:T(8,128)} collective-permute-done((f32[516,576]{1,0:T(8,128)}, f32[516,576]{1,0:T(8,128)}, u32[]{:S(2)}, u32[]{:S(2)}) %collective-permute-start.64) | collective-permute-done | bytes 1188896 | tf_op jit(solution)/shard_map/ppermute | solution.py:476
  883.6 12.0 %collective-permute-done.73.refs_3_ = f32[516,576]{1,0:T(8,128)} collective-permute-done((f32[516,576]{1,0:T(8,128)}, f32[516,576]{1,0:T(8,128)}, u32[]{:S(2)}, u32[]{:S(2)}) %collective-permute-start.73) | collective-permute-done | bytes 1188896 | tf_op jit(solution)/shard_map/ppermute | solution.py:476
  1007.8 5.3 shard_map.545
  (760 shorter events, 484.2 us)
Async XLA Ops:
  7.2 42.1 %all-gather.13.cloned.1.call-start = ((), (), s32[]{:S(2)}) async-start(), calls=%async_computation.7 | async-start | bytes 1658880 | tf_op jit(solution)/shard_map/all_gather | solution.py:608
  9.1 94.5 %all-gather.15.cloned.1.call-start = ((), (), s32[]{:S(2)}) async-start(), calls=%async_computation.8 | async-start | bytes 3317760 | tf_op jit(solution)/shard_map/all_gather | solution.py:608
  15.3 149.6 %all-gather.17.cloned.1.call-start = ((), (), s32[]{:S(2)}) async-start(), calls=%async_computation.9 | async-start | bytes 3317760 | tf_op jit(solution)/shard_map/all_gather | solution.py:608
  17.4 31.8 %collective-permute-start.86 = (f32[1152]{0:T(1024)S(1)}, f32[1152]{0:T(1024)S(1)}, u32[]{:S(2)}, u32[]{:S(2)}) collective-permute-start(f32[1152]{0:T(1024)S(1)} %copy-done.116), channel_id=1, source_target_pairs={{0,2},{1,3},{2,0},{3,1},{4,6},{5,7},{6,4},{7,5},{8,10},{9,11},{10,... | collective-permute-start | bytes 13832 | tf_op jit(solution)/shard_map/ppermute | solution.py:476
  94.1 147.5 %all-gather.19.cloned.1.call-start = ((), (), s32[]{:S(2)}) async-start(), calls=%async_computation.10 | async-start | bytes 3317760 | tf_op jit(solution)/shard_map/all_gather | solution.py:608
  106.6 45.4 %collective-permute-start.16 = (f32[3,144,1152]{2,1,0:T(8,128)}, f32[3,144,1152]{2,1,0:T(8,128)}, u32[]{:S(2)}, u32[]{:S(2)}) collective-permute-start(f32[3,144,1152]{2,1,0:T(8,128)} %fusion.7.refs_1_), channel_id=1, source_target_pairs={{0,8},{4,12},{8,0},{12,4},{16,24},{20,28},{24,16},{28,20},{1,9},{5... | collective-permute-start | bytes 5971976 | tf_op jit(solution)/shard_map/ppermute | solution.py:467
  108.1 45.1 %collective-permute-start.17 = (f32[3,144,1152]{2,1,0:T(8,128)}, f32[3,144,1152]{2,1,0:T(8,128)}, u32[]{:S(2)}, u32[]{:S(2)}) collective-permute-start(f32[3,144,1152]{2,1,0:T(8,128)} %fusion.7.refs_1_), channel_id=1, source_target_pairs={{0,16},{4,20},{8,24},{12,28},{16,0},{20,4},{24,8},{28,12},{1,17},{... | collective-permute-start | bytes 5971976 | tf_op jit(solution)/shard_map/ppermute | solution.py:471
  122.4 38.4 %collective-permute-start.22 = (f32[516,1152]{1,0:T(8,128)}, f32[516,1152]{1,0:T(8,128)}, u32[]{:S(2)}, u32[]{:S(2)}) collective-permute-start(f32[516,1152]{1,0:T(8,128)} %convert_multiply_fusion), channel_id=1, source_target_pairs={{0,4},{4,0},{8,12},{12,8},{16,20},{20,16},{24,28},{28,24},{1,5},{5... | collective-permute-start | bytes 7133192 | tf_op jit(solution)/shard_map/ppermute | solution.py:463
  160.1 165.1 %all-gather.21.cloned.1.call-start = ((), (), s32[]{:S(2)}) async-start(), calls=%async_computation.11 | async-start | bytes 3317760 | tf_op jit(solution)/shard_map/all_gather | solution.py:608
  160.3 35.1 %collective-permute-start.19 = (f32[3,144,1152]{2,1,0:T(8,128)}, f32[3,144,1152]{2,1,0:T(8,128)}, u32[]{:S(2)}, u32[]{:S(2)}) collective-permute-start(f32[3,144,1152]{2,1,0:T(8,128)} %collective-permute-done.17.refs_5_), channel_id=1, source_target_pairs={{0,4},{4,0},{8,12},{12,8},{16,20},{20,16},{24,28},{28,24},{1,5},{5... | collective-permute-start | bytes 5971976 | tf_op jit(solution)/shard_map/ppermute | solution.py:463
  160.8 34.6 %collective-permute-start.18 = (f32[3,144,1152]{2,1,0:T(8,128)}, f32[3,144,1152]{2,1,0:T(8,128)}, u32[]{:S(2)}, u32[]{:S(2)}) collective-permute-start(f32[3,144,1152]{2,1,0:T(8,128)} %collective-permute-done.16.refs_3_), channel_id=1, source_target_pairs={{0,4},{4,0},{8,12},{12,8},{16,20},{20,16},{24,28},{28,24},{1,5},{5... | collective-permute-start | bytes 5971976 | tf_op jit(solution)/shard_map/ppermute | solution.py:463
  189.0 46.6 %collective-permute-start.25 = (f32[3,144,1152]{2,1,0:T(8,128)S(1)}, f32[3,144,1152]{2,1,0:T(8,128)}, u32[]{:S(2)}, u32[]{:S(2)}) collective-permute-start(f32[3,144,1152]{2,1,0:T(8,128)S(1)} %fusion.6.refs_1_), channel_id=1, source_target_pairs={{0,8},{4,12},{8,0},{12,4},{16,24},{20,28},{24,16},{28,20},{1,9},{5... | collective-permute-start | bytes 5971976 | tf_op jit(solution)/shard_map/ppermute | solution.py:467
  191.3 45.7 %collective-permute-start.26 = (f32[3,144,1152]{2,1,0:T(8,128)S(1)}, f32[3,144,1152]{2,1,0:T(8,128)}, u32[]{:S(2)}, u32[]{:S(2)}) collective-permute-start(f32[3,144,1152]{2,1,0:T(8,128)S(1)} %fusion.6.refs_1_), channel_id=1, source_target_pairs={{0,16},{4,20},{8,24},{12,28},{16,0},{20,4},{24,8},{28,12},{1,17},{... | collective-permute-start | bytes 5971976 | tf_op jit(solution)/shard_map/ppermute | solution.py:471
  248.2 38.5 %collective-permute-start.27 = (f32[516,1152]{1,0:T(8,128)}, f32[516,1152]{1,0:T(8,128)}, u32[]{:S(2)}, u32[]{:S(2)}) collective-permute-start(f32[516,1152]{1,0:T(8,128)} %get-tuple-element.394), channel_id=1, source_target_pairs={{0,4},{4,0},{8,12},{12,8},{16,20},{20,16},{24,28},{28,24},{1,5},{5... | collective-permute-start | bytes 7133192 | tf_op jit(solution)/shard_map/ppermute | solution.py:463
  248.2 32.2 %collective-permute-start.28 = (f32[2,144,1152]{2,1,0:T(8,128)}, f32[2,144,1152]{2,1,0:T(8,128)}, u32[]{:S(2)}, u32[]{:S(2)}) collective-permute-start(f32[2,144,1152]{2,1,0:T(8,128)} %slice.351), channel_id=1, source_target_pairs={{0,8},{4,12},{8,0},{12,4},{16,24},{20,28},{24,16},{28,20},{1,9},{5... | collective-permute-start | bytes 3981320 | tf_op jit(solution)/shard_map/ppermute | solution.py:467
  253.9 280.0 %all-gather.23.cloned.1.call-start = ((), (), s32[]{:S(2)}) async-start(), calls=%async_computation.12 | async-start | bytes 12165120 | tf_op jit(solution)/shard_map/all_gather | solution.py:1251
  258.7 63.9 %collective-permute-start.30 = (f32[3,144,1152]{2,1,0:T(8,128)S(1)}, f32[3,144,1152]{2,1,0:T(8,128)S(1)}, u32[]{:S(2)}, u32[]{:S(2)}) collective-permute-start(f32[3,144,1152]{2,1,0:T(8,128)S(1)} %fusion.5.refs_1_), channel_id=1, source_target_pairs={{0,8},{4,12},{8,0},{12,4},{16,24},{20,28},{24,16},{28,20},{1,9},{5... | collective-permute-start | bytes 5971976 | tf_op jit(solution)/shard_map/ppermute | solution.py:467
  260.1 63.7 %collective-permute-start.31 = (f32[3,144,1152]{2,1,0:T(8,128)S(1)}, f32[3,144,1152]{2,1,0:T(8,128)S(1)}, u32[]{:S(2)}, u32[]{:S(2)}) collective-permute-start(f32[3,144,1152]{2,1,0:T(8,128)S(1)} %fusion.5.refs_1_), channel_id=1, source_target_pairs={{0,16},{4,20},{8,24},{12,28},{16,0},{20,4},{24,8},{28,12},{1,17},{... | collective-permute-start | bytes 5971976 | tf_op jit(solution)/shard_map/ppermute | solution.py:471
  346.0 31.1 %collective-permute-start.33 = (f32[2,144,1152]{2,1,0:T(8,128)}, f32[2,144,1152]{2,1,0:T(8,128)}, u32[]{:S(2)}, u32[]{:S(2)}) collective-permute-start(f32[2,144,1152]{2,1,0:T(8,128)} %get-tuple-element.418), channel_id=1, source_target_pairs={{0,8},{4,12},{8,0},{12,4},{16,24},{20,28},{24,16},{28,20},{1,9},{5... | collective-permute-start | bytes 3981320 | tf_op jit(solution)/shard_map/ppermute | solution.py:467
  363.7 255.4 %reduce-scatter.9.cloned.1.call-start = ((), (), s32[]{:S(2)}) async-start(), calls=%async_computation.5 | async-start | bytes 3317760 | tf_op jit(solution)/shard_map/reduce_scatter | solution.py:657
  393.3 60.7 %collective-permute-start.38 = (f32[4,144,1152]{2,1,0:T(8,128)}, f32[4,144,1152]{2,1,0:T(8,128)}, u32[]{:S(2)}, u32[]{:S(2)}) collective-permute-start(f32[4,144,1152]{2,1,0:T(8,128)} %pad_maximum_fusion.2), channel_id=1, source_target_pairs={{0,8},{4,12},{8,0},{12,4},{16,24},{20,28},{24,16},{28,20},{1,9},{5... | collective-permute-start | bytes 7962632 | tf_op jit(solution)/shard_map/ppermute | solution.py:467
  394.8 60.7 %collective-permute-start.39 = (f32[4,144,1152]{2,1,0:T(8,128)}, f32[4,144,1152]{2,1,0:T(8,128)}, u32[]{:S(2)}, u32[]{:S(2)}) collective-permute-start(f32[4,144,1152]{2,1,0:T(8,128)} %pad_maximum_fusion.3), channel_id=1, source_target_pairs={{0,16},{4,20},{8,24},{12,28},{16,0},{20,4},{24,8},{28,12},{1,17},{... | collective-permute-start | bytes 7962632 | tf_op jit(solution)/shard_map/ppermute | solution.py:471
  409.3 72.7 %collective-permute-start.36 = (f32[2,144,1152]{2,1,0:T(8,128)}, f32[2,144,1152]{2,1,0:T(8,128)}, u32[]{:S(2)}, u32[]{:S(2)}) collective-permute-start(f32[2,144,1152]{2,1,0:T(8,128)} %get-tuple-element.434), channel_id=1, source_target_pairs={{0,8},{4,12},{8,0},{12,4},{16,24},{20,28},{24,16},{28,20},{1,9},{5... | collective-permute-start | bytes 3981320 | tf_op jit(solution)/shard_map/ppermute | solution.py:467
  409.9 73.3 %collective-permute-start.37 = (f32[2,144,1152]{2,1,0:T(8,128)}, f32[2,144,1152]{2,1,0:T(8,128)}, u32[]{:S(2)}, u32[]{:S(2)}) collective-permute-start(f32[2,144,1152]{2,1,0:T(8,128)} %get-tuple-element.435), channel_id=1, source_target_pairs={{0,16},{4,20},{8,24},{12,28},{16,0},{20,4},{24,8},{28,12},{1,17},{... | collective-permute-start | bytes 3981320 | tf_op jit(solution)/shard_map/ppermute | solution.py:471
  489.5 44.4 %collective-permute-start.41 = (f32[12,144,1152]{2,1,0:T(8,128)}, f32[12,144,1152]{2,1,0:T(8,128)}, u32[]{:S(2)}, u32[]{:S(2)}) collective-permute-start(f32[12,144,1152]{2,1,0:T(8,128)} %dynamic-slice_bitcast_fusion), channel_id=1, source_target_pairs={{0,4},{4,0},{8,12},{12,8},{16,20},{20,16},{24,28},{28,24},{1,5},{5... | collective-permute-start | bytes 23887880 | tf_op jit(solution)/shard_map/ppermute | solution.py:463
  494.7 176.4 %reduce-scatter.7.cloned.1.call-start = ((), (), s32[]{:S(2)}) async-start(), calls=%async_computation.4 | async-start | bytes 3317760 | tf_op jit(solution)/shard_map/reduce_scatter | solution.py:657
  494.8 39.1 %collective-permute-start.42 = (f32[4,144,1152]{2,1,0:T(8,128)}, f32[4,144,1152]{2,1,0:T(8,128)S(1)}, u32[]{:S(2)}, u32[]{:S(2)}) collective-permute-start(f32[4,144,1152]{2,1,0:T(8,128)} %dynamic-slice_bitcast_fusion.2), channel_id=1, source_target_pairs={{0,4},{4,0},{8,12},{12,8},{16,20},{20,16},{24,28},{28,24},{1,5},{5... | collective-permute-start | bytes 7962632 | tf_op jit(solution)/shard_map/ppermute | solution.py:463
  505.8 60.4 %collective-permute-start.45 = (f32[4,144,1152]{2,1,0:T(8,128)}, f32[4,144,1152]{2,1,0:T(8,128)}, u32[]{:S(2)}, u32[]{:S(2)}) collective-permute-start(f32[4,144,1152]{2,1,0:T(8,128)} %pad_maximum_fusion.4), channel_id=1, source_target_pairs={{0,8},{4,12},{8,0},{12,4},{16,24},{20,28},{24,16},{28,20},{1,9},{5... | collective-permute-start | bytes 7962632 | tf_op jit(solution)/shard_map/ppermute | solution.py:467
  506.5 60.0 %collective-permute-start.46 = (f32[4,144,1152]{2,1,0:T(8,128)}, f32[4,144,1152]{2,1,0:T(8,128)}, u32[]{:S(2)}, u32[]{:S(2)}) collective-permute-start(f32[4,144,1152]{2,1,0:T(8,128)} %pad_maximum_fusion.5), channel_id=1, source_target_pairs={{0,16},{4,20},{8,24},{12,28},{16,0},{20,4},{24,8},{28,12},{1,17},{... | collective-permute-start | bytes 7962632 | tf_op jit(solution)/shard_map/ppermute | solution.py:471
  520.4 86.8 %collective-permute-start.40 = (f32[16,72,1152]{2,1,0:T(8,128)}, f32[16,72,1152]{2,1,0:T(8,128)}, u32[]{:S(2)}, u32[]{:S(2)}) collective-permute-start(f32[16,72,1152]{2,1,0:T(8,128)} %dynamic-slice_bitcast_fusion.1), channel_id=1, source_target_pairs={{0,4},{4,0},{8,12},{12,8},{16,20},{20,16},{24,28},{28,24},{1,5},{5... | collective-permute-start | bytes 15925256 | tf_op jit(solution)/shard_map/ppermute | solution.py:463
  574.7 183.8 %reduce-scatter.11.cloned.1.call-start = ((), (), s32[]{:S(2)}) async-start(), calls=%async_computation.6 | async-start | bytes 3317760 | tf_op jit(solution)/shard_map/reduce_scatter | solution.py:657
  604.5 58.0 %collective-permute-start.49 = (f32[4,144,1152]{2,1,0:T(8,128)}, f32[4,144,1152]{2,1,0:T(8,128)}, u32[]{:S(2)}, u32[]{:S(2)}) collective-permute-start(f32[4,144,1152]{2,1,0:T(8,128)} %pad_maximum_fusion.6), channel_id=1, source_target_pairs={{0,8},{4,12},{8,0},{12,4},{16,24},{20,28},{24,16},{28,20},{1,9},{5... | collective-permute-start | bytes 7962632 | tf_op jit(solution)/shard_map/ppermute | solution.py:467
  605.1 58.2 %collective-permute-start.50 = (f32[4,144,1152]{2,1,0:T(8,128)}, f32[4,144,1152]{2,1,0:T(8,128)}, u32[]{:S(2)}, u32[]{:S(2)}) collective-permute-start(f32[4,144,1152]{2,1,0:T(8,128)} %pad_maximum_fusion.7), channel_id=1, source_target_pairs={{0,16},{4,20},{8,24},{12,28},{16,0},{20,4},{24,8},{28,12},{1,17},{... | collective-permute-start | bytes 7962632 | tf_op jit(solution)/shard_map/ppermute | solution.py:471
  668.5 118.6 %reduce-scatter.13.cloned.1.call-start = ((), (), s32[]{:S(2)}) async-start(), calls=%async_computation.13 | async-start | bytes 1658880
  716.6 32.3 %collective-permute-start.55 = (f32[144,1152]{1,0:T(8,128)}, f32[144,1152]{1,0:T(8,128)S(1)}, u32[]{:S(2)}, u32[]{:S(2)}) collective-permute-start(f32[144,1152]{1,0:T(8,128)} %bitcast.104.refs_0_), channel_id=1, source_target_pairs={{0,8},{4,12},{8,0},{12,4},{16,24},{20,28},{24,16},{28,20},{1,9},{5... | collective-permute-start | bytes 1990664 | tf_op jit(solution)/shard_map/ppermute | solution.py:467
  718.1 30.8 %collective-permute-start.56 = (f32[144,1152]{1,0:T(8,128)}, f32[144,1152]{1,0:T(8,128)S(1)}, u32[]{:S(2)}, u32[]{:S(2)}) collective-permute-start(f32[144,1152]{1,0:T(8,128)} %bitcast.104.refs_0_), channel_id=1, source_target_pairs={{0,16},{4,20},{8,24},{12,28},{16,0},{20,4},{24,8},{28,12},{1,17},{... | collective-permute-start | bytes 1990664 | tf_op jit(solution)/shard_map/ppermute | solution.py:471
  758.5 76.8 %collective-permute-start.69 = (f32[576,1152]{1,0:T(8,128)}, f32[576,1152]{1,0:T(8,128)}, u32[]{:S(2)}, u32[]{:S(2)}) collective-permute-start(f32[576,1152]{1,0:T(8,128)} %shard_map.529.refs_0_), channel_id=1, source_target_pairs={{0,4},{4,0},{8,12},{12,8},{16,20},{20,16},{24,28},{28,24},{1,5},{5... | collective-permute-start | bytes 7962632 | tf_op jit(solution)/shard_map/ppermute | solution.py:463
  758.6 60.9 %collective-permute-start.59 = (f32[516,576]{1,0:T(8,128)}, f32[516,576]{1,0:T(8,128)}, u32[]{:S(2)}, u32[]{:S(2)}) collective-permute-start(f32[516,576]{1,0:T(8,128)} %fusion.42), channel_id=1, source_target_pairs={{0,2},{1,3},{2,0},{3,1},{4,6},{5,7},{6,4},{7,5},{8,10},{9,11},{10,... | collective-permute-start | bytes 3566600 | tf_op jit(solution)/shard_map/ppermute | solution.py:476
  762.1 57.3 %collective-permute-start.65 = (f32[144,1152]{1,0:T(8,128)}, f32[144,1152]{1,0:T(8,128)S(1)}, u32[]{:S(2)}, u32[]{:S(2)}) collective-permute-start(f32[144,1152]{1,0:T(8,128)} %bitcast.380), channel_id=1, source_target_pairs={{0,8},{4,12},{8,0},{12,4},{16,24},{20,28},{24,16},{28,20},{1,9},{5... | collective-permute-start | bytes 1990664 | tf_op jit(solution)/shard_map/ppermute | solution.py:467
  762.6 56.9 %collective-permute-start.66 = (f32[144,1152]{1,0:T(8,128)}, f32[144,1152]{1,0:T(8,128)}, u32[]{:S(2)}, u32[]{:S(2)}) collective-permute-start(f32[144,1152]{1,0:T(8,128)} %bitcast.381), channel_id=1, source_target_pairs={{0,16},{4,20},{8,24},{12,28},{16,0},{20,4},{24,8},{28,12},{1,17},{... | collective-permute-start | bytes 1990664 | tf_op jit(solution)/shard_map/ppermute | solution.py:471
  787.0 45.1 %collective-permute-start.71 = (f32[72,1152]{1,0:T(8,128)}, f32[72,1152]{1,0:T(8,128)}, u32[]{:S(2)}, u32[]{:S(2)}) collective-permute-start(f32[72,1152]{1,0:T(8,128)} %bitcast.383), channel_id=1, source_target_pairs={{0,8},{4,12},{8,0},{12,4},{16,24},{20,28},{24,16},{28,20},{1,9},{5... | collective-permute-start | bytes 995336 | tf_op jit(solution)/shard_map/ppermute | solution.py:467
  819.5 60.4 %collective-permute-start.74 = (f32[576,1152]{1,0:T(8,128)S(1)}, f32[576,1152]{1,0:T(8,128)}, u32[]{:S(2)}, u32[]{:S(2)}) collective-permute-start(f32[576,1152]{1,0:T(8,128)S(1)} %shard_map.530.refs_0_), channel_id=1, source_target_pairs={{0,4},{4,0},{8,12},{12,8},{16,20},{20,16},{24,28},{28,24},{1,5},{5... | collective-permute-start | bytes 7962632 | tf_op jit(solution)/shard_map/ppermute | solution.py:463
  833.6 32.4 %collective-permute-start.64 = (f32[516,576]{1,0:T(8,128)}, f32[516,576]{1,0:T(8,128)}, u32[]{:S(2)}, u32[]{:S(2)}) collective-permute-start(f32[516,576]{1,0:T(8,128)} %fusion.43), channel_id=1, source_target_pairs={{0,1},{1,2},{2,3},{3,0},{4,5},{5,6},{6,7},{7,4},{8,9},{9,10},{10,1... | collective-permute-start | bytes 3566600 | tf_op jit(solution)/shard_map/ppermute | solution.py:476
  845.7 63.0 %collective-permute-start.77 = (f32[576,1152]{1,0:T(8,128)}, f32[576,1152]{1,0:T(8,128)}, u32[]{:S(2)}, u32[]{:S(2)}) collective-permute-start(f32[576,1152]{1,0:T(8,128)} %shard_map.532.refs_0_), channel_id=1, source_target_pairs={{0,4},{4,0},{8,12},{12,8},{16,20},{20,16},{24,28},{28,24},{1,5},{5... | collective-permute-start | bytes 7962632 | tf_op jit(solution)/shard_map/ppermute | solution.py:463
  873.6 42.8 %collective-permute-start.78 = (f32[288,1152]{1,0:T(8,128)}, f32[288,1152]{1,0:T(8,128)}, u32[]{:S(2)}, u32[]{:S(2)}) collective-permute-start(f32[288,1152]{1,0:T(8,128)} %shard_map.533.refs_0_), channel_id=1, source_target_pairs={{0,4},{4,0},{8,12},{12,8},{16,20},{20,16},{24,28},{28,24},{1,5},{5... | collective-permute-start | bytes 3981320 | tf_op jit(solution)/shard_map/ppermute | solution.py:463
  919.3 43.6 %collective-permute-start.84 = (f32[6,2,1152]{2,1,0:T(2,128)S(1)}, f32[6,2,1152]{2,1,0:T(2,128)S(1)}, u32[]{:S(2)}, u32[]{:S(2)}) collective-permute-start(f32[6,2,1152]{2,1,0:T(2,128)S(1)} %pad_maximum_fusion.13.refs_0_), channel_id=1, source_target_pairs={{0,3},{1,0},{2,1},{3,2},{4,7},{5,4},{6,5},{7,6},{8,11},{9,8},{10,9... | collective-permute-start | bytes 165896 | tf_op jit(solution)/shard_map/ppermute | solution.py:476
  922.8 40.1 %collective-permute-start.83 = (f32[6,2,1152]{2,1,0:T(2,128)S(1)}, f32[6,2,1152]{2,1,0:T(2,128)S(1)}, u32[]{:S(2)}, u32[]{:S(2)}) collective-permute-start(f32[6,2,1152]{2,1,0:T(2,128)S(1)} %pad_maximum_fusion.13.refs_0_), channel_id=1, source_target_pairs={{0,2},{1,3},{2,0},{3,1},{4,6},{5,7},{6,4},{7,5},{8,10},{9,11},{10,... | collective-permute-start | bytes 165896 | tf_op jit(solution)/shard_map/ppermute | solution.py:476
  923.7 39.2 %collective-permute-start.82 = (f32[6,2,1152]{2,1,0:T(2,128)S(1)}, f32[6,2,1152]{2,1,0:T(2,128)S(1)}, u32[]{:S(2)}, u32[]{:S(2)}) collective-permute-start(f32[6,2,1152]{2,1,0:T(2,128)S(1)} %pad_maximum_fusion.13.refs_0_), channel_id=1, source_target_pairs={{0,1},{1,2},{2,3},{3,0},{4,5},{5,6},{6,7},{7,4},{8,9},{9,10},{10,1... | collective-permute-start | bytes 165896 | tf_op jit(solution)/shard_map/ppermute | solution.py:476
  (196 other events, 2909.4 us)
Sparse Core Ops, SparseCore 0:
  10.2 36.6 all-gather.12
  49.0 54.5 all-gather.14
  105.7 54.1 all-gather.16
  161.9 54.1 all-gather.18
  254.0 53.5 all-gather.20
  363.8 169.9 all-gather.22
  536.7 50.7 reduce-scatter.8
  590.4 52.3 reduce-scatter.6
  668.6 51.8 reduce-scatter.10
  723.2 31.3 reduce-scatter.12

commit v5 on v4

--- a/solution.py
+++ b/solution.py
@@ -1315,6 +1315,7 @@
         )
 
     stay, turn_one, turn_two, turn_three = [input_product(shift) for shift in range(4)]
+    turn_one = turn_mp(order.after(turn_one), 1)
     attn_add = order.mark(*attn_add)
     attn_sides = swap_plane(order, *order.mark(*cut_sides(attn_grad, quarter, *attn_add)))
     skip_given = order.mark(skip_given)
@@ -1339,6 +1340,7 @@
     small_core = to_core(small)
     attn_sides = order.mark(*attn_sides)
     attn_piece = sum_deep(order, attn_grad, quarter, *attn_sides)
+    turn_one = order.mark(turn_one)
     fc1_piece = order.mark(fc1_piece)
     skip_add = order.mark(*skip_add)
     skip_sides = swap_plane(order, *order.mark(*cut_sides(skip_grad, quarter, *skip_add)))
@@ -1402,31 +1404,29 @@
     fc2_held = order.mark(hold(fc2_piece, fc2_near, fc2_far))
     fc2_other = to_core(fc2_held)
     fc1_far = order.mark(*fc1_far)
+    fc1_held = order.mark(hold(fc1_piece, fc1_near, fc1_far))
     skip_piece = order.mark(skip_piece)
     skip_near = spread(skip_piece)
-    turn_two = order.mark(turn_two)
-    turn_one = turn_mp(order.after(turn_one), 1)
-    fc1_held = order.mark(hold(fc1_piece, fc1_near, fc1_far))
     attn_near = order.mark(*attn_near)
     attn_far = spread_far(attn_near)
-    fc1_other = to_core(order.after(fc1_held))
+    fc2_sum, fc2_moments = order.mark(
+        *interleave(fc2_held, order.mark(fc2_other), own_state(fc2_rows)[None])
+    )
     skip_near = order.mark(*skip_near)
     skip_far = spread_far(skip_near)
+    attn_far = order.mark(*attn_far)
+    attn_held = order.mark(hold(attn_piece, attn_near, attn_far))
+    attn_other = to_core(attn_held)
+    turn_two = order.mark(turn_two)
+    turn_three = turn_mp(order.after(turn_three), 3)
+    fc1_other = to_core(order.after(fc1_held))
+    skip_far = order.mark(*skip_far)
+    skip_held = order.mark(hold(skip_piece, skip_near, skip_far))
+    skip_other = to_core(skip_held)
     small = order.mark(small + order.mark(small_y))
     small = jnp.concatenate(
         [small, weight_sq, jnp.zeros((D - 6,), jnp.float32)], 0
     ).reshape(6, 2, D)
-    fc2_sum, fc2_moments = order.mark(
-        *interleave(fc2_held, order.mark(fc2_other), own_state(fc2_rows)[None])
-    )
-    attn_far = order.mark(*attn_far)
-    attn_held = order.mark(hold(attn_piece, attn_near, attn_far))
-    attn_other = to_core(attn_held)
-    turn_one = order.mark(turn_one)
-    turn_three = turn_mp(order.after(turn_three), 3)
-    skip_far = order.mark(*skip_far)
-    skip_held = order.mark(hold(skip_piece, skip_near, skip_far))
-    skip_other = to_core(skip_held)
     fc1_sum, fc1_moments = order.mark(
         *interleave(fc1_held, order.mark(fc1_other), own_state(fc1_cols)[None])
     )

time: 1030 us -> 1010 us (0.981)
  waiting for transfers between devices: 337 us -> 310 us
    ppermute x18, waiting for transfers between devices: 53.9 us -> 22.8 us  [turn_mp(): lax.ppermute(array, 'mp', [(i, (i + shift) % count) for i in range(count)])]
    unnamed x319 -> x301, local copies, waits for them, and re-layouts: 99.1 us -> 92.5 us
  transfers between devices with their start and end apart: 101 -> 101, of which waited for: 43 -> 44; matrix products, arithmetic and copies ran while one was open for 34% -> 35% of each run, Pallas kernels for 10% -> 10%
where the time goes in v5:
time: 1010 us; the launch traced here: 1000 us
  waiting for transfers between devices  310 us (31%)
  local copies, waits for them, and re-layouts  212 us (21%)
  Pallas kernels  132 us (13%)
  other arithmetic  120 us (12%)
  matrix products  115 us (11%)
  starting transfers between devices  89.5 us (9%)
  between operations  21.1 us (2%)
    ppermute x25, waiting for transfers between devices, to_x(): return lax.ppermute(array, 'dp', [(i, i ^ 2) for i in range(8)])  214 us
    unnamed x301, local copies, waits for them, and re-layouts  92.5 us
    ppermute x25, waiting for transfers between devices, to_y(): return lax.ppermute(array, 'dp', [(i, i ^ 4) for i in range(8)])  45.7 us
    dot_general x5, matrix products, matmul(): return jnp.dot(left_side, right_side, preferred_element_type=jnp.float32)  37.6 us
    ppermute x25, starting transfers between devices, to_y(): return lax.ppermute(array, 'dp', [(i, i ^ 4) for i in range(8)])  32 us
    pallas_call x4, Pallas kernels, assemble(): pl.pallas_call(kernel, in_specs=[pl.BlockSpec(memory_space=pltpu.SMEM)] +...  30 us
    pallas_call x8, Pallas kernels, place_rows(): pl.pallas_call(kernel, in_specs=in_specs, out_specs=out_specs, out_shape=...  27.1 us
    ppermute x18, starting transfers between devices, turn_mp(): lax.ppermute(array, 'mp', [(i, (i + shift) % count) for i in range(count)])  26.4 us
  transfers between devices with their start and end apart: 101, of which 44 were waited for; matrix products, arithmetic and copies ran while one was open for 35% of the time, Pallas kernels for 10%

profile of v5, /device:TPU:0, one launch (start us, length us, event | category | flops | bytes accessed | tf_op | source)
XLA Modules:
  0.0 1000.1 jit_solution(15825121892981474557)
XLA Ops:
  34.8 6.9 copy.138
  58.0 16.4 %collective-permute-done.4.refs_3_ = f32[3,72,1152]{2,1,0:T(8,128)} collective-permute-done((f32[3,72,1152]{2,1,0:T(8,128)}, f32[3,72,1152]{2,1,0:T(8,128)}, u32[]{:S(2)}, u32[]{:S(2)}) %collective-permute-start.4) | collective-permute-done | bytes 995360 | tf_op jit(solution)/shard_map/ppermute | solution.py:467
  79.7 5.8 collective-permute-done.12.refs_9_
  85.5 5.4 collective-permute-done.11.refs_7_
  94.7 8.9 all-gather.15.cloned.1.call-done
  109.6 6.5 shard_map.521
  145.8 6.2 collective-permute-done.16.refs_3_
  164.9 13.3 %collective-permute-done.20.refs_7_ = f32[1,144,1152]{2,1,0:T(8,128)} collective-permute-done((f32[1,144,1152]{2,1,0:T(8,128)S(1)}, f32[1,144,1152]{2,1,0:T(8,128)}, u32[]{:S(2)}, u32[]{:S(2)}) %collective-permute-start.20) | collective-permute-done | bytes 663584 | tf_op jit(solution)/shard_map/ppermute | solution.py:467
  178.2 8.4 collective-permute-done.21.refs_9_
  196.5 10.5 %shard_map.522 = (bf16[12,288,1152]{2,1,0:T(8,128)(2,1)}, bf16[4,288,1152]{2,1,0:T(8,128)(2,1)S(1)}) custom-call(s32[17]{0:T(128)S(1)} %stack.384.table_ref, f32[4,288,1152]{2,1,0:T(8,128)} %bitcast.394, f32[3,144,1152]{2,1,0:T(8,128)} %fusion.7.refs_1_, f32[3,144,1152]{2,1,0:T(8,128)} %collective-permute-done.15.refs_2_, ...), custom_call_target="tpu_custom_call" | custom-call | bytes 1024 | tf_op jit(solution)/shard_map/pallas_call | solution.py:553
  208.5 8.6 convolution_convert_fusion.qkv_ref
  217.0 9.2 shard_map.523
  229.4 6.2 fusion
  260.7 6.0 collective-permute-done.29.refs_5_
  266.7 13.7 %collective-permute-done.28.refs_4_ = f32[2,144,1152]{2,1,0:T(8,128)} collective-permute-done((f32[2,144,1152]{2,1,0:T(8,128)}, f32[2,144,1152]{2,1,0:T(8,128)}, u32[]{:S(2)}, u32[]{:S(2)}) %collective-permute-start.28) | collective-permute-done | bytes 1327136 | tf_op jit(solution)/shard_map/ppermute | solution.py:467
  280.4 6.2 shard_map.524
  290.9 9.4 multiply_convert_fusion
  300.3 8.0 fusion.35
  313.9 8.6 collective-permute-done.30.refs_2_
  330.5 6.8 shard_map.525
  337.3 8.5 fusion.36
  348.2 13.3 %fusion.31 = (f32[2304]{0:T(1024)S(1)}, bf16[1032,2304]{1,0:T(8,128)(2,1)}) fusion(f32[1032,2304]{1,0:T(8,128)S(1)} %bitcast.441, bf16[1032,1152]{1,0:T(8,128)(2,1)S(1)} %copy-done.81, bf16[2304,1152]{1,0:T(8,128)(2,1)S(1)} %bitcast.376), kind=kOutput, calls=%fused_computation.237 | convolution fusion | flops 5511571456 | bytes 21961728 | tf_op jit(solution)/shard_map/td,fd->tf/dot_general | solution.py:1243
  363.7 13.4 %collective-permute-done.33 = f32[2,144,1152]{2,1,0:T(8,128)} collective-permute-done((f32[2,144,1152]{2,1,0:T(8,128)}, f32[2,144,1152]{2,1,0:T(8,128)}, u32[]{:S(2)}, u32[]{:S(2)}) %collective-permute-start.33) | collective-permute-done | bytes 1327136 | tf_op jit(solution)/shard_map/ppermute | solution.py:467
  384.0 9.0 fusion.37
  396.2 7.9 fusion.38
  425.7 16.9 %shard_map.526 = bf16[2,258,3456]{2,1,0:T(8,128)(2,1)S(1)} custom-call(bf16[2,258,3456]{2,1,0:T(8,128)(2,1)S(1)} %copy-done.15, bf16[2,258,1152]{2,1,0:T(8,128)(2,1)S(1)} %reshape.350.grad_ref), custom_call_target="tpu_custom_call" | custom-call | bytes 1024 | tf_op jit(solution)/shard_map/pallas_call | solution.py:1020
  455.5 5.3 fusion.3
  460.8 9.1 fusion.39
  495.3 10.4 %multiply_reduce_fusion.5 = (f32[1152]{0:T(1024)S(1)}, f32[516]{0:T(1024)S(1)}, f32[516]{0:T(1024)S(1)}, f32[1152]{0:T(1024)S(1)}, f32[516,1152]{1,0:T(8,128)S(1)}) fusion(f32[516,1152]{1,0:T(8,128)} %get-tuple-element.449, f32[1152]{0:T(1024)S(1)} %copy-done.97, bf16[516,3456]{1,0:T(8,128)(2,1)} %reshape.351, bf16[3456,1152]{1,0:T(8,128)(2,1)} %bitcast.431), kind=kOutput, calls=%fused_computation.44 | convolution fusion | flops 4112871936 | bytes 16302624 | tf_op jit(solution)/shard_map/dot_general | solution.py:30
  525.0 8.8 all-gather.23.cloned.1.call-done
  536.3 14.6 %shard_map.527 = f32[16,144,1152]{2,1,0:T(8,128)} custom-call(s32[1]{0:T(128)} %bitcast.26.core_ref, f32[12,2,144,1152]{3,2,1,0:T(8,128)} %bitcast.392, f32[4,2,144,1152]{3,2,1,0:T(8,128)S(1)} %copy-done.22, f32[12,144,1152]{2,1,0:T(8,128)} %collective-permute-done.41.refs_2_, f32[4,144,1152]{2,1,0:T(8,128)S(1)} %collective-permute-done.42.refs_3_), custom_call_target="tpu_custom_call" | custom-call | bytes 1024 | tf_op jit(solution)/shard_map/pallas_call | solution.py:753
  555.5 10.7 %collective-permute-done.45 = f32[4,144,1152]{2,1,0:T(8,128)} collective-permute-done((f32[4,144,1152]{2,1,0:T(8,128)}, f32[4,144,1152]{2,1,0:T(8,128)}, u32[]{:S(2)}, u32[]{:S(2)}) %collective-permute-start.45) | collective-permute-done | bytes 2654240 | tf_op jit(solution)/shard_map/ppermute | solution.py:467
  569.4 5.2 fusion.2
  581.2 15.9 %collective-permute-done.43 = f32[2,144,1152]{2,1,0:T(8,128)S(1)} collective-permute-done((f32[2,144,1152]{2,1,0:T(8,128)}, f32[2,144,1152]{2,1,0:T(8,128)S(1)}, u32[]{:S(2)}, u32[]{:S(2)}) %collective-permute-start.43) | collective-permute-done | bytes 1327136 | tf_op jit(solution)/shard_map/ppermute | solution.py:467
  607.2 9.5 shard_map.528
  619.3 43.1 %collective-permute-done.50 = f32[4,144,1152]{2,1,0:T(8,128)} collective-permute-done((f32[4,144,1152]{2,1,0:T(8,128)}, f32[4,144,1152]{2,1,0:T(8,128)}, u32[]{:S(2)}, u32[]{:S(2)}) %collective-permute-start.50) | collective-permute-done | bytes 2654240 | tf_op jit(solution)/shard_map/ppermute | solution.py:467
  663.2 5.3 fusion.1
  671.1 12.1 %collective-permute-done.47 = f32[2,72,1152]{2,1,0:T(8,128)} collective-permute-done((f32[2,72,1152]{2,1,0:T(8,128)}, f32[2,72,1152]{2,1,0:T(8,128)}, u32[]{:S(2)}, u32[]{:S(2)}) %collective-permute-start.47) | collective-permute-done | bytes 663584 | tf_op jit(solution)/shard_map/ppermute | solution.py:467
  690.2 23.2 %collective-permute-done.52 = f32[4,72,1152]{2,1,0:T(8,128)S(1)} collective-permute-done((f32[4,72,1152]{2,1,0:T(8,128)S(1)}, f32[4,72,1152]{2,1,0:T(8,128)S(1)}, u32[]{:S(2)}, u32[]{:S(2)}) %collective-permute-start.52) | collective-permute-done | bytes 1327136 | tf_op jit(solution)/shard_map/ppermute | solution.py:467
  720.9 6.8 add_convert_fusion
  732.2 11.6 %collective-permute-done.58.refs_1_ = f32[144,1152]{1,0:T(8,128)S(1)} collective-permute-done((f32[144,1152]{1,0:T(8,128)S(1)}, f32[144,1152]{1,0:T(8,128)S(1)}, u32[]{:S(2)}, u32[]{:S(2)}) %collective-permute-start.58) | collective-permute-done | bytes 663584 | tf_op jit(solution)/shard_map/ppermute | solution.py:467
  749.1 5.6 collective-permute-done.61.refs_3_
  764.6 7.1 collective-permute-done.65.refs_3_
  773.2 13.6 %collective-permute-done.66.refs_4_ = f32[72,1152]{1,0:T(8,128)S(1)} collective-permute-done((f32[72,1152]{1,0:T(8,128)S(1)}, f32[72,1152]{1,0:T(8,128)S(1)}, u32[]{:S(2)}, u32[]{:S(2)}) %collective-permute-start.66) | collective-permute-done | bytes 331808 | tf_op jit(solution)/shard_map/ppermute | solution.py:471
  790.7 7.7 reduce-scatter.13.cloned.1.call-done
  818.5 17.1 %collective-permute-done.60.refs_2_ = f32[516,576]{1,0:T(8,128)} collective-permute-done((f32[516,576]{1,0:T(8,128)}, f32[516,576]{1,0:T(8,128)}, u32[]{:S(2)}, u32[]{:S(2)}) %collective-permute-start.60) | collective-permute-done | bytes 1188896 | tf_op jit(solution)/shard_map/ppermute | solution.py:476
  862.5 5.7 collective-permute-done.72.refs_3_
  986.6 5.3 shard_map.545
  (742 shorter events, 485.6 us)
Async XLA Ops:
  7.2 42.1 %all-gather.13.cloned.1.call-start = ((), (), s32[]{:S(2)}) async-start(), calls=%async_computation.7 | async-start | bytes 1658880 | tf_op jit(solution)/shard_map/all_gather | solution.py:608
  9.1 94.5 %all-gather.15.cloned.1.call-start = ((), (), s32[]{:S(2)}) async-start(), calls=%async_computation.8 | async-start | bytes 3317760 | tf_op jit(solution)/shard_map/all_gather | solution.py:608
  15.3 149.6 %all-gather.17.cloned.1.call-start = ((), (), s32[]{:S(2)}) async-start(), calls=%async_computation.9 | async-start | bytes 3317760 | tf_op jit(solution)/shard_map/all_gather | solution.py:608
  17.3 31.8 %collective-permute-start.86 = (f32[1152]{0:T(1024)S(1)}, f32[1152]{0:T(1024)S(1)}, u32[]{:S(2)}, u32[]{:S(2)}) collective-permute-start(f32[1152]{0:T(1024)S(1)} %copy-done.107), channel_id=1, source_target_pairs={{0,2},{1,3},{2,0},{3,1},{4,6},{5,7},{6,4},{7,5},{8,10},{9,11},{10,... | collective-permute-start | bytes 13832 | tf_op jit(solution)/shard_map/ppermute | solution.py:476
  94.1 147.5 %all-gather.19.cloned.1.call-start = ((), (), s32[]{:S(2)}) async-start(), calls=%async_computation.10 | async-start | bytes 3317760 | tf_op jit(solution)/shard_map/all_gather | solution.py:608
  106.6 45.4 %collective-permute-start.16 = (f32[3,144,1152]{2,1,0:T(8,128)}, f32[3,144,1152]{2,1,0:T(8,128)}, u32[]{:S(2)}, u32[]{:S(2)}) collective-permute-start(f32[3,144,1152]{2,1,0:T(8,128)} %fusion.7.refs_1_), channel_id=1, source_target_pairs={{0,8},{4,12},{8,0},{12,4},{16,24},{20,28},{24,16},{28,20},{1,9},{5... | collective-permute-start | bytes 5971976 | tf_op jit(solution)/shard_map/ppermute | solution.py:467
  108.1 45.1 %collective-permute-start.17 = (f32[3,144,1152]{2,1,0:T(8,128)}, f32[3,144,1152]{2,1,0:T(8,128)}, u32[]{:S(2)}, u32[]{:S(2)}) collective-permute-start(f32[3,144,1152]{2,1,0:T(8,128)} %fusion.7.refs_1_), channel_id=1, source_target_pairs={{0,16},{4,20},{8,24},{12,28},{16,0},{20,4},{24,8},{28,12},{1,17},{... | collective-permute-start | bytes 5971976 | tf_op jit(solution)/shard_map/ppermute | solution.py:471
  122.4 38.4 %collective-permute-start.22 = (f32[516,1152]{1,0:T(8,128)}, f32[516,1152]{1,0:T(8,128)}, u32[]{:S(2)}, u32[]{:S(2)}) collective-permute-start(f32[516,1152]{1,0:T(8,128)} %convert_multiply_fusion), channel_id=1, source_target_pairs={{0,4},{4,0},{8,12},{12,8},{16,20},{20,16},{24,28},{28,24},{1,5},{5... | collective-permute-start | bytes 7133192 | tf_op jit(solution)/shard_map/ppermute | solution.py:463
  160.1 165.1 %all-gather.21.cloned.1.call-start = ((), (), s32[]{:S(2)}) async-start(), calls=%async_computation.11 | async-start | bytes 3317760 | tf_op jit(solution)/shard_map/all_gather | solution.py:608
  160.3 35.1 %collective-permute-start.19 = (f32[3,144,1152]{2,1,0:T(8,128)}, f32[3,144,1152]{2,1,0:T(8,128)}, u32[]{:S(2)}, u32[]{:S(2)}) collective-permute-start(f32[3,144,1152]{2,1,0:T(8,128)} %collective-permute-done.17.refs_5_), channel_id=1, source_target_pairs={{0,4},{4,0},{8,12},{12,8},{16,20},{20,16},{24,28},{28,24},{1,5},{5... | collective-permute-start | bytes 5971976 | tf_op jit(solution)/shard_map/ppermute | solution.py:463
  160.8 34.6 %collective-permute-start.18 = (f32[3,144,1152]{2,1,0:T(8,128)}, f32[3,144,1152]{2,1,0:T(8,128)}, u32[]{:S(2)}, u32[]{:S(2)}) collective-permute-start(f32[3,144,1152]{2,1,0:T(8,128)} %collective-permute-done.16.refs_3_), channel_id=1, source_target_pairs={{0,4},{4,0},{8,12},{12,8},{16,20},{20,16},{24,28},{28,24},{1,5},{5... | collective-permute-start | bytes 5971976 | tf_op jit(solution)/shard_map/ppermute | solution.py:463
  189.0 46.6 %collective-permute-start.25 = (f32[3,144,1152]{2,1,0:T(8,128)S(1)}, f32[3,144,1152]{2,1,0:T(8,128)}, u32[]{:S(2)}, u32[]{:S(2)}) collective-permute-start(f32[3,144,1152]{2,1,0:T(8,128)S(1)} %fusion.6.refs_1_), channel_id=1, source_target_pairs={{0,8},{4,12},{8,0},{12,4},{16,24},{20,28},{24,16},{28,20},{1,9},{5... | collective-permute-start | bytes 5971976 | tf_op jit(solution)/shard_map/ppermute | solution.py:467
  191.3 45.7 %collective-permute-start.26 = (f32[3,144,1152]{2,1,0:T(8,128)S(1)}, f32[3,144,1152]{2,1,0:T(8,128)}, u32[]{:S(2)}, u32[]{:S(2)}) collective-permute-start(f32[3,144,1152]{2,1,0:T(8,128)S(1)} %fusion.6.refs_1_), channel_id=1, source_target_pairs={{0,16},{4,20},{8,24},{12,28},{16,0},{20,4},{24,8},{28,12},{1,17},{... | collective-permute-start | bytes 5971976 | tf_op jit(solution)/shard_map/ppermute | solution.py:471
  248.1 38.5 %collective-permute-start.27 = (f32[516,1152]{1,0:T(8,128)}, f32[516,1152]{1,0:T(8,128)}, u32[]{:S(2)}, u32[]{:S(2)}) collective-permute-start(f32[516,1152]{1,0:T(8,128)} %get-tuple-element.394), channel_id=1, source_target_pairs={{0,4},{4,0},{8,12},{12,8},{16,20},{20,16},{24,28},{28,24},{1,5},{5... | collective-permute-start | bytes 7133192 | tf_op jit(solution)/shard_map/ppermute | solution.py:463
  248.2 32.2 %collective-permute-start.28 = (f32[2,144,1152]{2,1,0:T(8,128)}, f32[2,144,1152]{2,1,0:T(8,128)}, u32[]{:S(2)}, u32[]{:S(2)}) collective-permute-start(f32[2,144,1152]{2,1,0:T(8,128)} %slice.351), channel_id=1, source_target_pairs={{0,8},{4,12},{8,0},{12,4},{16,24},{20,28},{24,16},{28,20},{1,9},{5... | collective-permute-start | bytes 3981320 | tf_op jit(solution)/shard_map/ppermute | solution.py:467
  253.9 279.9 %all-gather.23.cloned.1.call-start = ((), (), s32[]{:S(2)}) async-start(), calls=%async_computation.12 | async-start | bytes 12165120 | tf_op jit(solution)/shard_map/all_gather | solution.py:1251
  258.6 63.9 %collective-permute-start.30 = (f32[3,144,1152]{2,1,0:T(8,128)S(1)}, f32[3,144,1152]{2,1,0:T(8,128)S(1)}, u32[]{:S(2)}, u32[]{:S(2)}) collective-permute-start(f32[3,144,1152]{2,1,0:T(8,128)S(1)} %fusion.5.refs_1_), channel_id=1, source_target_pairs={{0,8},{4,12},{8,0},{12,4},{16,24},{20,28},{24,16},{28,20},{1,9},{5... | collective-permute-start | bytes 5971976 | tf_op jit(solution)/shard_map/ppermute | solution.py:467
  260.1 63.7 %collective-permute-start.31 = (f32[3,144,1152]{2,1,0:T(8,128)S(1)}, f32[3,144,1152]{2,1,0:T(8,128)S(1)}, u32[]{:S(2)}, u32[]{:S(2)}) collective-permute-start(f32[3,144,1152]{2,1,0:T(8,128)S(1)} %fusion.5.refs_1_), channel_id=1, source_target_pairs={{0,16},{4,20},{8,24},{12,28},{16,0},{20,4},{24,8},{28,12},{1,17},{... | collective-permute-start | bytes 5971976 | tf_op jit(solution)/shard_map/ppermute | solution.py:471
  346.0 31.1 %collective-permute-start.33 = (f32[2,144,1152]{2,1,0:T(8,128)}, f32[2,144,1152]{2,1,0:T(8,128)}, u32[]{:S(2)}, u32[]{:S(2)}) collective-permute-start(f32[2,144,1152]{2,1,0:T(8,128)} %get-tuple-element.418), channel_id=1, source_target_pairs={{0,8},{4,12},{8,0},{12,4},{16,24},{20,28},{24,16},{28,20},{1,9},{5... | collective-permute-start | bytes 3981320 | tf_op jit(solution)/shard_map/ppermute | solution.py:467
  346.7 30.8 %collective-permute-start.34 = (f32[2,144,1152]{2,1,0:T(8,128)}, f32[2,144,1152]{2,1,0:T(8,128)}, u32[]{:S(2)}, u32[]{:S(2)}) collective-permute-start(f32[2,144,1152]{2,1,0:T(8,128)} %get-tuple-element.419), channel_id=1, source_target_pairs={{0,16},{4,20},{8,24},{12,28},{16,0},{20,4},{24,8},{28,12},{1,17},{... | collective-permute-start | bytes 3981320 | tf_op jit(solution)/shard_map/ppermute | solution.py:471
  363.7 255.7 %reduce-scatter.9.cloned.1.call-start = ((), (), s32[]{:S(2)}) async-start(), calls=%async_computation.5 | async-start | bytes 3317760 | tf_op jit(solution)/shard_map/reduce_scatter | solution.py:657
  393.3 60.7 %collective-permute-start.38 = (f32[4,144,1152]{2,1,0:T(8,128)}, f32[4,144,1152]{2,1,0:T(8,128)}, u32[]{:S(2)}, u32[]{:S(2)}) collective-permute-start(f32[4,144,1152]{2,1,0:T(8,128)} %pad_maximum_fusion.2), channel_id=1, source_target_pairs={{0,8},{4,12},{8,0},{12,4},{16,24},{20,28},{24,16},{28,20},{1,9},{5... | collective-permute-start | bytes 7962632 | tf_op jit(solution)/shard_map/ppermute | solution.py:467
  394.8 60.7 %collective-permute-start.39 = (f32[4,144,1152]{2,1,0:T(8,128)}, f32[4,144,1152]{2,1,0:T(8,128)}, u32[]{:S(2)}, u32[]{:S(2)}) collective-permute-start(f32[4,144,1152]{2,1,0:T(8,128)} %pad_maximum_fusion.3), channel_id=1, source_target_pairs={{0,16},{4,20},{8,24},{12,28},{16,0},{20,4},{24,8},{28,12},{1,17},{... | collective-permute-start | bytes 7962632 | tf_op jit(solution)/shard_map/ppermute | solution.py:471
  409.3 72.7 %collective-permute-start.36 = (f32[2,144,1152]{2,1,0:T(8,128)}, f32[2,144,1152]{2,1,0:T(8,128)}, u32[]{:S(2)}, u32[]{:S(2)}) collective-permute-start(f32[2,144,1152]{2,1,0:T(8,128)} %get-tuple-element.434), channel_id=1, source_target_pairs={{0,8},{4,12},{8,0},{12,4},{16,24},{20,28},{24,16},{28,20},{1,9},{5... | collective-permute-start | bytes 3981320 | tf_op jit(solution)/shard_map/ppermute | solution.py:467
  409.9 73.3 %collective-permute-start.37 = (f32[2,144,1152]{2,1,0:T(8,128)}, f32[2,144,1152]{2,1,0:T(8,128)}, u32[]{:S(2)}, u32[]{:S(2)}) collective-permute-start(f32[2,144,1152]{2,1,0:T(8,128)} %get-tuple-element.435), channel_id=1, source_target_pairs={{0,16},{4,20},{8,24},{12,28},{16,0},{20,4},{24,8},{28,12},{1,17},{... | collective-permute-start | bytes 3981320 | tf_op jit(solution)/shard_map/ppermute | solution.py:471
  489.4 44.4 %collective-permute-start.41 = (f32[12,144,1152]{2,1,0:T(8,128)}, f32[12,144,1152]{2,1,0:T(8,128)}, u32[]{:S(2)}, u32[]{:S(2)}) collective-permute-start(f32[12,144,1152]{2,1,0:T(8,128)} %dynamic-slice_bitcast_fusion), channel_id=1, source_target_pairs={{0,4},{4,0},{8,12},{12,8},{16,20},{20,16},{24,28},{28,24},{1,5},{5... | collective-permute-start | bytes 23887880 | tf_op jit(solution)/shard_map/ppermute | solution.py:463
  494.7 176.4 %reduce-scatter.7.cloned.1.call-start = ((), (), s32[]{:S(2)}) async-start(), calls=%async_computation.4 | async-start | bytes 3317760 | tf_op jit(solution)/shard_map/reduce_scatter | solution.py:657
  494.7 39.1 %collective-permute-start.42 = (f32[4,144,1152]{2,1,0:T(8,128)}, f32[4,144,1152]{2,1,0:T(8,128)S(1)}, u32[]{:S(2)}, u32[]{:S(2)}) collective-permute-start(f32[4,144,1152]{2,1,0:T(8,128)} %dynamic-slice_bitcast_fusion.2), channel_id=1, source_target_pairs={{0,4},{4,0},{8,12},{12,8},{16,20},{20,16},{24,28},{28,24},{1,5},{5... | collective-permute-start | bytes 7962632 | tf_op jit(solution)/shard_map/ppermute | solution.py:463
  505.8 60.4 %collective-permute-start.45 = (f32[4,144,1152]{2,1,0:T(8,128)}, f32[4,144,1152]{2,1,0:T(8,128)}, u32[]{:S(2)}, u32[]{:S(2)}) collective-permute-start(f32[4,144,1152]{2,1,0:T(8,128)} %pad_maximum_fusion.4), channel_id=1, source_target_pairs={{0,8},{4,12},{8,0},{12,4},{16,24},{20,28},{24,16},{28,20},{1,9},{5... | collective-permute-start | bytes 7962632 | tf_op jit(solution)/shard_map/ppermute | solution.py:467
  506.4 60.0 %collective-permute-start.46 = (f32[4,144,1152]{2,1,0:T(8,128)}, f32[4,144,1152]{2,1,0:T(8,128)}, u32[]{:S(2)}, u32[]{:S(2)}) collective-permute-start(f32[4,144,1152]{2,1,0:T(8,128)} %pad_maximum_fusion.5), channel_id=1, source_target_pairs={{0,16},{4,20},{8,24},{12,28},{16,0},{20,4},{24,8},{28,12},{1,17},{... | collective-permute-start | bytes 7962632 | tf_op jit(solution)/shard_map/ppermute | solution.py:471
  520.3 86.9 %collective-permute-start.40 = (f32[16,72,1152]{2,1,0:T(8,128)}, f32[16,72,1152]{2,1,0:T(8,128)}, u32[]{:S(2)}, u32[]{:S(2)}) collective-permute-start(f32[16,72,1152]{2,1,0:T(8,128)} %dynamic-slice_bitcast_fusion.1), channel_id=1, source_target_pairs={{0,4},{4,0},{8,12},{12,8},{16,20},{20,16},{24,28},{28,24},{1,5},{5... | collective-permute-start | bytes 15925256 | tf_op jit(solution)/shard_map/ppermute | solution.py:463
  574.6 184.2 %reduce-scatter.11.cloned.1.call-start = ((), (), s32[]{:S(2)}) async-start(), calls=%async_computation.6 | async-start | bytes 3317760 | tf_op jit(solution)/shard_map/reduce_scatter | solution.py:657
  604.4 58.0 %collective-permute-start.50 = (f32[4,144,1152]{2,1,0:T(8,128)}, f32[4,144,1152]{2,1,0:T(8,128)}, u32[]{:S(2)}, u32[]{:S(2)}) collective-permute-start(f32[4,144,1152]{2,1,0:T(8,128)} %pad_maximum_fusion.6), channel_id=1, source_target_pairs={{0,8},{4,12},{8,0},{12,4},{16,24},{20,28},{24,16},{28,20},{1,9},{5... | collective-permute-start | bytes 7962632 | tf_op jit(solution)/shard_map/ppermute | solution.py:467
  605.0 58.2 %collective-permute-start.51 = (f32[4,144,1152]{2,1,0:T(8,128)}, f32[4,144,1152]{2,1,0:T(8,128)}, u32[]{:S(2)}, u32[]{:S(2)}) collective-permute-start(f32[4,144,1152]{2,1,0:T(8,128)} %pad_maximum_fusion.7), channel_id=1, source_target_pairs={{0,16},{4,20},{8,24},{12,28},{16,0},{20,4},{24,8},{28,12},{1,17},{... | collective-permute-start | bytes 7962632 | tf_op jit(solution)/shard_map/ppermute | solution.py:471
  607.1 63.9 %collective-permute-start.49 = (f32[516,576]{1,0:T(8,128)}, f32[516,576]{1,0:T(8,128)S(1)}, u32[]{:S(2)}, u32[]{:S(2)}) collective-permute-start(f32[516,576]{1,0:T(8,128)} %fusion.43), channel_id=1, source_target_pairs={{0,1},{1,2},{2,3},{3,0},{4,5},{5,6},{6,7},{7,4},{8,9},{9,10},{10,1... | collective-permute-start | bytes 3566600 | tf_op jit(solution)/shard_map/ppermute | solution.py:476
  668.5 129.9 %reduce-scatter.13.cloned.1.call-start = ((), (), s32[]{:S(2)}) async-start(), calls=%async_computation.13 | async-start | bytes 1658880
  716.8 32.3 %collective-permute-start.56 = (f32[144,1152]{1,0:T(8,128)}, f32[144,1152]{1,0:T(8,128)S(1)}, u32[]{:S(2)}, u32[]{:S(2)}) collective-permute-start(f32[144,1152]{1,0:T(8,128)} %bitcast.104.refs_0_), channel_id=1, source_target_pairs={{0,8},{4,12},{8,0},{12,4},{16,24},{20,28},{24,16},{28,20},{1,9},{5... | collective-permute-start | bytes 1990664 | tf_op jit(solution)/shard_map/ppermute | solution.py:467
  718.3 30.9 %collective-permute-start.57 = (f32[144,1152]{1,0:T(8,128)}, f32[144,1152]{1,0:T(8,128)S(1)}, u32[]{:S(2)}, u32[]{:S(2)}) collective-permute-start(f32[144,1152]{1,0:T(8,128)} %bitcast.104.refs_0_), channel_id=1, source_target_pairs={{0,16},{4,20},{8,24},{12,28},{16,0},{20,4},{24,8},{28,12},{1,17},{... | collective-permute-start | bytes 1990664 | tf_op jit(solution)/shard_map/ppermute | solution.py:471
  758.8 46.3 %collective-permute-start.71 = (f32[576,1152]{1,0:T(8,128)}, f32[576,1152]{1,0:T(8,128)}, u32[]{:S(2)}, u32[]{:S(2)}) collective-permute-start(f32[576,1152]{1,0:T(8,128)} %shard_map.529.refs_0_), channel_id=1, source_target_pairs={{0,4},{4,0},{8,12},{12,8},{16,20},{20,16},{24,28},{28,24},{1,5},{5... | collective-permute-start | bytes 7962632 | tf_op jit(solution)/shard_map/ppermute | solution.py:463
  758.9 76.7 %collective-permute-start.60 = (f32[516,576]{1,0:T(8,128)}, f32[516,576]{1,0:T(8,128)}, u32[]{:S(2)}, u32[]{:S(2)}) collective-permute-start(f32[516,576]{1,0:T(8,128)} %fusion.42), channel_id=1, source_target_pairs={{0,2},{1,3},{2,0},{3,1},{4,6},{5,7},{6,4},{7,5},{8,10},{9,11},{10,... | collective-permute-start | bytes 3566600 | tf_op jit(solution)/shard_map/ppermute | solution.py:476
  762.5 39.0 %collective-permute-start.63 = (f32[144,1152]{1,0:T(8,128)}, f32[144,1152]{1,0:T(8,128)S(1)}, u32[]{:S(2)}, u32[]{:S(2)}) collective-permute-start(f32[144,1152]{1,0:T(8,128)} %bitcast.380), channel_id=1, source_target_pairs={{0,8},{4,12},{8,0},{12,4},{16,24},{20,28},{24,16},{28,20},{1,9},{5... | collective-permute-start | bytes 1990664 | tf_op jit(solution)/shard_map/ppermute | solution.py:467
  763.1 39.6 %collective-permute-start.64 = (f32[144,1152]{1,0:T(8,128)}, f32[144,1152]{1,0:T(8,128)}, u32[]{:S(2)}, u32[]{:S(2)}) collective-permute-start(f32[144,1152]{1,0:T(8,128)} %bitcast.381), channel_id=1, source_target_pairs={{0,16},{4,20},{8,24},{12,28},{16,0},{20,4},{24,8},{28,12},{1,17},{... | collective-permute-start | bytes 1990664 | tf_op jit(solution)/shard_map/ppermute | solution.py:471
  835.6 36.1 %collective-permute-start.77 = (f32[576,1152]{1,0:T(8,128)}, f32[576,1152]{1,0:T(8,128)}, u32[]{:S(2)}, u32[]{:S(2)}) collective-permute-start(f32[576,1152]{1,0:T(8,128)} %shard_map.532.refs_0_), channel_id=1, source_target_pairs={{0,4},{4,0},{8,12},{12,8},{16,20},{20,16},{24,28},{28,24},{1,5},{5... | collective-permute-start | bytes 7962632 | tf_op jit(solution)/shard_map/ppermute | solution.py:463
  836.1 32.1 %collective-permute-start.72 = (f32[516,576]{1,0:T(8,128)}, f32[516,576]{1,0:T(8,128)}, u32[]{:S(2)}, u32[]{:S(2)}) collective-permute-start(f32[516,576]{1,0:T(8,128)} %fusion.41), channel_id=1, source_target_pairs={{0,3},{1,0},{2,1},{3,2},{4,7},{5,4},{6,5},{7,6},{8,11},{9,8},{10,9... | collective-permute-start | bytes 3566600 | tf_op jit(solution)/shard_map/ppermute | solution.py:476
  852.0 37.0 %collective-permute-start.78 = (f32[288,1152]{1,0:T(8,128)}, f32[288,1152]{1,0:T(8,128)}, u32[]{:S(2)}, u32[]{:S(2)}) collective-permute-start(f32[288,1152]{1,0:T(8,128)} %shard_map.533.refs_0_), channel_id=1, source_target_pairs={{0,4},{4,0},{8,12},{12,8},{16,20},{20,16},{24,28},{28,24},{1,5},{5... | collective-permute-start | bytes 3981320 | tf_op jit(solution)/shard_map/ppermute | solution.py:463
  868.2 33.8 %collective-permute-start.81 = (f32[8,2,1152]{2,1,0:T(2,128)S(1)}, f32[8,2,1152]{2,1,0:T(2,128)S(1)}, u32[]{:S(2)}, u32[]{:S(2)}) collective-permute-start(f32[8,2,1152]{2,1,0:T(2,128)S(1)} %pad_maximum_fusion.12.refs_0_), channel_id=1, source_target_pairs={{0,3},{1,0},{2,1},{3,2},{4,7},{5,4},{6,5},{7,6},{8,11},{9,8},{10,9... | collective-permute-start | bytes 221192 | tf_op jit(solution)/shard_map/ppermute | solution.py:476
  870.9 31.2 %collective-permute-start.80 = (f32[8,2,1152]{2,1,0:T(2,128)S(1)}, f32[8,2,1152]{2,1,0:T(2,128)S(1)}, u32[]{:S(2)}, u32[]{:S(2)}) collective-permute-start(f32[8,2,1152]{2,1,0:T(2,128)S(1)} %pad_maximum_fusion.12.refs_0_), channel_id=1, source_target_pairs={{0,2},{1,3},{2,0},{3,1},{4,6},{5,7},{6,4},{7,5},{8,10},{9,11},{10,... | collective-permute-start | bytes 221192 | tf_op jit(solution)/shard_map/ppermute | solution.py:476
  902.1 31.6 %collective-permute-start.84 = (f32[6,2,1152]{2,1,0:T(2,128)S(1)}, f32[6,2,1152]{2,1,0:T(2,128)S(1)}, u32[]{:S(2)}, u32[]{:S(2)}) collective-permute-start(f32[6,2,1152]{2,1,0:T(2,128)S(1)} %pad_maximum_fusion.13.refs_0_), channel_id=1, source_target_pairs={{0,3},{1,0},{2,1},{3,2},{4,7},{5,4},{6,5},{7,6},{8,11},{9,8},{10,9... | collective-permute-start | bytes 165896 | tf_op jit(solution)/shard_map/ppermute | solution.py:476
  (187 other events, 2802.0 us)
Sparse Core Ops, SparseCore 0:
  10.2 36.6 all-gather.12
  49.0 54.5 all-gather.14
  105.7 54.1 all-gather.16
  161.9 54.1 all-gather.18
  254.0 53.5 all-gather.20
  363.8 169.9 all-gather.22
  536.7 50.7 reduce-scatter.8
  590.4 80.4 reduce-scatter.6
  673.8 52.3 reduce-scatter.10
  749.1 49.1 reduce-scatter.12

commit v6 on v5

--- a/solution.py
+++ b/solution.py
@@ -1404,9 +1404,9 @@
     fc2_held = order.mark(hold(fc2_piece, fc2_near, fc2_far))
     fc2_other = to_core(fc2_held)
     fc1_far = order.mark(*fc1_far)
-    fc1_held = order.mark(hold(fc1_piece, fc1_near, fc1_far))
     skip_piece = order.mark(skip_piece)
     skip_near = spread(skip_piece)
+    fc1_held = order.mark(hold(fc1_piece, fc1_near, fc1_far))
     attn_near = order.mark(*attn_near)
     attn_far = spread_far(attn_near)
     fc2_sum, fc2_moments = order.mark(

time: 1010 us -> 1020 us (level)
  local copies, waits for them, and re-layouts: 212 us -> 224 us
    unnamed x301 -> x313, local copies, waits for them, and re-layouts: 92.5 us -> 97.5 us
  transfers between devices with their start and end apart: 101 -> 101, of which waited for: 44 -> 42; matrix products, arithmetic and copies ran while one was open for 35% -> 36% of each run, Pallas kernels for 10% -> 10%
where the time goes in v6:
time: 1020 us; the launch traced here: 1010 us
  waiting for transfers between devices  307 us (30%)
  local copies, waits for them, and re-layouts  224 us (22%)
  Pallas kernels  132 us (13%)
  other arithmetic  121 us (12%)
  matrix products  115 us (11%)
  starting transfers between devices  89.2 us (9%)
  between operations  21 us (2%)
    ppermute x25, waiting for transfers between devices, to_x(): return lax.ppermute(array, 'dp', [(i, i ^ 2) for i in range(8)])  212 us
    unnamed x313, local copies, waits for them, and re-layouts  97.5 us
    ppermute x25, waiting for transfers between devices, to_y(): return lax.ppermute(array, 'dp', [(i, i ^ 4) for i in range(8)])  45.7 us
    dot_general x5, matrix products, matmul(): return jnp.dot(left_side, right_side, preferred_element_type=jnp.float32)  37.6 us
    ppermute x25, starting transfers between devices, to_y(): return lax.ppermute(array, 'dp', [(i, i ^ 4) for i in range(8)])  31.7 us
    pallas_call x4, Pallas kernels, assemble(): pl.pallas_call(kernel, in_specs=[pl.BlockSpec(memory_space=pltpu.SMEM)] +...  30 us
    pallas_call x8, Pallas kernels, place_rows(): pl.pallas_call(kernel, in_specs=in_specs, out_specs=out_specs, out_shape=...  27.3 us
    ppermute x18, starting transfers between devices, turn_mp(): lax.ppermute(array, 'mp', [(i, (i + shift) % count) for i in range(count)])  26.4 us
  transfers between devices with their start and end apart: 101, of which 42 were waited for; matrix products, arithmetic and copies ran while one was open for 36% of the time, Pallas kernels for 10%

profile of v6, /device:TPU:0, one launch (start us, length us, event | category | flops | bytes accessed | tf_op | source)
XLA Modules:
  0.0 1009.5 jit_solution(10146166200289207141)
XLA Ops:
  34.8 6.9 copy.138
  58.0 16.4 %collective-permute-done.4.refs_3_ = f32[3,72,1152]{2,1,0:T(8,128)} collective-permute-done((f32[3,72,1152]{2,1,0:T(8,128)}, f32[3,72,1152]{2,1,0:T(8,128)}, u32[]{:S(2)}, u32[]{:S(2)}) %collective-permute-start.4) | collective-permute-done | bytes 995360 | tf_op jit(solution)/shard_map/ppermute | solution.py:467
  79.7 5.8 collective-permute-done.12.refs_9_
  85.5 5.4 collective-permute-done.11.refs_7_
  94.7 8.9 all-gather.15.cloned.1.call-done
  109.6 6.5 shard_map.521
  145.8 6.2 collective-permute-done.16.refs_3_
  164.9 13.3 %collective-permute-done.20.refs_7_ = f32[1,144,1152]{2,1,0:T(8,128)} collective-permute-done((f32[1,144,1152]{2,1,0:T(8,128)S(1)}, f32[1,144,1152]{2,1,0:T(8,128)}, u32[]{:S(2)}, u32[]{:S(2)}) %collective-permute-start.20) | collective-permute-done | bytes 663584 | tf_op jit(solution)/shard_map/ppermute | solution.py:467
  178.2 8.4 collective-permute-done.21.refs_9_
  196.5 10.5 %shard_map.522 = (bf16[12,288,1152]{2,1,0:T(8,128)(2,1)}, bf16[4,288,1152]{2,1,0:T(8,128)(2,1)S(1)}) custom-call(s32[17]{0:T(128)S(1)} %stack.384.table_ref, f32[4,288,1152]{2,1,0:T(8,128)} %bitcast.391, f32[3,144,1152]{2,1,0:T(8,128)} %fusion.7.refs_1_, f32[3,144,1152]{2,1,0:T(8,128)} %collective-permute-done.15.refs_2_, ...), custom_call_target="tpu_custom_call" | custom-call | bytes 1024 | tf_op jit(solution)/shard_map/pallas_call | solution.py:553
  208.5 8.6 convolution_convert_fusion.qkv_ref
  217.0 9.2 shard_map.523
  229.4 6.2 fusion
  260.7 6.0 collective-permute-done.29.refs_5_
  266.7 13.7 %collective-permute-done.28.refs_4_ = f32[2,144,1152]{2,1,0:T(8,128)} collective-permute-done((f32[2,144,1152]{2,1,0:T(8,128)}, f32[2,144,1152]{2,1,0:T(8,128)}, u32[]{:S(2)}, u32[]{:S(2)}) %collective-permute-start.28) | collective-permute-done | bytes 1327136 | tf_op jit(solution)/shard_map/ppermute | solution.py:467
  280.4 6.2 shard_map.524
  290.9 9.4 multiply_convert_fusion
  300.4 8.0 fusion.35
  314.0 8.6 collective-permute-done.30.refs_2_
  330.5 6.8 shard_map.525
  337.3 8.5 fusion.36
  348.2 13.3 %fusion.31 = (f32[2304]{0:T(1024)S(1)}, bf16[1032,2304]{1,0:T(8,128)(2,1)}) fusion(f32[1032,2304]{1,0:T(8,128)S(1)} %bitcast.438, bf16[1032,1152]{1,0:T(8,128)(2,1)S(1)} %copy-done.88, bf16[2304,1152]{1,0:T(8,128)(2,1)S(1)} %bitcast.376), kind=kOutput, calls=%fused_computation.237 | convolution fusion | flops 5511571456 | bytes 21961728 | tf_op jit(solution)/shard_map/td,fd->tf/dot_general | solution.py:1243
  363.7 13.4 %collective-permute-done.33 = f32[2,144,1152]{2,1,0:T(8,128)} collective-permute-done((f32[2,144,1152]{2,1,0:T(8,128)}, f32[2,144,1152]{2,1,0:T(8,128)}, u32[]{:S(2)}, u32[]{:S(2)}) %collective-permute-start.33) | collective-permute-done | bytes 1327136 | tf_op jit(solution)/shard_map/ppermute | solution.py:467
  384.0 9.0 fusion.37
  396.3 7.9 fusion.38
  425.7 16.9 %shard_map.526 = bf16[2,258,3456]{2,1,0:T(8,128)(2,1)S(1)} custom-call(bf16[2,258,3456]{2,1,0:T(8,128)(2,1)S(1)} %copy-done.15, bf16[2,258,1152]{2,1,0:T(8,128)(2,1)S(1)} %reshape.350.grad_ref), custom_call_target="tpu_custom_call" | custom-call | bytes 1024 | tf_op jit(solution)/shard_map/pallas_call | solution.py:1020
  455.5 5.3 fusion.3
  460.8 9.1 fusion.39
  495.4 10.4 %multiply_reduce_fusion.5 = (f32[1152]{0:T(1024)S(1)}, f32[516]{0:T(1024)S(1)}, f32[516]{0:T(1024)S(1)}, f32[1152]{0:T(1024)S(1)}, f32[516,1152]{1,0:T(8,128)S(1)}) fusion(f32[516,1152]{1,0:T(8,128)} %get-tuple-element.449, f32[1152]{0:T(1024)S(1)} %copy-done.105, bf16[516,3456]{1,0:T(8,128)(2,1)} %reshape.351, bf16[3456,1152]{1,0:T(8,128)(2,1)} %bitcast.428), kind=kOutput, calls=%fused_computation.44 | convolution fusion | flops 4112871936 | bytes 16302624 | tf_op jit(solution)/shard_map/dot_general | solution.py:30
  525.0 8.8 all-gather.23.cloned.1.call-done
  536.3 14.6 %shard_map.527 = f32[16,144,1152]{2,1,0:T(8,128)} custom-call(s32[1]{0:T(128)} %bitcast.26.core_ref, f32[12,2,144,1152]{3,2,1,0:T(8,128)} %bitcast.389, f32[4,2,144,1152]{3,2,1,0:T(8,128)S(1)} %copy-done.22, f32[12,144,1152]{2,1,0:T(8,128)} %collective-permute-done.41.refs_2_, f32[4,144,1152]{2,1,0:T(8,128)S(1)} %collective-permute-done.42.refs_3_), custom_call_target="tpu_custom_call" | custom-call | bytes 1024 | tf_op jit(solution)/shard_map/pallas_call | solution.py:753
  555.5 10.7 %collective-permute-done.45 = f32[4,144,1152]{2,1,0:T(8,128)} collective-permute-done((f32[4,144,1152]{2,1,0:T(8,128)}, f32[4,144,1152]{2,1,0:T(8,128)}, u32[]{:S(2)}, u32[]{:S(2)}) %collective-permute-start.45) | collective-permute-done | bytes 2654240 | tf_op jit(solution)/shard_map/ppermute | solution.py:467
  569.4 5.2 fusion.2
  581.2 16.0 %collective-permute-done.43 = f32[2,144,1152]{2,1,0:T(8,128)S(1)} collective-permute-done((f32[2,144,1152]{2,1,0:T(8,128)}, f32[2,144,1152]{2,1,0:T(8,128)S(1)}, u32[]{:S(2)}, u32[]{:S(2)}) %collective-permute-start.43) | collective-permute-done | bytes 1327136 | tf_op jit(solution)/shard_map/ppermute | solution.py:467
  607.3 9.5 shard_map.528
  619.4 43.1 %collective-permute-done.50 = f32[4,144,1152]{2,1,0:T(8,128)} collective-permute-done((f32[4,144,1152]{2,1,0:T(8,128)}, f32[4,144,1152]{2,1,0:T(8,128)}, u32[]{:S(2)}, u32[]{:S(2)}) %collective-permute-start.50) | collective-permute-done | bytes 2654240 | tf_op jit(solution)/shard_map/ppermute | solution.py:467
  663.3 5.3 fusion.1
  671.1 12.1 %collective-permute-done.47 = f32[2,72,1152]{2,1,0:T(8,128)} collective-permute-done((f32[2,72,1152]{2,1,0:T(8,128)}, f32[2,72,1152]{2,1,0:T(8,128)}, u32[]{:S(2)}, u32[]{:S(2)}) %collective-permute-start.47) | collective-permute-done | bytes 663584 | tf_op jit(solution)/shard_map/ppermute | solution.py:467
  690.3 23.2 %collective-permute-done.52 = f32[4,72,1152]{2,1,0:T(8,128)S(1)} collective-permute-done((f32[4,72,1152]{2,1,0:T(8,128)S(1)}, f32[4,72,1152]{2,1,0:T(8,128)S(1)}, u32[]{:S(2)}, u32[]{:S(2)}) %collective-permute-start.52) | collective-permute-done | bytes 1327136 | tf_op jit(solution)/shard_map/ppermute | solution.py:467
  721.6 6.8 add_convert_fusion
  732.9 11.5 %collective-permute-done.58.refs_1_ = f32[144,1152]{1,0:T(8,128)S(1)} collective-permute-done((f32[144,1152]{1,0:T(8,128)S(1)}, f32[144,1152]{1,0:T(8,128)S(1)}, u32[]{:S(2)}, u32[]{:S(2)}) %collective-permute-start.58) | collective-permute-done | bytes 663584 | tf_op jit(solution)/shard_map/ppermute | solution.py:467
  749.7 5.7 collective-permute-done.61.refs_3_
  765.3 7.1 collective-permute-done.65.refs_3_
  774.6 12.8 %collective-permute-done.66.refs_4_ = f32[72,1152]{1,0:T(8,128)S(1)} collective-permute-done((f32[72,1152]{1,0:T(8,128)S(1)}, f32[72,1152]{1,0:T(8,128)S(1)}, u32[]{:S(2)}, u32[]{:S(2)}) %collective-permute-start.66) | collective-permute-done | bytes 331808 | tf_op jit(solution)/shard_map/ppermute | solution.py:471
  788.2 10.5 %reduce-scatter.13.cloned.1.call-done = f32[1,72,1152]{2,1,0:T(8,128)} async-done(((f32[4,72,1152]{2,1,0:T(8,128)}), f32[1,72,1152]{2,1,0:T(8,128)}) %reduce-scatter.13.cloned.1.call-update) | async-done | bytes 331792
  824.6 11.6 %collective-permute-done.60.refs_2_ = f32[516,576]{1,0:T(8,128)} collective-permute-done((f32[516,576]{1,0:T(8,128)}, f32[516,576]{1,0:T(8,128)}, u32[]{:S(2)}, u32[]{:S(2)}) %collective-permute-start.60) | collective-permute-done | bytes 1188896 | tf_op jit(solution)/shard_map/ppermute | solution.py:476
  866.1 7.4 collective-permute-done.72.refs_3_
  996.1 5.3 shard_map.545
  (754 shorter events, 496.4 us)
Async XLA Ops:
  7.2 42.1 %all-gather.13.cloned.1.call-start = ((), (), s32[]{:S(2)}) async-start(), calls=%async_computation.7 | async-start | bytes 1658880 | tf_op jit(solution)/shard_map/all_gather | solution.py:608
  9.1 94.5 %all-gather.15.cloned.1.call-start = ((), (), s32[]{:S(2)}) async-start(), calls=%async_computation.8 | async-start | bytes 3317760 | tf_op jit(solution)/shard_map/all_gather | solution.py:608
  15.3 149.6 %all-gather.17.cloned.1.call-start = ((), (), s32[]{:S(2)}) async-start(), calls=%async_computation.9 | async-start | bytes 3317760 | tf_op jit(solution)/shard_map/all_gather | solution.py:608
  17.3 31.8 %collective-permute-start.86 = (f32[1152]{0:T(1024)S(1)}, f32[1152]{0:T(1024)S(1)}, u32[]{:S(2)}, u32[]{:S(2)}) collective-permute-start(f32[1152]{0:T(1024)S(1)} %copy-done.114), channel_id=1, source_target_pairs={{0,2},{1,3},{2,0},{3,1},{4,6},{5,7},{6,4},{7,5},{8,10},{9,11},{10,... | collective-permute-start | bytes 13832 | tf_op jit(solution)/shard_map/ppermute | solution.py:476
  94.1 147.5 %all-gather.19.cloned.1.call-start = ((), (), s32[]{:S(2)}) async-start(), calls=%async_computation.10 | async-start | bytes 3317760 | tf_op jit(solution)/shard_map/all_gather | solution.py:608
  106.6 45.4 %collective-permute-start.16 = (f32[3,144,1152]{2,1,0:T(8,128)}, f32[3,144,1152]{2,1,0:T(8,128)}, u32[]{:S(2)}, u32[]{:S(2)}) collective-permute-start(f32[3,144,1152]{2,1,0:T(8,128)} %fusion.7.refs_1_), channel_id=1, source_target_pairs={{0,8},{4,12},{8,0},{12,4},{16,24},{20,28},{24,16},{28,20},{1,9},{5... | collective-permute-start | bytes 5971976 | tf_op jit(solution)/shard_map/ppermute | solution.py:467
  108.1 45.1 %collective-permute-start.17 = (f32[3,144,1152]{2,1,0:T(8,128)}, f32[3,144,1152]{2,1,0:T(8,128)}, u32[]{:S(2)}, u32[]{:S(2)}) collective-permute-start(f32[3,144,1152]{2,1,0:T(8,128)} %fusion.7.refs_1_), channel_id=1, source_target_pairs={{0,16},{4,20},{8,24},{12,28},{16,0},{20,4},{24,8},{28,12},{1,17},{... | collective-permute-start | bytes 5971976 | tf_op jit(solution)/shard_map/ppermute | solution.py:471
  122.4 38.4 %collective-permute-start.22 = (f32[516,1152]{1,0:T(8,128)}, f32[516,1152]{1,0:T(8,128)}, u32[]{:S(2)}, u32[]{:S(2)}) collective-permute-start(f32[516,1152]{1,0:T(8,128)} %convert_multiply_fusion), channel_id=1, source_target_pairs={{0,4},{4,0},{8,12},{12,8},{16,20},{20,16},{24,28},{28,24},{1,5},{5... | collective-permute-start | bytes 7133192 | tf_op jit(solution)/shard_map/ppermute | solution.py:463
  160.1 165.1 %all-gather.21.cloned.1.call-start = ((), (), s32[]{:S(2)}) async-start(), calls=%async_computation.11 | async-start | bytes 3317760 | tf_op jit(solution)/shard_map/all_gather | solution.py:608
  160.3 35.1 %collective-permute-start.19 = (f32[3,144,1152]{2,1,0:T(8,128)}, f32[3,144,1152]{2,1,0:T(8,128)}, u32[]{:S(2)}, u32[]{:S(2)}) collective-permute-start(f32[3,144,1152]{2,1,0:T(8,128)} %collective-permute-done.17.refs_5_), channel_id=1, source_target_pairs={{0,4},{4,0},{8,12},{12,8},{16,20},{20,16},{24,28},{28,24},{1,5},{5... | collective-permute-start | bytes 5971976 | tf_op jit(solution)/shard_map/ppermute | solution.py:463
  160.8 34.6 %collective-permute-start.18 = (f32[3,144,1152]{2,1,0:T(8,128)}, f32[3,144,1152]{2,1,0:T(8,128)}, u32[]{:S(2)}, u32[]{:S(2)}) collective-permute-start(f32[3,144,1152]{2,1,0:T(8,128)} %collective-permute-done.16.refs_3_), channel_id=1, source_target_pairs={{0,4},{4,0},{8,12},{12,8},{16,20},{20,16},{24,28},{28,24},{1,5},{5... | collective-permute-start | bytes 5971976 | tf_op jit(solution)/shard_map/ppermute | solution.py:463
  189.0 46.6 %collective-permute-start.25 = (f32[3,144,1152]{2,1,0:T(8,128)S(1)}, f32[3,144,1152]{2,1,0:T(8,128)}, u32[]{:S(2)}, u32[]{:S(2)}) collective-permute-start(f32[3,144,1152]{2,1,0:T(8,128)S(1)} %fusion.6.refs_1_), channel_id=1, source_target_pairs={{0,8},{4,12},{8,0},{12,4},{16,24},{20,28},{24,16},{28,20},{1,9},{5... | collective-permute-start | bytes 5971976 | tf_op jit(solution)/shard_map/ppermute | solution.py:467
  191.3 45.7 %collective-permute-start.26 = (f32[3,144,1152]{2,1,0:T(8,128)S(1)}, f32[3,144,1152]{2,1,0:T(8,128)}, u32[]{:S(2)}, u32[]{:S(2)}) collective-permute-start(f32[3,144,1152]{2,1,0:T(8,128)S(1)} %fusion.6.refs_1_), channel_id=1, source_target_pairs={{0,16},{4,20},{8,24},{12,28},{16,0},{20,4},{24,8},{28,12},{1,17},{... | collective-permute-start | bytes 5971976 | tf_op jit(solution)/shard_map/ppermute | solution.py:471
  248.2 38.5 %collective-permute-start.27 = (f32[516,1152]{1,0:T(8,128)}, f32[516,1152]{1,0:T(8,128)}, u32[]{:S(2)}, u32[]{:S(2)}) collective-permute-start(f32[516,1152]{1,0:T(8,128)} %get-tuple-element.394), channel_id=1, source_target_pairs={{0,4},{4,0},{8,12},{12,8},{16,20},{20,16},{24,28},{28,24},{1,5},{5... | collective-permute-start | bytes 7133192 | tf_op jit(solution)/shard_map/ppermute | solution.py:463
  248.2 32.2 %collective-permute-start.28 = (f32[2,144,1152]{2,1,0:T(8,128)}, f32[2,144,1152]{2,1,0:T(8,128)}, u32[]{:S(2)}, u32[]{:S(2)}) collective-permute-start(f32[2,144,1152]{2,1,0:T(8,128)} %slice.351), channel_id=1, source_target_pairs={{0,8},{4,12},{8,0},{12,4},{16,24},{20,28},{24,16},{28,20},{1,9},{5... | collective-permute-start | bytes 3981320 | tf_op jit(solution)/shard_map/ppermute | solution.py:467
  253.9 279.9 %all-gather.23.cloned.1.call-start = ((), (), s32[]{:S(2)}) async-start(), calls=%async_computation.12 | async-start | bytes 12165120 | tf_op jit(solution)/shard_map/all_gather | solution.py:1251
  258.7 63.9 %collective-permute-start.30 = (f32[3,144,1152]{2,1,0:T(8,128)S(1)}, f32[3,144,1152]{2,1,0:T(8,128)S(1)}, u32[]{:S(2)}, u32[]{:S(2)}) collective-permute-start(f32[3,144,1152]{2,1,0:T(8,128)S(1)} %fusion.5.refs_1_), channel_id=1, source_target_pairs={{0,8},{4,12},{8,0},{12,4},{16,24},{20,28},{24,16},{28,20},{1,9},{5... | collective-permute-start | bytes 5971976 | tf_op jit(solution)/shard_map/ppermute | solution.py:467
  260.2 63.7 %collective-permute-start.31 = (f32[3,144,1152]{2,1,0:T(8,128)S(1)}, f32[3,144,1152]{2,1,0:T(8,128)S(1)}, u32[]{:S(2)}, u32[]{:S(2)}) collective-permute-start(f32[3,144,1152]{2,1,0:T(8,128)S(1)} %fusion.5.refs_1_), channel_id=1, source_target_pairs={{0,16},{4,20},{8,24},{12,28},{16,0},{20,4},{24,8},{28,12},{1,17},{... | collective-permute-start | bytes 5971976 | tf_op jit(solution)/shard_map/ppermute | solution.py:471
  346.0 31.1 %collective-permute-start.33 = (f32[2,144,1152]{2,1,0:T(8,128)}, f32[2,144,1152]{2,1,0:T(8,128)}, u32[]{:S(2)}, u32[]{:S(2)}) collective-permute-start(f32[2,144,1152]{2,1,0:T(8,128)} %get-tuple-element.418), channel_id=1, source_target_pairs={{0,8},{4,12},{8,0},{12,4},{16,24},{20,28},{24,16},{28,20},{1,9},{5... | collective-permute-start | bytes 3981320 | tf_op jit(solution)/shard_map/ppermute | solution.py:467
  363.7 255.7 %reduce-scatter.9.cloned.1.call-start = ((), (), s32[]{:S(2)}) async-start(), calls=%async_computation.5 | async-start | bytes 3317760 | tf_op jit(solution)/shard_map/reduce_scatter | solution.py:657
  393.3 60.7 %collective-permute-start.38 = (f32[4,144,1152]{2,1,0:T(8,128)}, f32[4,144,1152]{2,1,0:T(8,128)}, u32[]{:S(2)}, u32[]{:S(2)}) collective-permute-start(f32[4,144,1152]{2,1,0:T(8,128)} %pad_maximum_fusion.2), channel_id=1, source_target_pairs={{0,8},{4,12},{8,0},{12,4},{16,24},{20,28},{24,16},{28,20},{1,9},{5... | collective-permute-start | bytes 7962632 | tf_op jit(solution)/shard_map/ppermute | solution.py:467
  394.8 60.7 %collective-permute-start.39 = (f32[4,144,1152]{2,1,0:T(8,128)}, f32[4,144,1152]{2,1,0:T(8,128)}, u32[]{:S(2)}, u32[]{:S(2)}) collective-permute-start(f32[4,144,1152]{2,1,0:T(8,128)} %pad_maximum_fusion.3), channel_id=1, source_target_pairs={{0,16},{4,20},{8,24},{12,28},{16,0},{20,4},{24,8},{28,12},{1,17},{... | collective-permute-start | bytes 7962632 | tf_op jit(solution)/shard_map/ppermute | solution.py:471
  409.3 72.7 %collective-permute-start.36 = (f32[2,144,1152]{2,1,0:T(8,128)}, f32[2,144,1152]{2,1,0:T(8,128)}, u32[]{:S(2)}, u32[]{:S(2)}) collective-permute-start(f32[2,144,1152]{2,1,0:T(8,128)} %get-tuple-element.434), channel_id=1, source_target_pairs={{0,8},{4,12},{8,0},{12,4},{16,24},{20,28},{24,16},{28,20},{1,9},{5... | collective-permute-start | bytes 3981320 | tf_op jit(solution)/shard_map/ppermute | solution.py:467
  409.9 73.3 %collective-permute-start.37 = (f32[2,144,1152]{2,1,0:T(8,128)}, f32[2,144,1152]{2,1,0:T(8,128)}, u32[]{:S(2)}, u32[]{:S(2)}) collective-permute-start(f32[2,144,1152]{2,1,0:T(8,128)} %get-tuple-element.435), channel_id=1, source_target_pairs={{0,16},{4,20},{8,24},{12,28},{16,0},{20,4},{24,8},{28,12},{1,17},{... | collective-permute-start | bytes 3981320 | tf_op jit(solution)/shard_map/ppermute | solution.py:471
  489.5 44.4 %collective-permute-start.41 = (f32[12,144,1152]{2,1,0:T(8,128)}, f32[12,144,1152]{2,1,0:T(8,128)}, u32[]{:S(2)}, u32[]{:S(2)}) collective-permute-start(f32[12,144,1152]{2,1,0:T(8,128)} %dynamic-slice_bitcast_fusion), channel_id=1, source_target_pairs={{0,4},{4,0},{8,12},{12,8},{16,20},{20,16},{24,28},{28,24},{1,5},{5... | collective-permute-start | bytes 23887880 | tf_op jit(solution)/shard_map/ppermute | solution.py:463
  494.7 176.4 %reduce-scatter.7.cloned.1.call-start = ((), (), s32[]{:S(2)}) async-start(), calls=%async_computation.4 | async-start | bytes 3317760 | tf_op jit(solution)/shard_map/reduce_scatter | solution.py:657
  494.8 39.1 %collective-permute-start.42 = (f32[4,144,1152]{2,1,0:T(8,128)}, f32[4,144,1152]{2,1,0:T(8,128)S(1)}, u32[]{:S(2)}, u32[]{:S(2)}) collective-permute-start(f32[4,144,1152]{2,1,0:T(8,128)} %dynamic-slice_bitcast_fusion.2), channel_id=1, source_target_pairs={{0,4},{4,0},{8,12},{12,8},{16,20},{20,16},{24,28},{28,24},{1,5},{5... | collective-permute-start | bytes 7962632 | tf_op jit(solution)/shard_map/ppermute | solution.py:463
  505.8 60.4 %collective-permute-start.45 = (f32[4,144,1152]{2,1,0:T(8,128)}, f32[4,144,1152]{2,1,0:T(8,128)}, u32[]{:S(2)}, u32[]{:S(2)}) collective-permute-start(f32[4,144,1152]{2,1,0:T(8,128)} %pad_maximum_fusion.4), channel_id=1, source_target_pairs={{0,8},{4,12},{8,0},{12,4},{16,24},{20,28},{24,16},{28,20},{1,9},{5... | collective-permute-start | bytes 7962632 | tf_op jit(solution)/shard_map/ppermute | solution.py:467
  506.5 60.0 %collective-permute-start.46 = (f32[4,144,1152]{2,1,0:T(8,128)}, f32[4,144,1152]{2,1,0:T(8,128)}, u32[]{:S(2)}, u32[]{:S(2)}) collective-permute-start(f32[4,144,1152]{2,1,0:T(8,128)} %pad_maximum_fusion.5), channel_id=1, source_target_pairs={{0,16},{4,20},{8,24},{12,28},{16,0},{20,4},{24,8},{28,12},{1,17},{... | collective-permute-start | bytes 7962632 | tf_op jit(solution)/shard_map/ppermute | solution.py:471
  520.4 86.9 %collective-permute-start.40 = (f32[16,72,1152]{2,1,0:T(8,128)}, f32[16,72,1152]{2,1,0:T(8,128)}, u32[]{:S(2)}, u32[]{:S(2)}) collective-permute-start(f32[16,72,1152]{2,1,0:T(8,128)} %dynamic-slice_bitcast_fusion.1), channel_id=1, source_target_pairs={{0,4},{4,0},{8,12},{12,8},{16,20},{20,16},{24,28},{28,24},{1,5},{5... | collective-permute-start | bytes 15925256 | tf_op jit(solution)/shard_map/ppermute | solution.py:463
  574.7 184.8 %reduce-scatter.11.cloned.1.call-start = ((), (), s32[]{:S(2)}) async-start(), calls=%async_computation.6 | async-start | bytes 3317760 | tf_op jit(solution)/shard_map/reduce_scatter | solution.py:657
  604.5 58.0 %collective-permute-start.50 = (f32[4,144,1152]{2,1,0:T(8,128)}, f32[4,144,1152]{2,1,0:T(8,128)}, u32[]{:S(2)}, u32[]{:S(2)}) collective-permute-start(f32[4,144,1152]{2,1,0:T(8,128)} %pad_maximum_fusion.6), channel_id=1, source_target_pairs={{0,8},{4,12},{8,0},{12,4},{16,24},{20,28},{24,16},{28,20},{1,9},{5... | collective-permute-start | bytes 7962632 | tf_op jit(solution)/shard_map/ppermute | solution.py:467
  605.1 58.2 %collective-permute-start.51 = (f32[4,144,1152]{2,1,0:T(8,128)}, f32[4,144,1152]{2,1,0:T(8,128)}, u32[]{:S(2)}, u32[]{:S(2)}) collective-permute-start(f32[4,144,1152]{2,1,0:T(8,128)} %pad_maximum_fusion.7), channel_id=1, source_target_pairs={{0,16},{4,20},{8,24},{12,28},{16,0},{20,4},{24,8},{28,12},{1,17},{... | collective-permute-start | bytes 7962632 | tf_op jit(solution)/shard_map/ppermute | solution.py:471
  607.2 63.9 %collective-permute-start.49 = (f32[516,576]{1,0:T(8,128)}, f32[516,576]{1,0:T(8,128)S(1)}, u32[]{:S(2)}, u32[]{:S(2)}) collective-permute-start(f32[516,576]{1,0:T(8,128)} %fusion.43), channel_id=1, source_target_pairs={{0,1},{1,2},{2,3},{3,0},{4,5},{5,6},{6,7},{7,4},{8,9},{9,10},{10,1... | collective-permute-start | bytes 3566600 | tf_op jit(solution)/shard_map/ppermute | solution.py:476
  668.5 130.2 %reduce-scatter.13.cloned.1.call-start = ((), (), s32[]{:S(2)}) async-start(), calls=%async_computation.13 | async-start | bytes 1658880
  717.5 32.1 %collective-permute-start.56 = (f32[144,1152]{1,0:T(8,128)}, f32[144,1152]{1,0:T(8,128)S(1)}, u32[]{:S(2)}, u32[]{:S(2)}) collective-permute-start(f32[144,1152]{1,0:T(8,128)} %bitcast.104.refs_0_), channel_id=1, source_target_pairs={{0,8},{4,12},{8,0},{12,4},{16,24},{20,28},{24,16},{28,20},{1,9},{5... | collective-permute-start | bytes 1990664 | tf_op jit(solution)/shard_map/ppermute | solution.py:467
  759.5 52.0 %collective-permute-start.71 = (f32[576,1152]{1,0:T(8,128)}, f32[576,1152]{1,0:T(8,128)}, u32[]{:S(2)}, u32[]{:S(2)}) collective-permute-start(f32[576,1152]{1,0:T(8,128)} %shard_map.529.refs_0_), channel_id=1, source_target_pairs={{0,4},{4,0},{8,12},{12,8},{16,20},{20,16},{24,28},{28,24},{1,5},{5... | collective-permute-start | bytes 7962632 | tf_op jit(solution)/shard_map/ppermute | solution.py:463
  759.6 76.6 %collective-permute-start.60 = (f32[516,576]{1,0:T(8,128)}, f32[516,576]{1,0:T(8,128)}, u32[]{:S(2)}, u32[]{:S(2)}) collective-permute-start(f32[516,576]{1,0:T(8,128)} %fusion.42), channel_id=1, source_target_pairs={{0,2},{1,3},{2,0},{3,1},{4,6},{5,7},{6,4},{7,5},{8,10},{9,11},{10,... | collective-permute-start | bytes 3566600 | tf_op jit(solution)/shard_map/ppermute | solution.py:476
  763.2 43.3 %collective-permute-start.63 = (f32[144,1152]{1,0:T(8,128)}, f32[144,1152]{1,0:T(8,128)}, u32[]{:S(2)}, u32[]{:S(2)}) collective-permute-start(f32[144,1152]{1,0:T(8,128)} %bitcast.380), channel_id=1, source_target_pairs={{0,8},{4,12},{8,0},{12,4},{16,24},{20,28},{24,16},{28,20},{1,9},{5... | collective-permute-start | bytes 1990664 | tf_op jit(solution)/shard_map/ppermute | solution.py:467
  763.7 44.3 %collective-permute-start.64 = (f32[144,1152]{1,0:T(8,128)}, f32[144,1152]{1,0:T(8,128)}, u32[]{:S(2)}, u32[]{:S(2)}) collective-permute-start(f32[144,1152]{1,0:T(8,128)} %bitcast.381), channel_id=1, source_target_pairs={{0,16},{4,20},{8,24},{12,28},{16,0},{20,4},{24,8},{28,12},{1,17},{... | collective-permute-start | bytes 1990664 | tf_op jit(solution)/shard_map/ppermute | solution.py:471
  836.3 40.8 %collective-permute-start.77 = (f32[576,1152]{1,0:T(8,128)}, f32[576,1152]{1,0:T(8,128)}, u32[]{:S(2)}, u32[]{:S(2)}) collective-permute-start(f32[576,1152]{1,0:T(8,128)} %shard_map.532.refs_0_), channel_id=1, source_target_pairs={{0,4},{4,0},{8,12},{12,8},{16,20},{20,16},{24,28},{28,24},{1,5},{5... | collective-permute-start | bytes 7962632 | tf_op jit(solution)/shard_map/ppermute | solution.py:463
  836.7 36.8 %collective-permute-start.72 = (f32[516,576]{1,0:T(8,128)}, f32[516,576]{1,0:T(8,128)}, u32[]{:S(2)}, u32[]{:S(2)}) collective-permute-start(f32[516,576]{1,0:T(8,128)} %fusion.41), channel_id=1, source_target_pairs={{0,3},{1,0},{2,1},{3,2},{4,7},{5,4},{6,5},{7,6},{8,11},{9,8},{10,9... | collective-permute-start | bytes 3566600 | tf_op jit(solution)/shard_map/ppermute | solution.py:476
  853.4 40.8 %collective-permute-start.78 = (f32[288,1152]{1,0:T(8,128)}, f32[288,1152]{1,0:T(8,128)}, u32[]{:S(2)}, u32[]{:S(2)}) collective-permute-start(f32[288,1152]{1,0:T(8,128)} %shard_map.533.refs_0_), channel_id=1, source_target_pairs={{0,4},{4,0},{8,12},{12,8},{16,20},{20,16},{24,28},{28,24},{1,5},{5... | collective-permute-start | bytes 3981320 | tf_op jit(solution)/shard_map/ppermute | solution.py:463
  873.6 33.9 %collective-permute-start.81 = (f32[8,2,1152]{2,1,0:T(2,128)S(1)}, f32[8,2,1152]{2,1,0:T(2,128)S(1)}, u32[]{:S(2)}, u32[]{:S(2)}) collective-permute-start(f32[8,2,1152]{2,1,0:T(2,128)S(1)} %pad_maximum_fusion.12.refs_0_), channel_id=1, source_target_pairs={{0,3},{1,0},{2,1},{3,2},{4,7},{5,4},{6,5},{7,6},{8,11},{9,8},{10,9... | collective-permute-start | bytes 221192 | tf_op jit(solution)/shard_map/ppermute | solution.py:476
  874.0 33.4 %collective-permute-start.80 = (f32[8,2,1152]{2,1,0:T(2,128)S(1)}, f32[8,2,1152]{2,1,0:T(2,128)S(1)}, u32[]{:S(2)}, u32[]{:S(2)}) collective-permute-start(f32[8,2,1152]{2,1,0:T(2,128)S(1)} %pad_maximum_fusion.12.refs_0_), channel_id=1, source_target_pairs={{0,2},{1,3},{2,0},{3,1},{4,6},{5,7},{6,4},{7,5},{8,10},{9,11},{10,... | collective-permute-start | bytes 221192 | tf_op jit(solution)/shard_map/ppermute | solution.py:476
  907.5 35.6 %collective-permute-start.84 = (f32[6,2,1152]{2,1,0:T(2,128)S(1)}, f32[6,2,1152]{2,1,0:T(2,128)S(1)}, u32[]{:S(2)}, u32[]{:S(2)}) collective-permute-start(f32[6,2,1152]{2,1,0:T(2,128)S(1)} %pad_maximum_fusion.13.refs_0_), channel_id=1, source_target_pairs={{0,3},{1,0},{2,1},{3,2},{4,7},{5,4},{6,5},{7,6},{8,11},{9,8},{10,9... | collective-permute-start | bytes 165896 | tf_op jit(solution)/shard_map/ppermute | solution.py:476
  911.2 31.8 %collective-permute-start.83 = (f32[6,2,1152]{2,1,0:T(2,128)S(1)}, f32[6,2,1152]{2,1,0:T(2,128)S(1)}, u32[]{:S(2)}, u32[]{:S(2)}) collective-permute-start(f32[6,2,1152]{2,1,0:T(2,128)S(1)} %pad_maximum_fusion.13.refs_0_), channel_id=1, source_target_pairs={{0,2},{1,3},{2,0},{3,1},{4,6},{5,7},{6,4},{7,5},{8,10},{9,11},{10,... | collective-permute-start | bytes 165896 | tf_op jit(solution)/shard_map/ppermute | solution.py:476
  911.2 31.8 %collective-permute-start.82 = (f32[6,2,1152]{2,1,0:T(2,128)S(1)}, f32[6,2,1152]{2,1,0:T(2,128)S(1)}, u32[]{:S(2)}, u32[]{:S(2)}) collective-permute-start(f32[6,2,1152]{2,1,0:T(2,128)S(1)} %pad_maximum_fusion.13.refs_0_), channel_id=1, source_target_pairs={{0,1},{1,2},{2,3},{3,0},{4,5},{5,6},{6,7},{7,4},{8,9},{9,10},{10,1... | collective-permute-start | bytes 165896 | tf_op jit(solution)/shard_map/ppermute | solution.py:476
  (193 other events, 2749.9 us)
Sparse Core Ops, SparseCore 0:
  10.2 36.6 all-gather.12
  49.0 54.5 all-gather.14
  105.7 54.1 all-gather.16
  161.9 54.1 all-gather.18
  254.0 53.5 all-gather.20
  363.8 169.9 all-gather.22
  536.7 50.7 reduce-scatter.8
  590.4 80.4 reduce-scatter.6
  673.8 52.3 reduce-scatter.10
  749.7 48.9 reduce-scatter.12
